TPU v7x, 128 devices: a whole 4x4x4 slice. The times are simulated.
128 devices in a mesh: tm: 32 (over z, x_hi, y), space: 4 (over x_lo, core).
Axes of the slice: x: 4 (x_hi: 2, x_lo: 2; x = x_hi * 2 + x_lo), y: 4, z: 4, core: 2. Of those that a mesh axis runs over, the one named last changes fastest.
Arguments:
- video_in: bfloat16 [32, 256, 64, 128], P('tm', 'space'), may hold values from -6 to 6
- cotangent: bfloat16 [32, 256, 64, 128], P('tm', 'space'), may hold values from -6 to 6
- kernel_a: bfloat16 [3, 3, 3, 64, 64], replicated, may hold values from -0.15625 to 0.15625
- kernel_b: bfloat16 [3, 3, 3, 64, 64], replicated, may hold values from -0.15625 to 0.15625
- plane_kernel: bfloat16 [3, 3, 64, 64], replicated, may hold values from -0.25 to 0.25
- plane_head: bfloat16 [64], replicated, may hold values from -0.75 to 0.75
- time_kernel: bfloat16 [3, 64, 64], replicated, may hold values from -0.4375 to 0.4375
- time_mixer: bfloat16 [64, 64], replicated, may hold values from -12 to 12
- time_head: bfloat16 [64], replicated, may hold values from -0.75 to 0.75
- listed: int32 [8], replicated, may hold values from 0 to 31, as said below
Outputs:
- video: bfloat16 [32, 256, 64, 128], P('tm', 'space')
- input_grad: bfloat16 [32, 256, 64, 128], P('tm', 'space')
- plane_scores: float32 [32, 4, 16, 128], P('tm', 'space')
- time_scores: float32 [4, 32, 64], P('space', 'tm')
Inputs may be any that keep to these rules, and one draw needn't show every extreme that they name: `listed`: 8 distinct frame indices; the first is always frame 32 // 2, and frames 0 and 31 are always among the others, which stand in random order.
All inputs are finite; a program needn't handle non-finite values.
Results may differ from a plain program's by a relative error of at most 0.0053.
Values may be sent and summed in bfloat16 or wider, within the bound.
No kernel may reach another device: no remote copies, remote signals or barrier semaphores. Data moves between devices by JAX's collectives and lax.ppermute only.
A program may use at most 128 MiB of HBM per device.

v0:
```python
import jax
import jax.numpy as jnp
from jax import lax
from jax.sharding import PartitionSpec as P

LISTED = 8


def padded_2(array, sides, width):
    for axis, dim in sides:
        size, length = (lax.axis_size(axis), array.shape[dim])
        up = [(i, (i + 1) % size) for i in range(size - 1)]
        down = [(j, i) for i, j in up]
        last = lax.slice_in_dim(array, length - width, length, axis=dim)
        initial = lax.slice_in_dim(array, 0, width, axis=dim)
        before = lax.ppermute(last, axis, up)
        after = lax.ppermute(initial, axis, down)
        array = jnp.concatenate([before, array, after], axis=dim)
    return array


def cube_conv(volume, kernel):
    padded = padded_2(volume, (("tm", 0), ("space", 1)), 1)
    return lax.conv_general_dilated(
        padded[None],
        kernel,
        (1, 1, 1),
        [(0, 0), (0, 0), (1, 1)],
        dimension_numbers=("NDHCW", "DHWIO", "NDHCW"),
        preferred_element_type=jnp.float32,
    )[0]


def flipped(kernel):
    return jnp.swapaxes(kernel[::-1, ::-1, ::-1], 3, 4)


def silu_slope(values):
    logistic = jax.nn.sigmoid(values)
    return logistic * (1.0 + values * (1.0 - logistic))


def plane_map(rimmed, kernel, head):
    conv_out = lax.conv_general_dilated(
        rimmed,
        kernel,
        (1, 1),
        [(0, 0), (1, 1)],
        dimension_numbers=("NHCW", "HWIO", "NHCW"),
        preferred_element_type=jnp.float32,
    )
    return jnp.einsum(
        "nhow,o->nhw",
        jax.nn.silu(conv_out),
        head.astype(jnp.float32),
        precision=lax.Precision.HIGHEST,
    )


def pool_pairs(volume):
    shaped = volume.astype(jnp.float32).reshape(
        volume.shape[0], volume.shape[1] // 2, 2, volume.shape[2], volume.shape[3] // 2, 2
    )
    return jnp.mean(shaped, axis=(2, 5)).astype(jnp.bfloat16)


def time_conv(rimmed, kernel):
    length = rimmed.shape[0] - 2
    total = jnp.zeros((length, rimmed.shape[1], kernel.shape[2], rimmed.shape[3]), jnp.float32)
    for offset in range(3):
        total = total + jnp.einsum(
            "thcw,co->thow",
            rimmed[offset : offset + length],
            kernel[offset],
            preferred_element_type=jnp.float32,
        )
    return total


def time_head_map(time_mean, mixer, head):
    mixed_units = jnp.einsum(
        "hcw,co->how", time_mean, mixer.astype(jnp.float32), precision=lax.Precision.HIGHEST
    )
    return jnp.einsum(
        "how,o->hw",
        jax.nn.silu(mixed_units),
        head.astype(jnp.float32),
        precision=lax.Precision.HIGHEST,
    )


def shards(
    video_in,
    cotangent,
    kernel_a,
    kernel_b,
    plane_kernel,
    plane_head,
    time_kernel,
    time_mixer,
    time_head,
    listed,
):
    float_in = video_in.astype(jnp.float32)
    hidden_in = jax.nn.silu(float_in).astype(jnp.bfloat16)
    pre_act = cube_conv(hidden_in, kernel_a)
    inner_act = jax.nn.silu(pre_act).astype(jnp.bfloat16)
    generated = (float_in + cube_conv(inner_act, kernel_b)).astype(jnp.bfloat16)
    grad_pre = (cube_conv(cotangent, flipped(kernel_b)) * silu_slope(pre_act)).astype(jnp.bfloat16)
    input_grad = (
        cotangent.astype(jnp.float32)
        + cube_conv(grad_pre, flipped(kernel_a)) * silu_slope(float_in)
    ).astype(jnp.bfloat16)
    frames_here = generated.shape[0]
    rows_here = generated.shape[1]
    tm_count = lax.axis_size("tm")
    groups = tm_count // LISTED
    quarter = rows_here // groups
    rimmed = padded_2(generated, (("space", 1),), 1)
    frame_scores = plane_map(rimmed, plane_kernel, plane_head)
    first_frame = lax.axis_index("tm") * frames_here
    select = (
        listed[:, None] == first_frame + jnp.arange(frames_here, dtype=jnp.int32)[None, :]
    ).astype(jnp.float32)
    picked = jnp.einsum("kf,fhw->khw", select, frame_scores, precision=lax.Precision.HIGHEST)
    picked = picked.reshape(tm_count, quarter, frame_scores.shape[2])
    plane_scores = lax.psum_scatter(picked, "tm", scatter_dimension=0, tiled=True)[:, None]
    total_frames = frames_here * tm_count
    clip_time = lax.all_to_all(pool_pairs(generated), "tm", split_axis=1, concat_axis=0, tiled=True)
    padded_clip = jnp.pad(clip_time, ((1, 1), (0, 0), (0, 0), (0, 0)))
    totals = jnp.sum(jax.nn.silu(time_conv(padded_clip, time_kernel)), axis=0)
    time_mean = totals / total_frames
    time_scores = time_head_map(time_mean, time_mixer, time_head)[None]
    return (generated, input_grad, plane_scores, time_scores)


def solution(mesh):
    return jax.shard_map(
        shards,
        mesh=mesh,
        in_specs=(
            P("tm", "space", None, None),
            P("tm", "space", None, None),
            P(),
            P(),
            P(),
            P(),
            P(),
            P(),
            P(),
            P(),
        ),
        out_specs=(
            P("tm", "space", None, None),
            P("tm", "space", None, None),
            P("tm", "space", None, None),
            P("space", "tm", None),
        ),
        check_vma=False,
    )
```

profile of v0, /device:TPU:0, one launch (start us, length us, event | category | flops | bytes accessed | tf_op | source)
XLA Modules:
  0.0 638.1 jit_solution(1217996766784038675)
XLA Ops:
  28.4 7.2 %collective-permute-done.9 = bf16[1,64,64,128]{3,2,1,0:T(8,128)(2,1)} collective-permute-done((bf16[1,64,64,128]{3,2,1,0:T(8,128)(2,1)}, bf16[1,64,64,128]{3,2,1,0:T(8,128)(2,1)}, u32[]{:S(2)}, u32[]{:S(2)}) %collective-permute-start.9) | collective-permute-done | bytes 1048608 | tf_op jit(solution)/shard_map/ppermute | solution.py:17
  56.0 8.6 %copy.114 = bf16[3,1,64,128]{3,2,1,0:T(8,128)(2,1)S(1)} copy(bf16[3,1,64,128]{1,2,3,0:T(8,128)(2,1)} %get-tuple-element.13) | data formatting | bytes 98304 | tf_op jit(solution)/shard_map/slice | solution.py:15
  66.0 8.6 %copy.113 = bf16[3,1,64,128]{3,2,1,0:T(8,128)(2,1)S(1)} copy(bf16[3,1,64,128]{1,2,3,0:T(8,128)(2,1)} %get-tuple-element.12) | data formatting | bytes 98304 | tf_op jit(solution)/shard_map/slice | solution.py:14
  84.0 9.8 %copy.116 = bf16[3,1,64,128]{1,2,3,0:T(8,128)(2,1)} copy(bf16[3,1,64,128]{3,2,1,0:T(8,128)(2,1)S(1)} %collective-permute-done.11) | data formatting | bytes 98304 | tf_op jit(solution)/shard_map/ppermute | solution.py:17
  93.9 9.7 %copy.115 = bf16[3,1,64,128]{1,2,3,0:T(8,128)(2,1)} copy(bf16[3,1,64,128]{3,2,1,0:T(8,128)(2,1)S(1)} %collective-permute-done.10) | data formatting | bytes 98304 | tf_op jit(solution)/shard_map/ppermute | solution.py:16
  103.6 10.0 %maximum_bitcast_fusion = bf16[3,66,64,1,128]{1,2,4,0,3:T(8,128)(2,1)S(1)} fusion(bf16[3,1,64,128]{1,2,3,0:T(8,128)(2,1)} %copy.116, bf16[1,64,64,128]{1,2,3,0:T(8,128)(2,1)} %copy.112, bf16[1,64,64,128]{1,2,3,0:T(8,128)(2,1)S(1)} %copy.111, bf16[1,64,64,128]{1,2,3,0:T(8,128)(2,1)} %copy.110, bf16[3,1,64,128]{1,2,3,0:T(8,128)(2,1)} %copy.115), kind=kLoop, calls=%fused_computation.30 | loop fusion | flops 16220160 | bytes 6488064 | tf_op jit(solution)/shard_map/broadcast_in_dim | solution.py:25
  118.2 11.8 %copy.118 = bf16[3,66,64,1,8,17]{2,4,5,1,0,3:T(8,128)(2,1)} copy(bf16[3,66,64,1,8,17]{1,2,5,4,0,3:T(8,128)(2,1)} %bitcast.153) | data formatting | bytes 6893568 | tf_op jit(solution)/shard_map/conv_general_dilated | solution.py:24
  131.3 19.1 %broadcast_select_fusion.1 = f32[1,64,8,17,64]{4,2,3,1,0:T(8,128)S(1)} fusion(pred[8,17]{0,1:T(8,128)(4,1)S(1)} %copy-done.11, bf16[3,3,3,64,64]{4,3,2,1,0:T(8,128)(2,1)S(1)} %copy-done.7, bf16[3,66,64,1,7,2]{2,4,5,1,0,3:T(8,128)(2,1)S(1)} %slice.77, bf16[3,66,64,1,8,17]{2,4,5,1,0,3:T(8,128)(2,1)} %copy.118), kind=kOutput, calls=%fused_computation.54 | convolution fusion | flops 1937299456 | bytes 6251144 | tf_op jit(solution)/shard_map/conv_general_dilated | solution.py:24
  162.1 8.6 %copy.136 = bf16[3,66,64,1,128]{1,2,4,0,3:T(8,128)(2,1)} copy(bf16[3,66,64,1,128]{4,2,1,0,3:T(8,128)(2,1)} %maximum_bitcast_fusion.1) | data formatting | bytes 6488064
  170.8 7.8 %pad.5.clone = bf16[3,66,64,1,136]{1,2,4,0,3:T(8,128)(2,1)} pad(bf16[3,66,64,1,128]{1,2,4,0,3:T(8,128)(2,1)} %copy.136, bf16[]{:T(256)} %constant.25.clone.1), padding=0_0x0_0x0_0x0_0x1_7 | pad | bytes 6690818 | tf_op jit(solution)/shard_map/broadcast_in_dim | solution.py:25
  178.6 11.7 %copy.102 = bf16[3,66,64,1,8,17]{2,4,5,1,0,3:T(8,128)(2,1)} copy(bf16[3,66,64,1,8,17]{1,2,5,4,0,3:T(8,128)(2,1)} %bitcast.154) | data formatting | bytes 6893568 | tf_op jit(solution)/shard_map/conv_general_dilated | solution.py:24
  191.7 11.2 %broadcast_select_fusion.3 = f32[1,64,8,17,64]{4,2,3,1,0:T(8,128)S(1)} fusion(pred[8,17]{0,1:T(8,128)(4,1)S(1)} %copy-done.11, bf16[3,3,3,64,64]{4,3,2,1,0:T(8,128)(2,1)S(1)} %copy-done, bf16[3,66,64,1,7,2]{2,4,5,1,0,3:T(8,128)(2,1)S(1)} %slice.71, bf16[3,66,64,1,8,17]{2,4,5,1,0,3:T(8,128)(2,1)} %copy.102), kind=kOutput, calls=%fused_computation.56 | convolution fusion | flops 1937299456 | bytes 6251144 | tf_op jit(solution)/shard_map/conv_general_dilated | solution.py:24
  228.0 13.7 %collective-permute-done.13 = bf16[1,64,64,128]{3,2,1,0:T(8,128)(2,1)} collective-permute-done((bf16[1,64,64,128]{3,2,1,0:T(8,128)(2,1)S(1)}, bf16[1,64,64,128]{3,2,1,0:T(8,128)(2,1)}, u32[]{:S(2)}, u32[]{:S(2)}) %collective-permute-start.13) | collective-permute-done | bytes 1048608 | tf_op jit(solution)/shard_map/ppermute | solution.py:17
  248.9 15.3 %collective-permute-done.5 = bf16[1,64,64,128]{3,2,1,0:T(8,128)(2,1)} collective-permute-done((bf16[1,64,64,128]{3,2,1,0:T(8,128)(2,1)S(1)}, bf16[1,64,64,128]{3,2,1,0:T(8,128)(2,1)}, u32[]{:S(2)}, u32[]{:S(2)}) %collective-permute-start.5) | collective-permute-done | bytes 1048608 | tf_op jit(solution)/shard_map/ppermute | solution.py:17
  274.7 8.4 %copy.138 = bf16[3,66,64,1,128]{1,2,4,0,3:T(8,128)(2,1)} copy(bf16[3,66,64,1,128]{4,2,1,0,3:T(8,128)(2,1)} %maximum_bitcast_fusion.3) | data formatting | bytes 6488064
  283.2 7.8 %pad.11.clone = bf16[3,66,64,1,136]{1,2,4,0,3:T(8,128)(2,1)} pad(bf16[3,66,64,1,128]{1,2,4,0,3:T(8,128)(2,1)} %copy.138, bf16[]{:T(256)} %constant.25.clone.1), padding=0_0x0_0x0_0x0_0x1_7 | pad | bytes 6690818 | tf_op jit(solution)/shard_map/broadcast_in_dim | solution.py:25
  291.0 11.7 %copy.123 = bf16[3,66,64,1,8,17]{2,4,5,1,0,3:T(8,128)(2,1)} copy(bf16[3,66,64,1,8,17]{1,2,5,4,0,3:T(8,128)(2,1)} %bitcast.155) | data formatting | bytes 6893568 | tf_op jit(solution)/shard_map/conv_general_dilated | solution.py:24
  304.1 19.1 %broadcast_select_fusion = f32[1,64,8,17,64]{4,2,3,1,0:T(8,128)S(1)} fusion(pred[8,17]{0,1:T(8,128)(4,1)S(1)} %copy-done.11, bf16[3,3,3,64,64]{4,3,2,1,0:T(8,128)(2,1)S(1)} %copy-done, bf16[3,66,64,1,7,2]{2,4,5,1,0,3:T(8,128)(2,1)S(1)} %slice.79, bf16[3,66,64,1,8,17]{2,4,5,1,0,3:T(8,128)(2,1)} %copy.123), kind=kOutput, calls=%fused_computation.53 | convolution fusion | flops 1937299456 | bytes 6251144 | tf_op jit(solution)/shard_map/conv_general_dilated | solution.py:24
  334.7 8.4 %copy.137 = bf16[3,66,64,1,128]{1,2,4,0,3:T(8,128)(2,1)} copy(bf16[3,66,64,1,128]{4,2,1,0,3:T(8,128)(2,1)} %maximum_bitcast_fusion.2) | data formatting | bytes 6488064
  343.1 7.8 %pad.7.clone = bf16[3,66,64,1,136]{1,2,4,0,3:T(8,128)(2,1)} pad(bf16[3,66,64,1,128]{1,2,4,0,3:T(8,128)(2,1)} %copy.137, bf16[]{:T(256)} %constant.25.clone.1), padding=0_0x0_0x0_0x0_0x1_7 | pad | bytes 6690818 | tf_op jit(solution)/shard_map/broadcast_in_dim | solution.py:25
  350.9 11.7 %copy.107 = bf16[3,66,64,1,8,17]{2,4,5,1,0,3:T(8,128)(2,1)} copy(bf16[3,66,64,1,8,17]{1,2,5,4,0,3:T(8,128)(2,1)} %bitcast.156) | data formatting | bytes 6893568 | tf_op jit(solution)/shard_map/conv_general_dilated | solution.py:24
  364.0 11.2 %broadcast_select_fusion.2 = f32[1,64,8,17,64]{4,2,3,1,0:T(8,128)S(1)} fusion(pred[8,17]{0,1:T(8,128)(4,1)S(1)} %copy-done.11, bf16[3,3,3,64,64]{4,3,2,1,0:T(8,128)(2,1)S(1)} %copy-done.7, bf16[3,66,64,1,7,2]{2,4,5,1,0,3:T(8,128)(2,1)S(1)} %slice.73, bf16[3,66,64,1,8,17]{2,4,5,1,0,3:T(8,128)(2,1)} %copy.107), kind=kOutput, calls=%fused_computation.55 | convolution fusion | flops 1937299456 | bytes 6251144 | tf_op jit(solution)/shard_map/conv_general_dilated | solution.py:24
  403.1 20.0 %all-to-all-start = ((bf16[32,2,2048]{2,1,0:T(2,128)(2,1)}), bf16[32,2,2048]{2,1,0:T(2,128)(2,1)S(1)}, u32[]{:S(2)}, u32[]{:S(2)}) async-start(bf16[32,2,2048]{2,1,0:T(2,128)(2,1)} %reshape.239), calls=%async_computation.1 | async-start | bytes 524288 | tf_op jit(solution)/shard_map/all_to_all | solution.py:129
  447.1 183.8 %reduce-scatter.2.cloned.1.call-done = f32[1,16,128]{2,1,0:T(8,128)} async-done(((f32[32,16,128]{2,1,0:T(8,128)}), f32[1,16,128]{2,1,0:T(8,128)}) %reduce-scatter.2.cloned.1.call-update) | async-done | bytes 8208 | tf_op jit(solution)/shard_map/reduce_scatter | solution.py:127
  (114 shorter events, 180.2 us)
Async XLA Ops:
  7.2 184.5 %copy-start = (bf16[3,3,3,64,64]{4,3,2,1,0:T(8,128)(2,1)S(1)}, bf16[3,3,3,64,64]{4,3,2,1,0:T(8,128)(2,1)}, u32[]{:S(2)}) copy-start(bf16[3,3,3,64,64]{4,3,2,1,0:T(8,128)(2,1)} %param.12) | copy-start | bytes 663556
  7.2 28.4 %collective-permute-start.9 = (bf16[1,64,64,128]{3,2,1,0:T(8,128)(2,1)}, bf16[1,64,64,128]{3,2,1,0:T(8,128)(2,1)}, u32[]{:S(2)}, u32[]{:S(2)}) collective-permute-start(bf16[1,64,64,128]{3,2,1,0:T(8,128)(2,1)} %param.11), channel_id=1, source_target_pairs={{4,0},{8,4},{12,8},{16,12},{20,16},{24,20},{28,24},{32,28},{36,32}... | collective-permute-start | bytes 3145736 | tf_op jit(solution)/shard_map/ppermute | solution.py:17
  8.6 32.5 %collective-permute-start.8 = (bf16[1,64,64,128]{3,2,1,0:T(8,128)(2,1)}, bf16[1,64,64,128]{3,2,1,0:T(8,128)(2,1)}, u32[]{:S(2)}, u32[]{:S(2)}) collective-permute-start(bf16[1,64,64,128]{3,2,1,0:T(8,128)(2,1)} %param.11), channel_id=1, source_target_pairs={{0,4},{4,8},{8,12},{12,16},{16,20},{20,24},{24,28},{28,32},{32,36}... | collective-permute-start | bytes 3145736 | tf_op jit(solution)/shard_map/ppermute | solution.py:16
  16.9 60.8 %collective-permute-start.1 = (bf16[1,64,64,128]{3,2,1,0:T(8,128)(2,1)}, bf16[1,64,64,128]{3,2,1,0:T(8,128)(2,1)}, u32[]{:S(2)}, u32[]{:S(2)}) collective-permute-start(bf16[1,64,64,128]{3,2,1,0:T(8,128)(2,1)} %fusion.48), channel_id=1, source_target_pairs={{4,0},{8,4},{12,8},{16,12},{20,16},{24,20},{28,24},{32,28},{36,32}... | collective-permute-start | bytes 3145736 | tf_op jit(solution)/shard_map/ppermute | solution.py:17
  18.2 59.5 %collective-permute-start = (bf16[1,64,64,128]{3,2,1,0:T(8,128)(2,1)}, bf16[1,64,64,128]{3,2,1,0:T(8,128)(2,1)}, u32[]{:S(2)}, u32[]{:S(2)}) collective-permute-start(bf16[1,64,64,128]{3,2,1,0:T(8,128)(2,1)} %fusion.48), channel_id=1, source_target_pairs={{0,4},{4,8},{8,12},{12,16},{16,20},{20,24},{24,28},{28,32},{32,36}... | collective-permute-start | bytes 3145736 | tf_op jit(solution)/shard_map/ppermute | solution.py:16
  64.7 19.4 %collective-permute-start.11 = (bf16[3,1,64,128]{3,2,1,0:T(8,128)(2,1)S(1)}, bf16[3,1,64,128]{3,2,1,0:T(8,128)(2,1)S(1)}, u32[]{:S(2)}, u32[]{:S(2)}) collective-permute-start(bf16[3,1,64,128]{3,2,1,0:T(8,128)(2,1)S(1)} %copy.114), channel_id=1, source_target_pairs={{1,0},{2,1},{3,2},{5,4},{6,5},{7,6},{9,8},{10,9},{11,10},{13,12},{... | collective-permute-start | bytes 147464 | tf_op jit(solution)/shard_map/ppermute | solution.py:17
  74.6 19.3 %collective-permute-start.10 = (bf16[3,1,64,128]{3,2,1,0:T(8,128)(2,1)S(1)}, bf16[3,1,64,128]{3,2,1,0:T(8,128)(2,1)S(1)}, u32[]{:S(2)}, u32[]{:S(2)}) collective-permute-start(bf16[3,1,64,128]{3,2,1,0:T(8,128)(2,1)S(1)} %copy.113), channel_id=1, source_target_pairs={{0,1},{1,2},{2,3},{4,5},{5,6},{6,7},{8,9},{9,10},{10,11},{12,13},{... | collective-permute-start | bytes 147464 | tf_op jit(solution)/shard_map/ppermute | solution.py:16
  78.5 80.1 %collective-permute-start.3 = (bf16[3,1,64,128]{3,2,1,0:T(8,128)(2,1)S(1)}, bf16[3,1,64,128]{3,2,1,0:T(8,128)(2,1)S(1)}, u32[]{:S(2)}, u32[]{:S(2)}) collective-permute-start(bf16[3,1,64,128]{3,2,1,0:T(8,128)(2,1)S(1)} %get-tuple-element.19), channel_id=1, source_target_pairs={{1,0},{2,1},{3,2},{5,4},{6,5},{7,6},{9,8},{10,9},{11,10},{13,12},{... | collective-permute-start | bytes 147464 | tf_op jit(solution)/shard_map/ppermute | solution.py:17
  79.8 78.9 %collective-permute-start.2 = (bf16[3,1,64,128]{3,2,1,0:T(8,128)(2,1)S(1)}, bf16[3,1,64,128]{3,2,1,0:T(8,128)(2,1)S(1)}, u32[]{:S(2)}, u32[]{:S(2)}) collective-permute-start(bf16[3,1,64,128]{3,2,1,0:T(8,128)(2,1)S(1)} %get-tuple-element.18), channel_id=1, source_target_pairs={{0,1},{1,2},{2,3},{4,5},{5,6},{6,7},{8,9},{9,10},{10,11},{12,13},{... | collective-permute-start | bytes 147464 | tf_op jit(solution)/shard_map/ppermute | solution.py:16
  211.0 17.0 %copy-start.9 = (s32[8]{0:T(128)S(1)}, s32[8]{0:T(128)}, u32[]{:S(2)}) copy-start(s32[8]{0:T(128)} %param.19) | copy-start | bytes 100
  214.4 27.3 %collective-permute-start.13 = (bf16[1,64,64,128]{3,2,1,0:T(8,128)(2,1)S(1)}, bf16[1,64,64,128]{3,2,1,0:T(8,128)(2,1)}, u32[]{:S(2)}, u32[]{:S(2)}) collective-permute-start(bf16[1,64,64,128]{3,2,1,0:T(8,128)(2,1)S(1)} %get-tuple-element.20), channel_id=1, source_target_pairs={{4,0},{8,4},{12,8},{16,12},{20,16},{24,20},{28,24},{32,28},{36,32}... | collective-permute-start | bytes 3145736 | tf_op jit(solution)/shard_map/ppermute | solution.py:17
  215.7 27.7 %collective-permute-start.12 = (bf16[1,64,64,128]{3,2,1,0:T(8,128)(2,1)S(1)}, bf16[1,64,64,128]{3,2,1,0:T(8,128)(2,1)}, u32[]{:S(2)}, u32[]{:S(2)}) collective-permute-start(bf16[1,64,64,128]{3,2,1,0:T(8,128)(2,1)S(1)} %get-tuple-element.20), channel_id=1, source_target_pairs={{0,4},{4,8},{8,12},{12,16},{16,20},{20,24},{24,28},{28,32},{32,36}... | collective-permute-start | bytes 3145736 | tf_op jit(solution)/shard_map/ppermute | solution.py:16
  221.2 43.0 %collective-permute-start.5 = (bf16[1,64,64,128]{3,2,1,0:T(8,128)(2,1)S(1)}, bf16[1,64,64,128]{3,2,1,0:T(8,128)(2,1)}, u32[]{:S(2)}, u32[]{:S(2)}) collective-permute-start(bf16[1,64,64,128]{3,2,1,0:T(8,128)(2,1)S(1)} %get-tuple-element.21), channel_id=1, source_target_pairs={{4,0},{8,4},{12,8},{16,12},{20,16},{24,20},{28,24},{32,28},{36,32}... | collective-permute-start | bytes 3145736 | tf_op jit(solution)/shard_map/ppermute | solution.py:17
  222.5 43.4 %collective-permute-start.4 = (bf16[1,64,64,128]{3,2,1,0:T(8,128)(2,1)S(1)}, bf16[1,64,64,128]{3,2,1,0:T(8,128)(2,1)}, u32[]{:S(2)}, u32[]{:S(2)}) collective-permute-start(bf16[1,64,64,128]{3,2,1,0:T(8,128)(2,1)S(1)} %get-tuple-element.21), channel_id=1, source_target_pairs={{0,4},{4,8},{8,12},{12,16},{16,20},{20,24},{24,28},{28,32},{32,36}... | collective-permute-start | bytes 3145736 | tf_op jit(solution)/shard_map/ppermute | solution.py:16
  244.2 26.8 %collective-permute-start.15 = (bf16[3,1,64,128]{3,2,1,0:T(8,128)(2,1)S(1)}, bf16[3,1,64,128]{3,2,1,0:T(8,128)(2,1)S(1)}, u32[]{:S(2)}, u32[]{:S(2)}) collective-permute-start(bf16[3,1,64,128]{3,2,1,0:T(8,128)(2,1)S(1)} %get-tuple-element.15), channel_id=1, source_target_pairs={{1,0},{2,1},{3,2},{5,4},{6,5},{7,6},{9,8},{10,9},{11,10},{13,12},{... | collective-permute-start | bytes 147464 | tf_op jit(solution)/shard_map/ppermute | solution.py:17
  245.5 25.5 %collective-permute-start.14 = (bf16[3,1,64,128]{3,2,1,0:T(8,128)(2,1)S(1)}, bf16[3,1,64,128]{3,2,1,0:T(8,128)(2,1)S(1)}, u32[]{:S(2)}, u32[]{:S(2)}) collective-permute-start(bf16[3,1,64,128]{3,2,1,0:T(8,128)(2,1)S(1)} %get-tuple-element.14), channel_id=1, source_target_pairs={{0,1},{1,2},{2,3},{4,5},{5,6},{6,7},{8,9},{9,10},{10,11},{12,13},{... | collective-permute-start | bytes 147464 | tf_op jit(solution)/shard_map/ppermute | solution.py:16
  266.6 64.7 %collective-permute-start.7 = (bf16[3,1,64,128]{3,2,1,0:T(8,128)(2,1)S(1)}, bf16[3,1,64,128]{3,2,1,0:T(8,128)(2,1)S(1)}, u32[]{:S(2)}, u32[]{:S(2)}) collective-permute-start(bf16[3,1,64,128]{3,2,1,0:T(8,128)(2,1)S(1)} %get-tuple-element.17), channel_id=1, source_target_pairs={{1,0},{2,1},{3,2},{5,4},{6,5},{7,6},{9,8},{10,9},{11,10},{13,12},{... | collective-permute-start | bytes 147464 | tf_op jit(solution)/shard_map/ppermute | solution.py:17
  267.9 63.4 %collective-permute-start.6 = (bf16[3,1,64,128]{3,2,1,0:T(8,128)(2,1)S(1)}, bf16[3,1,64,128]{3,2,1,0:T(8,128)(2,1)S(1)}, u32[]{:S(2)}, u32[]{:S(2)}) collective-permute-start(bf16[3,1,64,128]{3,2,1,0:T(8,128)(2,1)S(1)} %get-tuple-element.16), channel_id=1, source_target_pairs={{0,1},{1,2},{2,3},{4,5},{5,6},{6,7},{8,9},{9,10},{10,11},{12,13},{... | collective-permute-start | bytes 147464 | tf_op jit(solution)/shard_map/ppermute | solution.py:16
  388.3 35.0 %copy-start.2 = (bf16[1,64,64,128]{3,2,1,0:T(8,128)(2,1)}, bf16[1,64,64,128]{3,2,1,0:T(8,128)(2,1)S(1)}, u32[]{:S(2)}) copy-start(bf16[1,64,64,128]{3,2,1,0:T(8,128)(2,1)S(1)} %get-tuple-element.25) | copy-start | bytes 3145732
  390.7 32.5 %collective-permute-start.17 = (bf16[1,1,64,128]{3,2,1,0:T(8,128)(2,1)S(1)}, bf16[1,1,64,128]{3,2,1,0:T(8,128)(2,1)S(1)}, u32[]{:S(2)}, u32[]{:S(2)}) collective-permute-start(bf16[1,1,64,128]{3,2,1,0:T(8,128)(2,1)S(1)} %get-tuple-element.23), channel_id=1, source_target_pairs={{1,0},{2,1},{3,2},{5,4},{6,5},{7,6},{9,8},{10,9},{11,10},{13,12},{... | collective-permute-start | bytes 49160 | tf_op jit(solution)/shard_map/ppermute | solution.py:17
  392.0 31.2 %collective-permute-start.16 = (bf16[1,1,64,128]{3,2,1,0:T(8,128)(2,1)S(1)}, bf16[1,1,64,128]{3,2,1,0:T(8,128)(2,1)S(1)}, u32[]{:S(2)}, u32[]{:S(2)}) collective-permute-start(bf16[1,1,64,128]{3,2,1,0:T(8,128)(2,1)S(1)} %get-tuple-element.22), channel_id=1, source_target_pairs={{0,1},{1,2},{2,3},{4,5},{5,6},{6,7},{8,9},{9,10},{10,11},{12,13},{... | collective-permute-start | bytes 49160 | tf_op jit(solution)/shard_map/ppermute | solution.py:16
  403.1 41.6 %all-to-all-start = ((bf16[32,2,2048]{2,1,0:T(2,128)(2,1)}), bf16[32,2,2048]{2,1,0:T(2,128)(2,1)S(1)}, u32[]{:S(2)}, u32[]{:S(2)}) async-start(bf16[32,2,2048]{2,1,0:T(2,128)(2,1)} %reshape.239), calls=%async_computation.1 | async-start | bytes 524288 | tf_op jit(solution)/shard_map/all_to_all | solution.py:129
  423.2 207.7 %reduce-scatter.2.cloned.1.call-start = ((), (), s32[]{:S(2)}) async-start(), calls=%async_computation.2 | async-start | bytes 270336 | tf_op jit(solution)/shard_map/reduce_scatter | solution.py:127
  445.2 185.7 %copy-start.1 = (bf16[3,3,3,64,64]{4,3,2,1,0:T(8,128)(2,1)S(1)}, bf16[3,3,3,64,64]{4,3,2,1,0:T(8,128)(2,1)}, u32[]{:S(2)}) copy-start(bf16[3,3,3,64,64]{4,3,2,1,0:T(8,128)(2,1)} %param.12) | copy-start | bytes 663556
  (8 other events, 46.8 us)
Sparse Core Ops, SparseCore 0:
  444.9 185.9 reduce-scatter.1
where the time goes:
time: 648 us; the launch traced here: 638 us
  waiting for transfers between devices  223 us (34%)
  local copies, waits for them, and re-layouts  212 us (33%)
  starting transfers between devices  71.9 us (11%)
  matrix products  71.9 us (11%)
  other arithmetic  44 us (7%)
  between operations  15 us (2%)
    reduce_scatter x1, waiting for transfers between devices, shards(): lax.psum_scatter(picked, 'tm', scatter_dimension=0, tiled=True)[:, None]  184 us
    conv_general_dilated x16, local copies, waits for them, and re-layouts, cube_conv(): lax.conv_general_dilated(padded[None], kernel, (1, 1, 1), [(0, 0), (0, 0)...  66 us
    conv_general_dilated x4, matrix products, cube_conv(): lax.conv_general_dilated(padded[None], kernel, (1, 1, 1), [(0, 0), (0, 0)...  60.5 us
    unnamed x35, local copies, waits for them, and re-layouts  54.5 us
    ppermute x9, starting transfers between devices, padded_2(): before = lax.ppermute(last, axis, up)  40.1 us
    ppermute x9, waiting for transfers between devices, padded_2(): after = lax.ppermute(initial, axis, down)  36.1 us
    broadcast_in_dim x4, local copies, waits for them, and re-layouts, cube_conv(): padded[None]  28 us
    broadcast_in_dim x4, other arithmetic, cube_conv(): padded[None]  20.6 us
  transfers between devices with their start and end apart: 20, of which 6 were waited for; matrix products, arithmetic and copies ran while one was open for 33% of the time, Pallas kernels for 0%

commit v1 on v0

v1 whole, which is shorter than its diff:
```python
import functools

import jax
import jax.numpy as jnp
from jax import lax
from jax.experimental import pallas as pl
from jax.experimental.pallas import tpu as pltpu
from jax.sharding import PartitionSpec as P

LISTED = 8
F32 = jnp.float32
BF16 = jnp.bfloat16
MIB = 1 << 20


def logistic(x):
    return 0.5 + 0.5 * jnp.tanh(0.5 * x)


def shifted(x, lane):
    width = x.shape[1]
    left = jnp.where(lane == 0, jnp.zeros_like(x), pltpu.roll(x, 1, 1))
    right = jnp.where(lane == width - 1, jnp.zeros_like(x), pltpu.roll(x, width - 1, 1))
    return left, x, right


def taps(x, silu_in):
    x = x.astype(F32)
    lane = lax.broadcasted_iota(jnp.int32, x.shape, 1)
    if silu_in:
        x = x * logistic(x)
    return [t.astype(BF16) for t in shifted(x, lane)]


def conv_rows(load, weight_ref, rows, emit, silu_in=False, frames=3):
    def pair(p):
        sides = []
        for j in range(2):
            parts = []
            for a in range(frames):
                parts += taps(load(a, 2 * p + j), silu_in)
            sides.append(jnp.concatenate(parts, axis=0))
        y = jnp.dot(weight_ref[...], jnp.concatenate(sides, axis=1), preferred_element_type=F32)
        n, w = y.shape[0] // 3, y.shape[1] // 2
        return [[y[b * n : (b + 1) * n, j * w : (j + 1) * w] for j in range(2)] for b in range(3)]

    y = pair(0)
    carry = (y[0][0] + y[1][1], y[0][1])

    def step(p, carry):
        y = pair(p)
        emit(2 * p - 2, carry[0] + y[2][0])
        emit(2 * p - 1, carry[1] + y[1][0] + y[2][1])
        return (y[0][0] + y[1][1], y[0][1])

    lax.fori_loop(1, rows // 2, step, carry)


def copies(pairs, sems):
    todo = [pltpu.make_async_copy(s, d, sems.at[i]) for i, (s, d) in enumerate(pairs)]
    for t in todo:
        t.start()
    for t in todo:
        t.wait()


def row_mask(first, r, limit):
    g = first + r
    return jnp.where((g >= 0) & (g < limit), 1.0, 0.0).astype(F32)


def first_kernel(pos, w, own, prev, nxt, up, dn, cor_p, cor_n, inner, slope, vol, sems):
    n = own.shape[0]
    copies(
        [
            (prev, vol.at[0, pl.ds(3, n)]),
            (own, vol.at[1, pl.ds(3, n)]),
            (nxt, vol.at[2, pl.ds(3, n)]),
            (up.at[pl.ds(0, 3)], vol.at[1, pl.ds(0, 3)]),
            (dn.at[pl.ds(0, 3)], vol.at[1, pl.ds(n + 3, 3)]),
            (cor_p.at[pl.ds(0, 3)], vol.at[0, pl.ds(0, 3)]),
            (cor_p.at[pl.ds(5, 3)], vol.at[0, pl.ds(n + 3, 3)]),
            (cor_n.at[pl.ds(0, 3)], vol.at[2, pl.ds(0, 3)]),
            (cor_n.at[pl.ds(5, 3)], vol.at[2, pl.ds(n + 3, 3)]),
        ],
        sems,
    )

    def emit(r, pre):
        s = logistic(pre)
        act = pre * s
        inner[r] = (act * row_mask(pos[0] - 2, r, pos[1])).astype(BF16)
        slope[r] = (s + act * (1.0 - s)).astype(BF16)

    conv_rows(lambda a, i: vol[a, i], w, n + 6, emit, silu_in=True)


def grad_kernel(pos, w, slope, own, prev, nxt, up, dn, cor_p, cor_n, grad, vol, sems):
    n = own.shape[0]
    copies(
        [
            (prev, vol.at[0, pl.ds(2, n)]),
            (own, vol.at[1, pl.ds(2, n)]),
            (nxt, vol.at[2, pl.ds(2, n)]),
            (up.at[pl.ds(3, 2)], vol.at[1, pl.ds(0, 2)]),
            (dn.at[pl.ds(3, 2)], vol.at[1, pl.ds(n + 2, 2)]),
            (cor_p.at[pl.ds(3, 2)], vol.at[0, pl.ds(0, 2)]),
            (cor_p.at[pl.ds(8, 2)], vol.at[0, pl.ds(n + 2, 2)]),
            (cor_n.at[pl.ds(3, 2)], vol.at[2, pl.ds(0, 2)]),
            (cor_n.at[pl.ds(8, 2)], vol.at[2, pl.ds(n + 2, 2)]),
        ],
        sems,
    )

    def emit(r, value):
        out = value * slope[r + 1].astype(F32)
        grad[r] = (out * row_mask(pos[0] - 1, r, pos[1])).astype(BF16)

    conv_rows(lambda a, i: vol[a, i], w, n + 4, emit)


def video_kernel(
    pos, listed, w, wp, head, pool, base, up, dn, own, prev, nxt, video, send, rim, sums, sems
):
    n = base.shape[0]
    copies(
        [
            (base, rim.at[pl.ds(1, n)]),
            (up.at[pl.ds(2, 1)], rim.at[pl.ds(0, 1)]),
            (dn.at[pl.ds(0, 1)], rim.at[pl.ds(n + 1, 1)]),
        ],
        sems,
    )
    vol = (prev, own, nxt)

    def emit(r, value):
        out = (rim[r].astype(F32) + value) * row_mask(pos[0] - 1, r, pos[1])
        rim[r] = out.astype(BF16)

    conv_rows(lambda a, i: vol[a][i], w, n + 4, emit)

    def emit_plane(r, value):
        act = value * logistic(value) * head[...]
        sums[pl.ds(r, 1)] = jnp.sum(act, axis=0, keepdims=True)

    conv_rows(lambda a, i: rim[i], wp, n + 2, emit_plane, frames=1)

    def pool_row(i, _):
        a, b = rim[2 * i + 1], rim[2 * i + 2]
        video[2 * i] = a
        video[2 * i + 1] = b
        both = jnp.dot(jnp.concatenate([a, b], axis=1), pool[...], preferred_element_type=F32)
        half = both.shape[0] // 2
        lane = lax.broadcasted_iota(jnp.int32, (half, both.shape[1]), 1)
        packed = jnp.where(lane < both.shape[1] // 2, both[:half], both[half:])
        send[i, pl.ds(0, half)] = packed.astype(BF16)
        return 0

    lax.fori_loop(0, n // 2, pool_row, 0)

    dests = send.shape[0]
    groups = dests // LISTED
    quarter = n // groups
    base_row = send.shape[1] - quarter
    for k in range(LISTED):
        hit = jnp.where(listed[k] == pos[2], 1.0, 0.0).astype(F32)
        for q in range(groups):
            send[k * groups + q, pl.ds(base_row, quarter)] = (
                sums[q * quarter : (q + 1) * quarter] * hit
            ).astype(BF16)


def input_grad_kernel(w, cot, vin, own, prev, nxt, out):
    n = cot.shape[0]
    vol = (prev, own, nxt)

    def emit(r, value):
        x = vin[r].astype(F32)
        s = logistic(x)
        out[r] = (cot[r].astype(F32) + value * (s * (1.0 + x * (1.0 - s)))).astype(BF16)

    conv_rows(lambda a, i: vol[a][i], w, n + 2, emit)


def time_kernel_body(pos, listed, wt, mixer, head, recv, plane, score, total):
    frames = recv.shape[0]
    half, width = wt.shape[1] // 3, recv.shape[2]
    units = wt.shape[0] // 2
    plane[...] = recv[listed[pos[2] // (frames // LISTED)], pl.ds(half, plane.shape[0])].astype(F32)
    total[...] = jnp.zeros_like(total)
    lane = lax.broadcasted_iota(jnp.int32, (units, width), 1)

    def piece(t):
        ok = jnp.where((t >= 0) & (t < frames), 1.0, 0.0).astype(BF16)
        return recv[jnp.clip(t, 0, frames - 1), pl.ds(0, half)] * ok

    def step(i, _):
        f = [piece(2 * i + d) for d in (-1, 0, 1, 2)]
        rhs = jnp.concatenate(
            [jnp.concatenate(f[:3], axis=0), jnp.concatenate(f[1:], axis=0)], axis=1
        )
        y = jnp.dot(wt[...], rhs, preferred_element_type=F32)
        a, b = y[:, :width], y[:, width:]
        left = a[:units] + pltpu.roll(a[units:], width // 2, 1)
        right = pltpu.roll(b[:units], width // 2, 1) + b[units:]
        q = jnp.where(lane < width // 2, left, right)
        total[...] += q * logistic(q)
        return 0

    lax.fori_loop(0, frames // 2, step, 0)
    both = total[...]
    mean = (both + pltpu.roll(both, width // 2, 1)) * (1.0 / frames)
    mixed = jnp.zeros_like(mean)
    rest = mean
    for _ in range(3):
        top = rest.astype(BF16)
        mixed = mixed + jnp.dot(mixer[...], top, preferred_element_type=F32)
        rest = rest - top.astype(F32)
    act = mixed * logistic(mixed) * head[...]
    score[...] = jnp.sum(act, axis=0, keepdims=True)[:, : width // 2]


VMEM = pl.BlockSpec(memory_space=pltpu.VMEM)
SMEM = pl.BlockSpec(memory_space=pltpu.SMEM)
ANY = pl.BlockSpec(memory_space=pl.ANY)


def call(body, outs, in_specs, scratch, flops, nbytes, limit=40):
    return pl.pallas_call(
        body,
        out_shape=outs,
        in_specs=in_specs,
        out_specs=jax.tree.map(lambda _: VMEM, outs),
        scratch_shapes=scratch,
        compiler_params=pltpu.CompilerParams(vmem_limit_bytes=limit * MIB),
        cost_estimate=pl.CostEstimate(flops=flops, bytes_accessed=nbytes, transcendentals=0),
    )


def stacked(kernel):
    a, b, e, c, o = kernel.shape
    return jnp.transpose(kernel, (1, 4, 0, 2, 3)).reshape(b * o, a * e * c)


def flipped(kernel):
    return jnp.swapaxes(kernel[::-1, ::-1, ::-1], 3, 4)


def shards(
    video_in,
    cotangent,
    kernel_a,
    kernel_b,
    plane_kernel,
    plane_head,
    time_kernel,
    time_mixer,
    time_head,
    listed,
):
    v, c = video_in[0], cotangent[0]
    n, ch, width = v.shape
    tm, sp = lax.axis_size("tm"), lax.axis_size("space")
    up_tm = [(i, i + 1) for i in range(tm - 1)]
    dn_tm = [(j, i) for i, j in up_tm]
    up_sp = [(i, i + 1) for i in range(sp - 1)]
    dn_sp = [(j, i) for i, j in up_sp]
    me = lax.axis_index("tm")
    pos = jnp.stack([lax.axis_index("space") * n, sp * n, me]).astype(jnp.int32)

    def both(x):
        return lax.ppermute(x, "tm", up_tm), lax.ppermute(x, "tm", dn_tm)

    up = lax.ppermute(jnp.concatenate([v[n - 3 :], c[n - 2 :]]), "space", up_sp)
    dn = lax.ppermute(jnp.concatenate([v[:3], c[:2]]), "space", dn_sp)
    v_p, v_n = both(v)
    cor_p, cor_n = both(jnp.concatenate([up, dn]))
    c_p, c_n = both(c)

    def rows(r, dtype=BF16):
        return jax.ShapeDtypeStruct((r, ch, width), dtype)

    def volume(r):
        return [pltpu.VMEM((3, r, ch, width), BF16), pltpu.SemaphoreType.DMA((9,))]

    flops = 2 * 27 * ch * ch * width * n
    wa, wb = stacked(kernel_a), stacked(kernel_b)
    wbt, wat = stacked(flipped(kernel_b)), stacked(flipped(kernel_a))
    inner, slope = call(
        first_kernel, (rows(n + 4), rows(n + 4)), [SMEM, VMEM] + [ANY] * 7, volume(n + 6), flops, 6 * MIB
    )(pos, wa, v, v_p, v_n, up, dn, cor_p, cor_n)
    in_p, in_n = both(inner)
    grad = call(
        grad_kernel, rows(n + 2), [SMEM, VMEM, VMEM] + [ANY] * 7, volume(n + 4), flops, 6 * MIB
    )(pos, wbt, slope, c, c_p, c_n, up, dn, cor_p, cor_n)
    gr_p, gr_n = both(grad)

    wp = stacked(plane_kernel[None])
    spread = lambda h: jnp.broadcast_to(h.astype(F32)[:, None], (ch, width))
    idx = jnp.arange(2 * width)[:, None] % width // 2
    pool = jnp.where(idx == jnp.arange(width)[None, :] % (width // 2), 0.25, 0.0).astype(BF16)
    quarter = n // (tm // LISTED)
    video, send = call(
        video_kernel,
        (rows(n), jax.ShapeDtypeStruct((tm, ch // 2 + quarter, width), BF16)),
        [SMEM, SMEM, VMEM, VMEM, VMEM, VMEM, ANY, ANY, ANY, VMEM, VMEM, VMEM],
        [
            pltpu.VMEM((n + 2, ch, width), BF16),
            pltpu.VMEM((n, width), F32),
            pltpu.SemaphoreType.DMA((3,)),
        ],
        flops * 4 // 3,
        6 * MIB,
    )(pos, listed, wb, wp, spread(plane_head), pool, v, up, dn, inner, in_p, in_n)
    recv = lax.all_to_all(send, "tm", split_axis=0, concat_axis=0, tiled=True)
    input_grad = call(input_grad_kernel, rows(n), [VMEM] * 6, [], flops, 6 * MIB)(
        wat, c, v, grad, gr_p, gr_n
    )
    wt = jnp.transpose(time_kernel.reshape(3, 2, ch // 2, ch), (1, 3, 0, 2)).reshape(2 * ch, 3 * ch // 2)
    plane_scores, time_scores = call(
        time_kernel_body,
        (jax.ShapeDtypeStruct((quarter, width), F32), jax.ShapeDtypeStruct((1, width // 2), F32)),
        [SMEM, SMEM, VMEM, VMEM, VMEM, VMEM],
        [pltpu.VMEM((ch, width), F32)],
        flops // 20,
        MIB,
    )(pos, listed, wt, time_mixer.T, spread(time_head), recv)
    return (video[None], input_grad[None], plane_scores[None, None], time_scores[None])


def solution(mesh):
    return jax.shard_map(
        shards,
        mesh=mesh,
        in_specs=(P("tm", "space", None, None), P("tm", "space", None, None)) + (P(),) * 8,
        out_specs=(
            P("tm", "space", None, None),
            P("tm", "space", None, None),
            P("tm", "space", None, None),
            P("space", "tm", None),
        ),
        check_vma=False,
    )
```

time: 648 us -> 194 us (0.30)
  the two profiles are of different devices: /device:TPU:0 before, /device:TPU:1 now
where the time goes in v1:
time: 194 us; the launch traced here: 192 us
  Pallas kernels  77 us (40%)
  starting transfers between devices  70.8 us (36%)
  waiting for transfers between devices  30.9 us (16%)
  local copies, waits for them, and re-layouts  12.2 us (6%)
    ppermute x10, starting transfers between devices, both(): return (lax.ppermute(x, 'tm', up_tm), lax.ppermute(x, 'tm', dn_tm))  43.7 us
    pallas_call x1, Pallas kernels, shards(): call(video_kernel, (rows(n), jax.ShapeDtypeStruct((tm, ch // 2 + quarter,...  27.8 us
    ppermute x10, waiting for transfers between devices, both(): return (lax.ppermute(x, 'tm', up_tm), lax.ppermute(x, 'tm', dn_tm))  25.2 us
    all_to_all x1, starting transfers between devices, shards(): recv = lax.all_to_all(send, 'tm', split_axis=0, concat_axis=0, tiled=True)  20.6 us
    pallas_call x1, Pallas kernels, shards(): call(first_kernel, (rows(n + 4), rows(n + 4)), [SMEM, VMEM] + [ANY] * 7,...  15.8 us
    pallas_call x1, Pallas kernels, shards(): call(grad_kernel, rows(n + 2), [SMEM, VMEM, VMEM] + [ANY] * 7, volume(n +...  14.4 us
    pallas_call x1, Pallas kernels, shards(): call(input_grad_kernel, rows(n), [VMEM] * 6, [], flops, 6 * MIB)  13.8 us
    pallas_call x1, Pallas kernels, shards(): call(time_kernel_body, (jax.ShapeDtypeStruct((quarter, width), F32), jax....  5.21 us
  transfers between devices with their start and end apart: 13, of which 5 were waited for; matrix products, arithmetic and copies ran while one was open for 5% of the time, Pallas kernels for 37%

profile of v1, /device:TPU:1, one launch (start us, length us, event | category | flops | bytes accessed | tf_op | source)
XLA Modules:
  0.0 192.1 jit_solution(12613391533286127534)
XLA Ops:
  0.6 4.1 %collective-permute-start.2 = (bf16[64,64,128]{2,1,0:T(8,128)(2,1)}, bf16[64,64,128]{2,1,0:T(8,128)(2,1)S(1)}, u32[]{:S(2)}, u32[]{:S(2)}) collective-permute-start(bf16[64,64,128]{2,1,0:T(8,128)(2,1)} %bitcast.35), channel_id=1, source_target_pairs={{0,4},{4,8},{8,12},{12,16},{16,20},{20,24},{24,28},{28,32},{32,36}... | collective-permute-start | bytes 3145736 | tf_op jit(solution)/shard_map/ppermute | solution.py:272
  4.7 1.3 collective-permute-start.3
  6.0 5.0 %collective-permute-start.8 = (bf16[64,64,128]{2,1,0:T(8,128)(2,1)}, bf16[64,64,128]{2,1,0:T(8,128)(2,1)}, u32[]{:S(2)}, u32[]{:S(2)}) collective-permute-start(bf16[64,64,128]{2,1,0:T(8,128)(2,1)} %bitcast.40), channel_id=1, source_target_pairs={{0,4},{4,8},{8,12},{12,16},{16,20},{20,24},{24,28},{28,32},{32,36}... | collective-permute-start | bytes 3145736 | tf_op jit(solution)/shard_map/ppermute | solution.py:272
  11.0 1.3 collective-permute-start.9
  14.0 4.5 %collective-permute-start = (bf16[5,64,128]{2,1,0:T(8,128)(2,1)S(1)}, bf16[5,64,128]{2,1,0:T(8,128)(2,1)S(1)}, u32[]{:S(2)}, u32[]{:S(2)}) collective-permute-start(bf16[5,64,128]{2,1,0:T(8,128)(2,1)S(1)} %pad_maximum_fusion), channel_id=1, source_target_pairs={{0,1},{1,2},{2,3},{4,5},{5,6},{6,7},{8,9},{9,10},{10,11},{12,13},{... | collective-permute-start | bytes 245768 | tf_op jit(solution)/shard_map/ppermute | solution.py:274
  18.5 1.4 collective-permute-done.up
  20.0 1.9 collective-permute-start.1
  22.5 4.2 %collective-permute-done.1.dn = bf16[5,64,128]{2,1,0:T(8,128)(2,1)S(1)} collective-permute-done((bf16[5,64,128]{2,1,0:T(8,128)(2,1)S(1)}, bf16[5,64,128]{2,1,0:T(8,128)(2,1)S(1)}, u32[]{:S(2)}, u32[]{:S(2)}) %collective-permute-start.1) | collective-permute-done | bytes 81952 | tf_op jit(solution)/shard_map/ppermute | solution.py:275
  27.4 4.3 %collective-permute-start.4 = (bf16[10,64,128]{2,1,0:T(8,128)(2,1)}, bf16[10,64,128]{2,1,0:T(8,128)(2,1)S(1)}, u32[]{:S(2)}, u32[]{:S(2)}) collective-permute-start(bf16[10,64,128]{2,1,0:T(8,128)(2,1)} %constant_dynamic-update-slice_fusion), channel_id=1, source_target_pairs={{0,4},{4,8},{8,12},{12,16},{16,20},{20,24},{24,28},{28,32},{32,36}... | collective-permute-start | bytes 491528 | tf_op jit(solution)/shard_map/ppermute | solution.py:272
  31.7 21.1 %collective-permute-done.4.cor_p = bf16[10,64,128]{2,1,0:T(8,128)(2,1)S(1)} collective-permute-done((bf16[10,64,128]{2,1,0:T(8,128)(2,1)}, bf16[10,64,128]{2,1,0:T(8,128)(2,1)S(1)}, u32[]{:S(2)}, u32[]{:S(2)}) %collective-permute-start.4) | collective-permute-done | bytes 163872 | tf_op jit(solution)/shard_map/ppermute | solution.py:272
  52.8 1.3 collective-permute-start.5
  54.1 1.6 copy.23
  56.2 3.9 %collective-permute-done.5.cor_n = bf16[10,64,128]{2,1,0:T(8,128)(2,1)S(1)} collective-permute-done((bf16[10,64,128]{2,1,0:T(8,128)(2,1)}, bf16[10,64,128]{2,1,0:T(8,128)(2,1)S(1)}, u32[]{:S(2)}, u32[]{:S(2)}) %collective-permute-start.5) | collective-permute-done | bytes 163872 | tf_op jit(solution)/shard_map/ppermute | solution.py:272
  60.2 15.8 %shard_map.129 = (bf16[68,64,128]{2,1,0:T(8,128)(2,1)}, bf16[68,64,128]{2,1,0:T(8,128)(2,1)S(1)}) custom-call(s32[3]{0:T(128)S(1)} %pad_add_fusion.pos, bf16[192,576]{1,0:T(8,128)(2,1)S(1)} %reshape.100.w, bf16[64,64,128]{2,1,0:T(8,128)(2,1)S(1)} %bitcast.37, bf16[64,64,128]{2,1,0:T(8,128)(2,1)S(1)} %collective-permute-done.2.prev, ...), custom_call_target="tpu_custom_call" | custom-call | flops 1811939328 | bytes 6291456 | tf_op jit(solution)/shard_map/pallas_call | solution.py:289
  77.0 15.2 %collective-permute-start.6 = (bf16[68,64,128]{2,1,0:T(8,128)(2,1)}, bf16[68,64,128]{2,1,0:T(8,128)(2,1)}, u32[]{:S(2)}, u32[]{:S(2)}) collective-permute-start(bf16[68,64,128]{2,1,0:T(8,128)(2,1)} %get-tuple-element.10.own), channel_id=1, source_target_pairs={{0,4},{4,8},{8,12},{12,16},{16,20},{20,24},{24,28},{28,32},{32,36}... | collective-permute-start | bytes 3342344 | tf_op jit(solution)/shard_map/ppermute | solution.py:272
  92.2 1.3 collective-permute-start.7
  94.7 1.2 copy-done.4
  96.0 14.4 %shard_map.131.own = bf16[66,64,128]{2,1,0:T(8,128)(2,1)} custom-call(s32[3]{0:T(128)S(1)} %pad_add_fusion.pos, bf16[192,576]{1,0:T(8,128)(2,1)S(1)} %reshape.102.w, bf16[68,64,128]{2,1,0:T(8,128)(2,1)S(1)} %copy-done.4, bf16[64,64,128]{2,1,0:T(8,128)(2,1)S(1)} %bitcast.42, bf16[64,64,128]{2,1,0:T(8,128)(2,1)} %collective-permute-done.8.prev, ...), custom_call_target="tpu_custom_call" | custom-call | flops 1811939328 | bytes 6291456 | tf_op jit(solution)/shard_map/pallas_call | solution.py:293
  110.4 8.7 %collective-permute-start.10 = (bf16[66,64,128]{2,1,0:T(8,128)(2,1)}, bf16[66,64,128]{2,1,0:T(8,128)(2,1)}, u32[]{:S(2)}, u32[]{:S(2)}) collective-permute-start(bf16[66,64,128]{2,1,0:T(8,128)(2,1)} %shard_map.131.own), channel_id=1, source_target_pairs={{0,4},{4,8},{8,12},{12,16},{16,20},{20,24},{24,28},{28,32},{32,36}... | collective-permute-start | bytes 3244040 | tf_op jit(solution)/shard_map/ppermute | solution.py:272
  119.1 1.3 collective-permute-start.11
  123.3 27.8 %shard_map.130 = (bf16[64,64,128]{2,1,0:T(8,128)(2,1)}, bf16[32,48,128]{2,1,0:T(8,128)(2,1)}) custom-call(s32[3]{0:T(128)S(1)} %pad_add_fusion.pos, s32[8]{0:T(128)S(1)} %copy-done.2, bf16[192,576]{1,0:T(8,128)(2,1)S(1)} %reshape.98.w, bf16[192,192]{1,0:T(8,128)(2,1)S(1)} %reshape.99.wp, f32[64,128]{1,0:T(8,128)S(1)} %broadcast_in_dim.38.head, ...), custom_call_target="tpu_custom_call" | custom-call | flops 2415919104 | bytes 6291456 | tf_op jit(solution)/shard_map/pallas_call | solution.py:303
  151.1 20.6 %all-to-all-start = ((bf16[32,48,128]{2,1,0:T(8,128)(2,1)}), bf16[32,48,128]{2,1,0:T(8,128)(2,1)S(1)}, u32[]{:S(2)}, u32[]{:S(2)}) async-start(bf16[32,48,128]{2,1,0:T(8,128)(2,1)} %get-tuple-element.13), calls=%async_computation | async-start | bytes 786432 | tf_op jit(solution)/shard_map/all_to_all | solution.py:315
  173.0 13.8 %shard_map.132 = bf16[64,64,128]{2,1,0:T(8,128)(2,1)} custom-call(bf16[192,576]{1,0:T(8,128)(2,1)S(1)} %reshape.101.w, bf16[64,64,128]{2,1,0:T(8,128)(2,1)S(1)} %bitcast.43, bf16[64,64,128]{2,1,0:T(8,128)(2,1)S(1)} %bitcast.39, bf16[66,64,128]{2,1,0:T(8,128)(2,1)} %shard_map.131.own, bf16[66,64,128]{2,1,0:T(8,128)(2,1)} %collective-permute-done.10.prev, ...), custom_call_target="tpu_custom_call" | custom-call | flops 1811939328 | bytes 6291456 | tf_op jit(solution)/shard_map/pallas_call | solution.py:316
  186.9 5.2 %shard_map.133 = (f32[16,128]{1,0:T(8,128)}, f32[1,64]{1,0:T(1,128)}) custom-call(s32[3]{0:T(128)S(1)} %pad_add_fusion.pos, s32[8]{0:T(128)S(1)} %copy-done.2, bf16[128,96]{1,0:T(8,128)(2,1)S(1)} %copy.28.wt, bf16[64,64]{1,0:T(8,128)(2,1)S(1)} %bitcast.34, f32[64,128]{1,0:T(8,128)S(1)} %broadcast_in_dim.43.head, bf16[32,48,128]{2,1,0:T(8,128)(2,1)S(1)} %all-to-all-done.recv), custom_call_target="tpu_custom_call" | custom-call | flops 90596968 | bytes 1048576 | tf_op jit(solution)/shard_map/pallas_call | solution.py:320
  (59 shorter events, 9.7 us)
Async XLA Ops:
  0.6 59.5 %collective-permute-start.2 = (bf16[64,64,128]{2,1,0:T(8,128)(2,1)}, bf16[64,64,128]{2,1,0:T(8,128)(2,1)S(1)}, u32[]{:S(2)}, u32[]{:S(2)}) collective-permute-start(bf16[64,64,128]{2,1,0:T(8,128)(2,1)} %bitcast.35), channel_id=1, source_target_pairs={{0,4},{4,8},{8,12},{12,16},{16,20},{20,24},{24,28},{28,32},{32,36}... | collective-permute-start | bytes 3145736 | tf_op jit(solution)/shard_map/ppermute | solution.py:272
  4.7 55.4 %collective-permute-start.3 = (bf16[64,64,128]{2,1,0:T(8,128)(2,1)}, bf16[64,64,128]{2,1,0:T(8,128)(2,1)}, u32[]{:S(2)}, u32[]{:S(2)}) collective-permute-start(bf16[64,64,128]{2,1,0:T(8,128)(2,1)} %bitcast.36), channel_id=1, source_target_pairs={{4,0},{8,4},{12,8},{16,12},{20,16},{24,20},{28,24},{32,28},{36,32}... | collective-permute-start | bytes 3145736 | tf_op jit(solution)/shard_map/ppermute | solution.py:272
  6.0 88.3 %collective-permute-start.8 = (bf16[64,64,128]{2,1,0:T(8,128)(2,1)}, bf16[64,64,128]{2,1,0:T(8,128)(2,1)}, u32[]{:S(2)}, u32[]{:S(2)}) collective-permute-start(bf16[64,64,128]{2,1,0:T(8,128)(2,1)} %bitcast.40), channel_id=1, source_target_pairs={{0,4},{4,8},{8,12},{12,16},{16,20},{20,24},{24,28},{28,32},{32,36}... | collective-permute-start | bytes 3145736 | tf_op jit(solution)/shard_map/ppermute | solution.py:272
  11.0 83.3 %collective-permute-start.9 = (bf16[64,64,128]{2,1,0:T(8,128)(2,1)}, bf16[64,64,128]{2,1,0:T(8,128)(2,1)}, u32[]{:S(2)}, u32[]{:S(2)}) collective-permute-start(bf16[64,64,128]{2,1,0:T(8,128)(2,1)} %bitcast.41), channel_id=1, source_target_pairs={{4,0},{8,4},{12,8},{16,12},{20,16},{24,20},{28,24},{32,28},{36,32}... | collective-permute-start | bytes 3145736 | tf_op jit(solution)/shard_map/ppermute | solution.py:272
  14.0 6.0 %collective-permute-start = (bf16[5,64,128]{2,1,0:T(8,128)(2,1)S(1)}, bf16[5,64,128]{2,1,0:T(8,128)(2,1)S(1)}, u32[]{:S(2)}, u32[]{:S(2)}) collective-permute-start(bf16[5,64,128]{2,1,0:T(8,128)(2,1)S(1)} %pad_maximum_fusion), channel_id=1, source_target_pairs={{0,1},{1,2},{2,3},{4,5},{5,6},{6,7},{8,9},{9,10},{10,11},{12,13},{... | collective-permute-start | bytes 245768 | tf_op jit(solution)/shard_map/ppermute | solution.py:274
  18.5 41.6 %copy-start = (bf16[1,64,64,128]{3,2,1,0:T(8,128)(2,1)S(1)}, bf16[1,64,64,128]{3,2,1,0:T(8,128)(2,1)}, u32[]{:S(2)}) copy-start(bf16[1,64,64,128]{3,2,1,0:T(8,128)(2,1)} %param.10) | copy-start | bytes 3145732
  20.0 6.8 %collective-permute-start.1 = (bf16[5,64,128]{2,1,0:T(8,128)(2,1)S(1)}, bf16[5,64,128]{2,1,0:T(8,128)(2,1)S(1)}, u32[]{:S(2)}, u32[]{:S(2)}) collective-permute-start(bf16[5,64,128]{2,1,0:T(8,128)(2,1)S(1)} %pad_maximum_fusion.1), channel_id=1, source_target_pairs={{1,0},{2,1},{3,2},{5,4},{6,5},{7,6},{9,8},{10,9},{11,10},{13,12},{... | collective-permute-start | bytes 245768 | tf_op jit(solution)/shard_map/ppermute | solution.py:275
  27.4 25.4 %collective-permute-start.4 = (bf16[10,64,128]{2,1,0:T(8,128)(2,1)}, bf16[10,64,128]{2,1,0:T(8,128)(2,1)S(1)}, u32[]{:S(2)}, u32[]{:S(2)}) collective-permute-start(bf16[10,64,128]{2,1,0:T(8,128)(2,1)} %constant_dynamic-update-slice_fusion), channel_id=1, source_target_pairs={{0,4},{4,8},{8,12},{12,16},{16,20},{20,24},{24,28},{28,32},{32,36}... | collective-permute-start | bytes 491528 | tf_op jit(solution)/shard_map/ppermute | solution.py:272
  52.8 7.4 %collective-permute-start.5 = (bf16[10,64,128]{2,1,0:T(8,128)(2,1)}, bf16[10,64,128]{2,1,0:T(8,128)(2,1)S(1)}, u32[]{:S(2)}, u32[]{:S(2)}) collective-permute-start(bf16[10,64,128]{2,1,0:T(8,128)(2,1)} %constant_dynamic-update-slice_fusion), channel_id=1, source_target_pairs={{4,0},{8,4},{12,8},{16,12},{20,16},{24,20},{28,24},{32,28},{36,32}... | collective-permute-start | bytes 491528 | tf_op jit(solution)/shard_map/ppermute | solution.py:272
  56.2 37.3 %copy-start.5 = (bf16[3,3,3,64,64]{4,3,2,1,0:T(8,128)(2,1)S(1)}, bf16[3,3,3,64,64]{4,3,2,1,0:T(8,128)(2,1)}, u32[]{:S(2)}) copy-start(bf16[3,3,3,64,64]{4,3,2,1,0:T(8,128)(2,1)} %param.13) | copy-start | bytes 663556
  76.0 1.0 copy-start.3
  77.0 46.1 %collective-permute-start.6 = (bf16[68,64,128]{2,1,0:T(8,128)(2,1)}, bf16[68,64,128]{2,1,0:T(8,128)(2,1)}, u32[]{:S(2)}, u32[]{:S(2)}) collective-permute-start(bf16[68,64,128]{2,1,0:T(8,128)(2,1)} %get-tuple-element.10.own), channel_id=1, source_target_pairs={{0,4},{4,8},{8,12},{12,16},{16,20},{20,24},{24,28},{28,32},{32,36}... | collective-permute-start | bytes 3342344 | tf_op jit(solution)/shard_map/ppermute | solution.py:272
  92.2 31.1 %collective-permute-start.7 = (bf16[68,64,128]{2,1,0:T(8,128)(2,1)}, bf16[68,64,128]{2,1,0:T(8,128)(2,1)}, u32[]{:S(2)}, u32[]{:S(2)}) collective-permute-start(bf16[68,64,128]{2,1,0:T(8,128)(2,1)} %get-tuple-element.10.own), channel_id=1, source_target_pairs={{4,0},{8,4},{12,8},{16,12},{20,16},{24,20},{28,24},{32,28},{36,32}... | collective-permute-start | bytes 3342344 | tf_op jit(solution)/shard_map/ppermute | solution.py:272
  93.5 1.2 copy-start.1
  94.7 1.2 copy-start.4
  96.0 24.4 %copy-start.6 = (bf16[3,3,3,64,64]{4,3,2,1,0:T(8,128)(2,1)S(1)}, bf16[3,3,3,64,64]{4,3,2,1,0:T(8,128)(2,1)}, u32[]{:S(2)}) copy-start(bf16[3,3,3,64,64]{4,3,2,1,0:T(8,128)(2,1)} %param.13) | copy-start | bytes 663556
  110.4 62.6 %collective-permute-start.10 = (bf16[66,64,128]{2,1,0:T(8,128)(2,1)}, bf16[66,64,128]{2,1,0:T(8,128)(2,1)}, u32[]{:S(2)}, u32[]{:S(2)}) collective-permute-start(bf16[66,64,128]{2,1,0:T(8,128)(2,1)} %shard_map.131.own), channel_id=1, source_target_pairs={{0,4},{4,8},{8,12},{12,16},{16,20},{20,24},{24,28},{28,32},{32,36}... | collective-permute-start | bytes 3244040 | tf_op jit(solution)/shard_map/ppermute | solution.py:272
  119.1 53.9 %collective-permute-start.11 = (bf16[66,64,128]{2,1,0:T(8,128)(2,1)}, bf16[66,64,128]{2,1,0:T(8,128)(2,1)}, u32[]{:S(2)}, u32[]{:S(2)}) collective-permute-start(bf16[66,64,128]{2,1,0:T(8,128)(2,1)} %shard_map.131.own), channel_id=1, source_target_pairs={{4,0},{8,4},{12,8},{16,12},{20,16},{24,20},{28,24},{32,28},{36,32}... | collective-permute-start | bytes 3244040 | tf_op jit(solution)/shard_map/ppermute | solution.py:272
  120.4 2.8 %copy-start.10 = (bf16[64]{0:T(256)(128)(2,1)S(1)}, bf16[64]{0:T(256)(128)(2,1)}, u32[]{:S(2)}) copy-start(bf16[64]{0:T(256)(128)(2,1)} %param.15) | copy-start | bytes 388
  120.4 2.9 %copy-start.2 = (s32[8]{0:T(128)S(1)}, s32[8]{0:T(128)}, u32[]{:S(2)}) copy-start(s32[8]{0:T(128)} %listed.3) | copy-start | bytes 100
  123.3 48.4 %copy-start.7 = (bf16[3,3,3,64,64]{4,3,2,1,0:T(8,128)(2,1)S(1)}, bf16[3,3,3,64,64]{4,3,2,1,0:T(8,128)(2,1)}, u32[]{:S(2)}) copy-start(bf16[3,3,3,64,64]{4,3,2,1,0:T(8,128)(2,1)} %param.12) | copy-start | bytes 663556
  151.1 35.7 %all-to-all-start = ((bf16[32,48,128]{2,1,0:T(8,128)(2,1)}), bf16[32,48,128]{2,1,0:T(8,128)(2,1)S(1)}, u32[]{:S(2)}, u32[]{:S(2)}) async-start(bf16[32,48,128]{2,1,0:T(8,128)(2,1)} %get-tuple-element.13), calls=%async_computation | async-start | bytes 786432 | tf_op jit(solution)/shard_map/all_to_all | solution.py:315
  171.8 1.1 copy-start.9
  173.0 13.8 %copy-start.11 = (bf16[64]{0:T(256)(128)(2,1)S(1)}, bf16[64]{0:T(256)(128)(2,1)}, u32[]{:S(2)}) copy-start(bf16[64]{0:T(256)(128)(2,1)} %param.18) | copy-start | bytes 388
  (1 other events, 0.8 us)

commit v2 on v1

--- a/solution.py
+++ b/solution.py
@@ -11,6 +11,7 @@
 F32 = jnp.float32
 BF16 = jnp.bfloat16
 MIB = 1 << 20
+UNROLL = 16
 
 
 def logistic(x):
@@ -32,7 +33,7 @@
     return [t.astype(BF16) for t in shifted(x, lane)]
 
 
-def conv_rows(load, weight_ref, rows, emit, silu_in=False, frames=3):
+def conv_rows(load, weight_ref, rows, emit, silu_in=False, frames=3, unroll=UNROLL):
     def pair(p):
         sides = []
         for j in range(2):
@@ -53,7 +54,7 @@
         emit(2 * p - 1, carry[1] + y[1][0] + y[2][1])
         return (y[0][0] + y[1][1], y[0][1])
 
-    lax.fori_loop(1, rows // 2, step, carry)
+    lax.fori_loop(1, rows // 2, step, carry, unroll=unroll)
 
 
 def copies(pairs, sems):
@@ -79,9 +80,9 @@
             (up.at[pl.ds(0, 3)], vol.at[1, pl.ds(0, 3)]),
             (dn.at[pl.ds(0, 3)], vol.at[1, pl.ds(n + 3, 3)]),
             (cor_p.at[pl.ds(0, 3)], vol.at[0, pl.ds(0, 3)]),
-            (cor_p.at[pl.ds(5, 3)], vol.at[0, pl.ds(n + 3, 3)]),
+            (cor_p.at[pl.ds(3, 3)], vol.at[0, pl.ds(n + 3, 3)]),
             (cor_n.at[pl.ds(0, 3)], vol.at[2, pl.ds(0, 3)]),
-            (cor_n.at[pl.ds(5, 3)], vol.at[2, pl.ds(n + 3, 3)]),
+            (cor_n.at[pl.ds(3, 3)], vol.at[2, pl.ds(n + 3, 3)]),
         ],
         sems,
     )
@@ -95,28 +96,15 @@
     conv_rows(lambda a, i: vol[a, i], w, n + 6, emit, silu_in=True)
 
 
-def grad_kernel(pos, w, slope, own, prev, nxt, up, dn, cor_p, cor_n, grad, vol, sems):
-    n = own.shape[0]
-    copies(
-        [
-            (prev, vol.at[0, pl.ds(2, n)]),
-            (own, vol.at[1, pl.ds(2, n)]),
-            (nxt, vol.at[2, pl.ds(2, n)]),
-            (up.at[pl.ds(3, 2)], vol.at[1, pl.ds(0, 2)]),
-            (dn.at[pl.ds(3, 2)], vol.at[1, pl.ds(n + 2, 2)]),
-            (cor_p.at[pl.ds(3, 2)], vol.at[0, pl.ds(0, 2)]),
-            (cor_p.at[pl.ds(8, 2)], vol.at[0, pl.ds(n + 2, 2)]),
-            (cor_n.at[pl.ds(3, 2)], vol.at[2, pl.ds(0, 2)]),
-            (cor_n.at[pl.ds(8, 2)], vol.at[2, pl.ds(n + 2, 2)]),
-        ],
-        sems,
-    )
+def grad_kernel(pos, w, slope, own, prev, nxt, grad):
+    n = own.shape[0] - 4
+    vol = (prev, own, nxt)
 
     def emit(r, value):
         out = value * slope[r + 1].astype(F32)
         grad[r] = (out * row_mask(pos[0] - 1, r, pos[1])).astype(BF16)
 
-    conv_rows(lambda a, i: vol[a, i], w, n + 4, emit)
+    conv_rows(lambda a, i: vol[a][i], w, n + 4, emit)
 
 
 def video_kernel(
@@ -156,7 +144,7 @@
         send[i, pl.ds(0, half)] = packed.astype(BF16)
         return 0
 
-    lax.fori_loop(0, n // 2, pool_row, 0)
+    lax.fori_loop(0, n // 2, pool_row, 0, unroll=8)
 
     dests = send.shape[0]
     groups = dests // LISTED
@@ -207,7 +195,7 @@
         total[...] += q * logistic(q)
         return 0
 
-    lax.fori_loop(0, frames // 2, step, 0)
+    lax.fori_loop(0, frames // 2, step, 0, unroll=8)
     both = total[...]
     mean = (both + pltpu.roll(both, width // 2, 1)) * (1.0 / frames)
     mixed = jnp.zeros_like(mean)
@@ -274,8 +262,14 @@
     up = lax.ppermute(jnp.concatenate([v[n - 3 :], c[n - 2 :]]), "space", up_sp)
     dn = lax.ppermute(jnp.concatenate([v[:3], c[:2]]), "space", dn_sp)
     v_p, v_n = both(v)
-    cor_p, cor_n = both(jnp.concatenate([up, dn]))
-    c_p, c_n = both(c)
+    cor_p, cor_n = both(jnp.concatenate([up[:3], dn[:3]]))
+    wa, wb = stacked(kernel_a), stacked(kernel_b)
+    wbt, wat = stacked(flipped(kernel_b)), stacked(flipped(kernel_a))
+    c_own = jnp.concatenate([up[3:], c, dn[3:]])
+    c_own, cor_p, cor_n, wa, wb, wbt, wat = lax.optimization_barrier(
+        (c_own, cor_p, cor_n, wa, wb, wbt, wat)
+    )
+    c_p, c_n = both(c_own)
 
     def rows(r, dtype=BF16):
         return jax.ShapeDtypeStruct((r, ch, width), dtype)
@@ -284,15 +278,13 @@
         return [pltpu.VMEM((3, r, ch, width), BF16), pltpu.SemaphoreType.DMA((9,))]
 
     flops = 2 * 27 * ch * ch * width * n
-    wa, wb = stacked(kernel_a), stacked(kernel_b)
-    wbt, wat = stacked(flipped(kernel_b)), stacked(flipped(kernel_a))
     inner, slope = call(
         first_kernel, (rows(n + 4), rows(n + 4)), [SMEM, VMEM] + [ANY] * 7, volume(n + 6), flops, 6 * MIB
     )(pos, wa, v, v_p, v_n, up, dn, cor_p, cor_n)
     in_p, in_n = both(inner)
     grad = call(
-        grad_kernel, rows(n + 2), [SMEM, VMEM, VMEM] + [ANY] * 7, volume(n + 4), flops, 6 * MIB
-    )(pos, wbt, slope, c, c_p, c_n, up, dn, cor_p, cor_n)
+        grad_kernel, rows(n + 2), [SMEM] + [VMEM] * 5, [], flops, 6 * MIB
+    )(pos, wbt, slope, c_own, c_p, c_n)
     gr_p, gr_n = both(grad)
 
     wp = stacked(plane_kernel[None])

time: 194 us -> 143 us (0.74)
  Pallas kernels: 77 us -> 32 us
  waiting for transfers between devices: 30.9 us -> 20.7 us
  starting transfers between devices: 70.8 us -> 73.5 us
    pallas_call x1, Pallas kernels: 27.8 us -> 9.21 us  [shards(): call(video_kernel, (rows(n), jax.ShapeDtypeStruct((tm, ch // 2 + quarter,...]
    pallas_call x1, Pallas kernels: 14.4 us -> 6.35 us  [shards(): call(grad_kernel, rows(n + 2), [SMEM] + [VMEM] * 5, [], flops, 6 * MIB)]
    pallas_call x1, Pallas kernels: 15.8 us -> 7.88 us  [shards(): call(first_kernel, (rows(n + 4), rows(n + 4)), [SMEM, VMEM] + [ANY] * 7,...]
    pallas_call x1, Pallas kernels: 13.8 us -> 6.26 us  [shards(): call(input_grad_kernel, rows(n), [VMEM] * 6, [], flops, 6 * MIB)]
    ppermute x10, waiting for transfers between devices: 25.2 us -> 18.7 us  [both(): return (lax.ppermute(x, 'tm', up_tm), lax.ppermute(x, 'tm', dn_tm))]
    ppermute x10, starting transfers between devices: 43.7 us -> 48.1 us  [both(): return (lax.ppermute(x, 'tm', up_tm), lax.ppermute(x, 'tm', dn_tm))]
    ppermute x1, waiting for transfers between devices: 4.24 us -> 0.01 us  [shards(): dn = lax.ppermute(jnp.concatenate([v[:3], c[:2]]), 'space', dn_sp)]
    pallas_call x1, Pallas kernels: 5.21 us -> 2.3 us  [shards(): call(time_kernel_body, (jax.ShapeDtypeStruct((quarter, width), F32), jax....]
  transfers between devices with their start and end apart: 13 -> 13, of which waited for: 5 -> 7; matrix products, arithmetic and copies ran while one was open for 5% -> 6% of each run, Pallas kernels for 37% -> 21%
where the time goes in v2:
time: 143 us; the launch traced here: 141 us
  starting transfers between devices  73.5 us (51%)
  Pallas kernels  32 us (22%)
  waiting for transfers between devices  20.7 us (14%)
  local copies, waits for them, and re-layouts  13 us (9%)
    ppermute x10, starting transfers between devices, both(): return (lax.ppermute(x, 'tm', up_tm), lax.ppermute(x, 'tm', dn_tm))  48.1 us
    all_to_all x1, starting transfers between devices, shards(): recv = lax.all_to_all(send, 'tm', split_axis=0, concat_axis=0, tiled=True)  19.6 us
    ppermute x10, waiting for transfers between devices, both(): return (lax.ppermute(x, 'tm', up_tm), lax.ppermute(x, 'tm', dn_tm))  18.7 us
    pallas_call x1, Pallas kernels, shards(): call(video_kernel, (rows(n), jax.ShapeDtypeStruct((tm, ch // 2 + quarter,...  9.21 us
    pallas_call x1, Pallas kernels, shards(): call(first_kernel, (rows(n + 4), rows(n + 4)), [SMEM, VMEM] + [ANY] * 7,...  7.88 us
    pallas_call x1, Pallas kernels, shards(): call(grad_kernel, rows(n + 2), [SMEM] + [VMEM] * 5, [], flops, 6 * MIB)  6.35 us
    pallas_call x1, Pallas kernels, shards(): call(input_grad_kernel, rows(n), [VMEM] * 6, [], flops, 6 * MIB)  6.26 us
    unnamed x29, local copies, waits for them, and re-layouts  5.55 us
  transfers between devices with their start and end apart: 13, of which 7 were waited for; matrix products, arithmetic and copies ran while one was open for 6% of the time, Pallas kernels for 21%

profile of v2, /device:TPU:1, one launch (start us, length us, event | category | flops | bytes accessed | tf_op | source)
XLA Modules:
  0.0 140.7 jit_solution(14092144073074774793)
XLA Ops:
  0.6 5.0 %collective-permute-start.4 = (bf16[64,64,128]{2,1,0:T(8,128)(2,1)}, bf16[64,64,128]{2,1,0:T(8,128)(2,1)}, u32[]{:S(2)}, u32[]{:S(2)}) collective-permute-start(bf16[64,64,128]{2,1,0:T(8,128)(2,1)} %bitcast.37), channel_id=1, source_target_pairs={{0,4},{4,8},{8,12},{12,16},{16,20},{20,24},{24,28},{28,32},{32,36}... | collective-permute-start | bytes 3145736 | tf_op jit(solution)/shard_map/ppermute | solution.py:260
  5.6 1.3 collective-permute-start.5
  8.5 4.0 %collective-permute-start = (bf16[5,64,128]{2,1,0:T(8,128)(2,1)S(1)}, bf16[5,64,128]{2,1,0:T(8,128)(2,1)S(1)}, u32[]{:S(2)}, u32[]{:S(2)}) collective-permute-start(bf16[5,64,128]{2,1,0:T(8,128)(2,1)S(1)} %pad_maximum_fusion.2), channel_id=1, source_target_pairs={{0,1},{1,2},{2,3},{4,5},{5,6},{6,7},{8,9},{9,10},{10,11},{12,13},{... | collective-permute-start | bytes 245768 | tf_op jit(solution)/shard_map/ppermute | solution.py:262
  12.5 1.9 %collective-permute-start.1 = (bf16[5,64,128]{2,1,0:T(8,128)(2,1)S(1)}, bf16[5,64,128]{2,1,0:T(8,128)(2,1)S(1)}, u32[]{:S(2)}, u32[]{:S(2)}) collective-permute-start(bf16[5,64,128]{2,1,0:T(8,128)(2,1)S(1)} %pad_maximum_fusion.3), channel_id=1, source_target_pairs={{1,0},{2,1},{3,2},{5,4},{6,5},{7,6},{9,8},{10,9},{11,10},{13,12},{... | collective-permute-start | bytes 245768 | tf_op jit(solution)/shard_map/ppermute | solution.py:263
  20.0 4.3 %collective-permute-start.2 = (bf16[6,64,128]{2,1,0:T(8,128)(2,1)S(1)}, bf16[6,64,128]{2,1,0:T(8,128)(2,1)S(1)}, u32[]{:S(2)}, u32[]{:S(2)}) collective-permute-start(bf16[6,64,128]{2,1,0:T(8,128)(2,1)S(1)} %pad_maximum_fusion.1), channel_id=1, source_target_pairs={{0,4},{4,8},{8,12},{12,16},{16,20},{20,24},{24,28},{28,32},{32,36}... | collective-permute-start | bytes 294920 | tf_op jit(solution)/shard_map/ppermute | solution.py:260
  24.3 1.3 collective-permute-start.3
  25.8 3.0 %collective-permute-done.2.cor_p = bf16[6,64,128]{2,1,0:T(8,128)(2,1)S(1)} collective-permute-done((bf16[6,64,128]{2,1,0:T(8,128)(2,1)S(1)}, bf16[6,64,128]{2,1,0:T(8,128)(2,1)S(1)}, u32[]{:S(2)}, u32[]{:S(2)}) %collective-permute-start.2) | collective-permute-done | bytes 98336 | tf_op jit(solution)/shard_map/ppermute | solution.py:260
  28.8 4.8 %collective-permute-done.3.cor_n = bf16[6,64,128]{2,1,0:T(8,128)(2,1)S(1)} collective-permute-done((bf16[6,64,128]{2,1,0:T(8,128)(2,1)S(1)}, bf16[6,64,128]{2,1,0:T(8,128)(2,1)S(1)}, u32[]{:S(2)}, u32[]{:S(2)}) %collective-permute-start.3) | collective-permute-done | bytes 98336 | tf_op jit(solution)/shard_map/ppermute | solution.py:260
  34.3 11.2 %collective-permute-start.8 = (bf16[68,64,128]{2,1,0:T(8,128)(2,1)S(1)}, bf16[68,64,128]{2,1,0:T(8,128)(2,1)}, u32[]{:S(2)}, u32[]{:S(2)}) collective-permute-start(bf16[68,64,128]{2,1,0:T(8,128)(2,1)S(1)} %pad_maximum_fusion.own), channel_id=1, source_target_pairs={{0,4},{4,8},{8,12},{12,16},{16,20},{20,24},{24,28},{28,32},{32,36}... | collective-permute-start | bytes 3342344 | tf_op jit(solution)/shard_map/ppermute | solution.py:260
  45.4 1.3 collective-permute-start.9
  48.9 7.9 %shard_map.129 = (bf16[68,64,128]{2,1,0:T(8,128)(2,1)}, bf16[68,64,128]{2,1,0:T(8,128)(2,1)S(1)}) custom-call(s32[3]{0:T(128)S(1)} %pad_add_fusion.pos, bf16[192,576]{1,0:T(8,128)(2,1)S(1)} %reshape.98.w, bf16[64,64,128]{2,1,0:T(8,128)(2,1)S(1)} %bitcast.39, bf16[64,64,128]{2,1,0:T(8,128)(2,1)} %collective-permute-done.4.prev, ...), custom_call_target="tpu_custom_call" | custom-call | flops 1811939328 | bytes 6291456 | tf_op jit(solution)/shard_map/pallas_call | solution.py:281
  56.8 9.7 %collective-permute-start.6 = (bf16[68,64,128]{2,1,0:T(8,128)(2,1)}, bf16[68,64,128]{2,1,0:T(8,128)(2,1)}, u32[]{:S(2)}, u32[]{:S(2)}) collective-permute-start(bf16[68,64,128]{2,1,0:T(8,128)(2,1)} %get-tuple-element.21.own), channel_id=1, source_target_pairs={{0,4},{4,8},{8,12},{12,16},{16,20},{20,24},{24,28},{28,32},{32,36}... | collective-permute-start | bytes 3342344 | tf_op jit(solution)/shard_map/ppermute | solution.py:260
  66.6 1.3 collective-permute-start.7
  68.7 3.1 %collective-permute-done.9.nxt = bf16[68,64,128]{2,1,0:T(8,128)(2,1)} collective-permute-done((bf16[68,64,128]{2,1,0:T(8,128)(2,1)S(1)}, bf16[68,64,128]{2,1,0:T(8,128)(2,1)}, u32[]{:S(2)}, u32[]{:S(2)}) %collective-permute-start.9) | collective-permute-done | bytes 1114144 | tf_op jit(solution)/shard_map/ppermute | solution.py:260
  71.8 6.3 %shard_map.131.own = bf16[66,64,128]{2,1,0:T(8,128)(2,1)} custom-call(s32[3]{0:T(128)S(1)} %pad_add_fusion.pos, bf16[192,576]{1,0:T(8,128)(2,1)S(1)} %reshape.100.w, bf16[68,64,128]{2,1,0:T(8,128)(2,1)S(1)} %get-tuple-element.25.slope, bf16[68,64,128]{2,1,0:T(8,128)(2,1)S(1)} %pad_maximum_fusion.own, bf16[68,64,128]{2,1,0:T(8,128)(2,1)} %collective-permute-done.8.prev, ...), custom_call_target="tpu_custom_call" | custom-call | flops 1811939328 | bytes 6291456 | tf_op jit(solution)/shard_map/pallas_call | solution.py:285
  78.2 11.5 %collective-permute-start.10 = (bf16[66,64,128]{2,1,0:T(8,128)(2,1)}, bf16[66,64,128]{2,1,0:T(8,128)(2,1)}, u32[]{:S(2)}, u32[]{:S(2)}) collective-permute-start(bf16[66,64,128]{2,1,0:T(8,128)(2,1)} %shard_map.131.own), channel_id=1, source_target_pairs={{0,4},{4,8},{8,12},{12,16},{16,20},{20,24},{24,28},{28,32},{32,36}... | collective-permute-start | bytes 3244040 | tf_op jit(solution)/shard_map/ppermute | solution.py:260
  89.6 1.3 collective-permute-start.11
  91.4 1.3 collective-permute-done.6.prev
  92.7 5.6 %collective-permute-done.7.nxt = bf16[68,64,128]{2,1,0:T(8,128)(2,1)} collective-permute-done((bf16[68,64,128]{2,1,0:T(8,128)(2,1)}, bf16[68,64,128]{2,1,0:T(8,128)(2,1)}, u32[]{:S(2)}, u32[]{:S(2)}) %collective-permute-start.7) | collective-permute-done | bytes 1114144 | tf_op jit(solution)/shard_map/ppermute | solution.py:260
  99.6 9.2 %shard_map.130 = (bf16[64,64,128]{2,1,0:T(8,128)(2,1)}, bf16[32,48,128]{2,1,0:T(8,128)(2,1)}) custom-call(s32[3]{0:T(128)S(1)} %pad_add_fusion.pos, s32[8]{0:T(128)S(1)} %copy-done.4, bf16[192,576]{1,0:T(8,128)(2,1)S(1)} %reshape.99.w, bf16[192,192]{1,0:T(8,128)(2,1)S(1)} %reshape.102.wp, f32[64,128]{1,0:T(8,128)S(1)} %broadcast_in_dim.38.head, ...), custom_call_target="tpu_custom_call" | custom-call | flops 2415919104 | bytes 6291456 | tf_op jit(solution)/shard_map/pallas_call | solution.py:295
  108.8 19.6 %all-to-all-start = ((bf16[32,48,128]{2,1,0:T(8,128)(2,1)}), bf16[32,48,128]{2,1,0:T(8,128)(2,1)S(1)}, u32[]{:S(2)}, u32[]{:S(2)}) async-start(bf16[32,48,128]{2,1,0:T(8,128)(2,1)} %get-tuple-element.27), calls=%async_computation | async-start | bytes 786432 | tf_op jit(solution)/shard_map/all_to_all | solution.py:307
  130.0 6.3 %shard_map.132 = bf16[64,64,128]{2,1,0:T(8,128)(2,1)} custom-call(bf16[192,576]{1,0:T(8,128)(2,1)S(1)} %reshape.101.w, bf16[64,64,128]{2,1,0:T(8,128)(2,1)S(1)} %bitcast.35, bf16[64,64,128]{2,1,0:T(8,128)(2,1)S(1)} %bitcast.41, bf16[66,64,128]{2,1,0:T(8,128)(2,1)} %shard_map.131.own, bf16[66,64,128]{2,1,0:T(8,128)(2,1)} %collective-permute-done.10.prev, ...), custom_call_target="tpu_custom_call" | custom-call | flops 1811939328 | bytes 6291456 | tf_op jit(solution)/shard_map/pallas_call | solution.py:308
  136.2 2.0 %all-to-all-done.recv = bf16[32,48,128]{2,1,0:T(8,128)(2,1)S(1)} async-done(((bf16[32,48,128]{2,1,0:T(8,128)(2,1)}), bf16[32,48,128]{2,1,0:T(8,128)(2,1)S(1)}, u32[]{:S(2)}, u32[]{:S(2)}) %all-to-all-start) | async-done | bytes 393248 | tf_op jit(solution)/shard_map/all_to_all | solution.py:307
  138.4 2.3 %shard_map.133 = (f32[16,128]{1,0:T(8,128)}, f32[1,64]{1,0:T(1,128)}) custom-call(s32[3]{0:T(128)S(1)} %pad_add_fusion.pos, s32[8]{0:T(128)S(1)} %copy-done.4, bf16[128,96]{1,0:T(8,128)(2,1)S(1)} %copy.28.wt, bf16[64,64]{1,0:T(8,128)(2,1)S(1)} %bitcast.36, f32[64,128]{1,0:T(8,128)S(1)} %broadcast_in_dim.43.head, bf16[32,48,128]{2,1,0:T(8,128)(2,1)S(1)} %all-to-all-done.recv), custom_call_target="tpu_custom_call" | custom-call | flops 90596968 | bytes 1048576 | tf_op jit(solution)/shard_map/pallas_call | solution.py:312
  (67 shorter events, 14.3 us)
Async XLA Ops:
  0.6 46.2 %collective-permute-start.4 = (bf16[64,64,128]{2,1,0:T(8,128)(2,1)}, bf16[64,64,128]{2,1,0:T(8,128)(2,1)}, u32[]{:S(2)}, u32[]{:S(2)}) collective-permute-start(bf16[64,64,128]{2,1,0:T(8,128)(2,1)} %bitcast.37), channel_id=1, source_target_pairs={{0,4},{4,8},{8,12},{12,16},{16,20},{20,24},{24,28},{28,32},{32,36}... | collective-permute-start | bytes 3145736 | tf_op jit(solution)/shard_map/ppermute | solution.py:260
  5.6 41.2 %collective-permute-start.5 = (bf16[64,64,128]{2,1,0:T(8,128)(2,1)}, bf16[64,64,128]{2,1,0:T(8,128)(2,1)}, u32[]{:S(2)}, u32[]{:S(2)}) collective-permute-start(bf16[64,64,128]{2,1,0:T(8,128)(2,1)} %bitcast.38), channel_id=1, source_target_pairs={{4,0},{8,4},{12,8},{16,12},{20,16},{24,20},{28,24},{32,28},{36,32}... | collective-permute-start | bytes 3145736 | tf_op jit(solution)/shard_map/ppermute | solution.py:260
  8.5 11.4 %collective-permute-start = (bf16[5,64,128]{2,1,0:T(8,128)(2,1)S(1)}, bf16[5,64,128]{2,1,0:T(8,128)(2,1)S(1)}, u32[]{:S(2)}, u32[]{:S(2)}) collective-permute-start(bf16[5,64,128]{2,1,0:T(8,128)(2,1)S(1)} %pad_maximum_fusion.2), channel_id=1, source_target_pairs={{0,1},{1,2},{2,3},{4,5},{5,6},{6,7},{8,9},{9,10},{10,11},{12,13},{... | collective-permute-start | bytes 245768 | tf_op jit(solution)/shard_map/ppermute | solution.py:262
  12.5 7.4 %collective-permute-start.1 = (bf16[5,64,128]{2,1,0:T(8,128)(2,1)S(1)}, bf16[5,64,128]{2,1,0:T(8,128)(2,1)S(1)}, u32[]{:S(2)}, u32[]{:S(2)}) collective-permute-start(bf16[5,64,128]{2,1,0:T(8,128)(2,1)S(1)} %pad_maximum_fusion.3), channel_id=1, source_target_pairs={{1,0},{2,1},{3,2},{5,4},{6,5},{7,6},{9,8},{10,9},{11,10},{13,12},{... | collective-permute-start | bytes 245768 | tf_op jit(solution)/shard_map/ppermute | solution.py:263
  17.3 1.3 copy-start.8
  18.6 7.0 %copy-start = (bf16[1,64,64,128]{3,2,1,0:T(8,128)(2,1)S(1)}, bf16[1,64,64,128]{3,2,1,0:T(8,128)(2,1)}, u32[]{:S(2)}) copy-start(bf16[1,64,64,128]{3,2,1,0:T(8,128)(2,1)} %param.11) | copy-start | bytes 3145732
  20.0 8.8 %collective-permute-start.2 = (bf16[6,64,128]{2,1,0:T(8,128)(2,1)S(1)}, bf16[6,64,128]{2,1,0:T(8,128)(2,1)S(1)}, u32[]{:S(2)}, u32[]{:S(2)}) collective-permute-start(bf16[6,64,128]{2,1,0:T(8,128)(2,1)S(1)} %pad_maximum_fusion.1), channel_id=1, source_target_pairs={{0,4},{4,8},{8,12},{12,16},{16,20},{20,24},{24,28},{28,32},{32,36}... | collective-permute-start | bytes 294920 | tf_op jit(solution)/shard_map/ppermute | solution.py:260
  24.3 9.4 %collective-permute-start.3 = (bf16[6,64,128]{2,1,0:T(8,128)(2,1)S(1)}, bf16[6,64,128]{2,1,0:T(8,128)(2,1)S(1)}, u32[]{:S(2)}, u32[]{:S(2)}) collective-permute-start(bf16[6,64,128]{2,1,0:T(8,128)(2,1)S(1)} %pad_maximum_fusion.1), channel_id=1, source_target_pairs={{4,0},{8,4},{12,8},{16,12},{20,16},{24,20},{28,24},{32,28},{36,32}... | collective-permute-start | bytes 294920 | tf_op jit(solution)/shard_map/ppermute | solution.py:260
  34.3 34.4 %collective-permute-start.8 = (bf16[68,64,128]{2,1,0:T(8,128)(2,1)S(1)}, bf16[68,64,128]{2,1,0:T(8,128)(2,1)}, u32[]{:S(2)}, u32[]{:S(2)}) collective-permute-start(bf16[68,64,128]{2,1,0:T(8,128)(2,1)S(1)} %pad_maximum_fusion.own), channel_id=1, source_target_pairs={{0,4},{4,8},{8,12},{12,16},{16,20},{20,24},{24,28},{28,32},{32,36}... | collective-permute-start | bytes 3342344 | tf_op jit(solution)/shard_map/ppermute | solution.py:260
  45.4 26.4 %collective-permute-start.9 = (bf16[68,64,128]{2,1,0:T(8,128)(2,1)S(1)}, bf16[68,64,128]{2,1,0:T(8,128)(2,1)}, u32[]{:S(2)}, u32[]{:S(2)}) collective-permute-start(bf16[68,64,128]{2,1,0:T(8,128)(2,1)S(1)} %pad_maximum_fusion.own), channel_id=1, source_target_pairs={{4,0},{8,4},{12,8},{16,12},{20,16},{24,20},{28,24},{32,28},{36,32}... | collective-permute-start | bytes 3342344 | tf_op jit(solution)/shard_map/ppermute | solution.py:260
  46.8 1.2 copy-start.1
  56.8 35.8 %collective-permute-start.6 = (bf16[68,64,128]{2,1,0:T(8,128)(2,1)}, bf16[68,64,128]{2,1,0:T(8,128)(2,1)}, u32[]{:S(2)}, u32[]{:S(2)}) collective-permute-start(bf16[68,64,128]{2,1,0:T(8,128)(2,1)} %get-tuple-element.21.own), channel_id=1, source_target_pairs={{0,4},{4,8},{8,12},{12,16},{16,20},{20,24},{24,28},{28,32},{32,36}... | collective-permute-start | bytes 3342344 | tf_op jit(solution)/shard_map/ppermute | solution.py:260
  66.6 31.7 %collective-permute-start.7 = (bf16[68,64,128]{2,1,0:T(8,128)(2,1)}, bf16[68,64,128]{2,1,0:T(8,128)(2,1)}, u32[]{:S(2)}, u32[]{:S(2)}) collective-permute-start(bf16[68,64,128]{2,1,0:T(8,128)(2,1)} %get-tuple-element.21.own), channel_id=1, source_target_pairs={{4,0},{8,4},{12,8},{16,12},{20,16},{24,20},{28,24},{32,28},{36,32}... | collective-permute-start | bytes 3342344 | tf_op jit(solution)/shard_map/ppermute | solution.py:260
  71.8 19.1 %copy-start.9 = (bf16[3,3,64,64]{3,2,1,0:T(8,128)(2,1)S(1)}, bf16[3,3,64,64]{3,2,1,0:T(8,128)(2,1)}, u32[]{:S(2)}) copy-start(bf16[3,3,64,64]{3,2,1,0:T(8,128)(2,1)} %param.14) | copy-start | bytes 221188
  71.8 26.4 %copy-start.12 = (bf16[64]{0:T(256)(128)(2,1)S(1)}, bf16[64]{0:T(256)(128)(2,1)}, u32[]{:S(2)}) copy-start(bf16[64]{0:T(256)(128)(2,1)} %param.15) | copy-start | bytes 388
  71.8 26.5 %copy-start.4 = (s32[8]{0:T(128)S(1)}, s32[8]{0:T(128)}, u32[]{:S(2)}) copy-start(s32[8]{0:T(128)} %listed.3) | copy-start | bytes 100
  78.2 50.6 %collective-permute-start.10 = (bf16[66,64,128]{2,1,0:T(8,128)(2,1)}, bf16[66,64,128]{2,1,0:T(8,128)(2,1)}, u32[]{:S(2)}, u32[]{:S(2)}) collective-permute-start(bf16[66,64,128]{2,1,0:T(8,128)(2,1)} %shard_map.131.own), channel_id=1, source_target_pairs={{0,4},{4,8},{8,12},{12,16},{16,20},{20,24},{24,28},{28,32},{32,36}... | collective-permute-start | bytes 3244040 | tf_op jit(solution)/shard_map/ppermute | solution.py:260
  89.6 39.1 %collective-permute-start.11 = (bf16[66,64,128]{2,1,0:T(8,128)(2,1)}, bf16[66,64,128]{2,1,0:T(8,128)(2,1)}, u32[]{:S(2)}, u32[]{:S(2)}) collective-permute-start(bf16[66,64,128]{2,1,0:T(8,128)(2,1)} %shard_map.131.own), channel_id=1, source_target_pairs={{4,0},{8,4},{12,8},{16,12},{20,16},{24,20},{28,24},{32,28},{36,32}... | collective-permute-start | bytes 3244040 | tf_op jit(solution)/shard_map/ppermute | solution.py:260
  98.3 1.2 copy-start.2
  99.6 28.8 %copy-start.10 = (bf16[3,64,64]{2,1,0:T(8,128)(2,1)S(1)}, bf16[3,64,64]{2,1,0:T(8,128)(2,1)}, u32[]{:S(2)}) copy-start(bf16[3,64,64]{2,1,0:T(8,128)(2,1)} %param.16) | copy-start | bytes 73732
  99.6 29.1 %copy-start.11 = (bf16[64,64]{1,0:T(8,128)(2,1)S(1)}, bf16[64,64]{1,0:T(8,128)(2,1)}, u32[]{:S(2)}) copy-start(bf16[64,64]{1,0:T(8,128)(2,1)} %param.17) | copy-start | bytes 24580
  108.8 29.5 %all-to-all-start = ((bf16[32,48,128]{2,1,0:T(8,128)(2,1)}), bf16[32,48,128]{2,1,0:T(8,128)(2,1)S(1)}, u32[]{:S(2)}, u32[]{:S(2)}) async-start(bf16[32,48,128]{2,1,0:T(8,128)(2,1)} %get-tuple-element.27), calls=%async_computation | async-start | bytes 786432 | tf_op jit(solution)/shard_map/all_to_all | solution.py:307
  128.6 9.7 %copy-start.13 = (bf16[64]{0:T(256)(128)(2,1)S(1)}, bf16[64]{0:T(256)(128)(2,1)}, u32[]{:S(2)}) copy-start(bf16[64]{0:T(256)(128)(2,1)} %param.18) | copy-start | bytes 388
  128.8 1.2 copy-start.3
  (3 other events, 2.5 us)

commit v3 on v2

--- a/solution.py
+++ b/solution.py
@@ -57,35 +57,14 @@
     lax.fori_loop(1, rows // 2, step, carry, unroll=unroll)
 
 
-def copies(pairs, sems):
-    todo = [pltpu.make_async_copy(s, d, sems.at[i]) for i, (s, d) in enumerate(pairs)]
-    for t in todo:
-        t.start()
-    for t in todo:
-        t.wait()
-
-
 def row_mask(first, r, limit):
     g = first + r
     return jnp.where((g >= 0) & (g < limit), 1.0, 0.0).astype(F32)
 
 
-def first_kernel(pos, w, own, prev, nxt, up, dn, cor_p, cor_n, inner, slope, vol, sems):
-    n = own.shape[0]
-    copies(
-        [
-            (prev, vol.at[0, pl.ds(3, n)]),
-            (own, vol.at[1, pl.ds(3, n)]),
-            (nxt, vol.at[2, pl.ds(3, n)]),
-            (up.at[pl.ds(0, 3)], vol.at[1, pl.ds(0, 3)]),
-            (dn.at[pl.ds(0, 3)], vol.at[1, pl.ds(n + 3, 3)]),
-            (cor_p.at[pl.ds(0, 3)], vol.at[0, pl.ds(0, 3)]),
-            (cor_p.at[pl.ds(3, 3)], vol.at[0, pl.ds(n + 3, 3)]),
-            (cor_n.at[pl.ds(0, 3)], vol.at[2, pl.ds(0, 3)]),
-            (cor_n.at[pl.ds(3, 3)], vol.at[2, pl.ds(n + 3, 3)]),
-        ],
-        sems,
-    )
+def first_kernel(pos, w, own, prev, nxt, inner, slope):
+    n = own.shape[0] - 6
+    vol = (prev, own, nxt)
 
     def emit(r, pre):
         s = logistic(pre)
@@ -93,7 +72,7 @@
         inner[r] = (act * row_mask(pos[0] - 2, r, pos[1])).astype(BF16)
         slope[r] = (s + act * (1.0 - s)).astype(BF16)
 
-    conv_rows(lambda a, i: vol[a, i], w, n + 6, emit, silu_in=True)
+    conv_rows(lambda a, i: vol[a][i], w, n + 6, emit, silu_in=True)
 
 
 def grad_kernel(pos, w, slope, own, prev, nxt, grad):
@@ -107,22 +86,12 @@
     conv_rows(lambda a, i: vol[a][i], w, n + 4, emit)
 
 
-def video_kernel(
-    pos, listed, w, wp, head, pool, base, up, dn, own, prev, nxt, video, send, rim, sums, sems
-):
-    n = base.shape[0]
-    copies(
-        [
-            (base, rim.at[pl.ds(1, n)]),
-            (up.at[pl.ds(2, 1)], rim.at[pl.ds(0, 1)]),
-            (dn.at[pl.ds(0, 1)], rim.at[pl.ds(n + 1, 1)]),
-        ],
-        sems,
-    )
+def video_kernel(pos, listed, w, wp, head, pool, base, own, prev, nxt, video, send, rim, sums):
+    n = base.shape[0] - 6
     vol = (prev, own, nxt)
 
     def emit(r, value):
-        out = (rim[r].astype(F32) + value) * row_mask(pos[0] - 1, r, pos[1])
+        out = (base[r + 2].astype(F32) + value) * row_mask(pos[0] - 1, r, pos[1])
         rim[r] = out.astype(BF16)
 
     conv_rows(lambda a, i: vol[a][i], w, n + 4, emit)
@@ -210,7 +179,6 @@
 
 VMEM = pl.BlockSpec(memory_space=pltpu.VMEM)
 SMEM = pl.BlockSpec(memory_space=pltpu.SMEM)
-ANY = pl.BlockSpec(memory_space=pl.ANY)
 
 
 def call(body, outs, in_specs, scratch, flops, nbytes, limit=40):
@@ -261,54 +229,51 @@
 
     up = lax.ppermute(jnp.concatenate([v[n - 3 :], c[n - 2 :]]), "space", up_sp)
     dn = lax.ppermute(jnp.concatenate([v[:3], c[:2]]), "space", dn_sp)
-    v_p, v_n = both(v)
-    cor_p, cor_n = both(jnp.concatenate([up[:3], dn[:3]]))
+    v_own = jnp.concatenate([up[:3], v, dn[:3]])
+    c_own = jnp.concatenate([up[3:], c, dn[3:]])
+    v_p, v_n = both(v_own)
+    c_p, c_n = both(c_own)
     wa, wb = stacked(kernel_a), stacked(kernel_b)
     wbt, wat = stacked(flipped(kernel_b)), stacked(flipped(kernel_a))
-    c_own = jnp.concatenate([up[3:], c, dn[3:]])
-    c_own, cor_p, cor_n, wa, wb, wbt, wat = lax.optimization_barrier(
-        (c_own, cor_p, cor_n, wa, wb, wbt, wat)
+    wp = stacked(plane_kernel[None])
+    spread = lambda h: jnp.broadcast_to(h.astype(F32)[:, None], (ch, width))
+    idx = jnp.arange(2 * width)[:, None] % width // 2
+    pool = jnp.where(idx == jnp.arange(width)[None, :] % (width // 2), 0.25, 0.0).astype(BF16)
+    wt = jnp.transpose(time_kernel.reshape(3, 2, ch // 2, ch), (1, 3, 0, 2)).reshape(2 * ch, 3 * ch // 2)
+    mixer, plane_row, time_row = time_mixer.T, spread(plane_head), spread(time_head)
+    wa, wb, wbt, wat, wp, wt, mixer, plane_row, time_row, pool = lax.optimization_barrier(
+        (wa, wb, wbt, wat, wp, wt, mixer, plane_row, time_row, pool)
     )
-    c_p, c_n = both(c_own)
 
     def rows(r, dtype=BF16):
         return jax.ShapeDtypeStruct((r, ch, width), dtype)
 
-    def volume(r):
-        return [pltpu.VMEM((3, r, ch, width), BF16), pltpu.SemaphoreType.DMA((9,))]
-
     flops = 2 * 27 * ch * ch * width * n
     inner, slope = call(
-        first_kernel, (rows(n + 4), rows(n + 4)), [SMEM, VMEM] + [ANY] * 7, volume(n + 6), flops, 6 * MIB
-    )(pos, wa, v, v_p, v_n, up, dn, cor_p, cor_n)
+        first_kernel, (rows(n + 4), rows(n + 4)), [SMEM] + [VMEM] * 4, [], flops, 6 * MIB
+    )(pos, wa, v_own, v_p, v_n)
     in_p, in_n = both(inner)
     grad = call(
         grad_kernel, rows(n + 2), [SMEM] + [VMEM] * 5, [], flops, 6 * MIB
     )(pos, wbt, slope, c_own, c_p, c_n)
     gr_p, gr_n = both(grad)
 
-    wp = stacked(plane_kernel[None])
-    spread = lambda h: jnp.broadcast_to(h.astype(F32)[:, None], (ch, width))
-    idx = jnp.arange(2 * width)[:, None] % width // 2
-    pool = jnp.where(idx == jnp.arange(width)[None, :] % (width // 2), 0.25, 0.0).astype(BF16)
     quarter = n // (tm // LISTED)
     video, send = call(
         video_kernel,
         (rows(n), jax.ShapeDtypeStruct((tm, ch // 2 + quarter, width), BF16)),
-        [SMEM, SMEM, VMEM, VMEM, VMEM, VMEM, ANY, ANY, ANY, VMEM, VMEM, VMEM],
+        [SMEM, SMEM] + [VMEM] * 8,
         [
             pltpu.VMEM((n + 2, ch, width), BF16),
             pltpu.VMEM((n, width), F32),
-            pltpu.SemaphoreType.DMA((3,)),
         ],
         flops * 4 // 3,
         6 * MIB,
-    )(pos, listed, wb, wp, spread(plane_head), pool, v, up, dn, inner, in_p, in_n)
+    )(pos, listed, wb, wp, plane_row, pool, v_own, inner, in_p, in_n)
     recv = lax.all_to_all(send, "tm", split_axis=0, concat_axis=0, tiled=True)
     input_grad = call(input_grad_kernel, rows(n), [VMEM] * 6, [], flops, 6 * MIB)(
         wat, c, v, grad, gr_p, gr_n
     )
-    wt = jnp.transpose(time_kernel.reshape(3, 2, ch // 2, ch), (1, 3, 0, 2)).reshape(2 * ch, 3 * ch // 2)
     plane_scores, time_scores = call(
         time_kernel_body,
         (jax.ShapeDtypeStruct((quarter, width), F32), jax.ShapeDtypeStruct((1, width // 2), F32)),
@@ -316,7 +281,7 @@
         [pltpu.VMEM((ch, width), F32)],
         flops // 20,
         MIB,
-    )(pos, listed, wt, time_mixer.T, spread(time_head), recv)
+    )(pos, listed, wt, mixer, time_row, recv)
     return (video[None], input_grad[None], plane_scores[None, None], time_scores[None])
 
 

time: 143 us -> 131 us (0.916)
  starting transfers between devices: 73.5 us -> 40 us
  waiting for transfers between devices: 20.7 us -> 42 us
  Pallas kernels: 32 us -> 29.4 us
  other arithmetic: 0.37 us -> 2.79 us
    ppermute x10 -> x8, starting transfers between devices: 48.1 us -> 20 us  [both(): return (lax.ppermute(x, 'tm', up_tm), lax.ppermute(x, 'tm', dn_tm))]
    ppermute x10 -> x8, waiting for transfers between devices: 18.7 us -> 34.4 us  [both(): return (lax.ppermute(x, 'tm', up_tm), lax.ppermute(x, 'tm', dn_tm))]
    all_to_all x1, starting transfers between devices: 19.6 us -> 13.5 us  [shards(): recv = lax.all_to_all(send, 'tm', split_axis=0, concat_axis=0, tiled=True)]
    unnamed x29 -> x19, local copies, waits for them, and re-layouts: 5.55 us -> 0.53 us
    ppermute x1, waiting for transfers between devices: 0.01 us -> 3.81 us  [shards(): dn = lax.ppermute(jnp.concatenate([v[:3], c[:2]]), 'space', dn_sp)]
    transpose x3, local copies, waits for them, and re-layouts: 1.87 us -> 5.18 us  [stacked(): return jnp.transpose(kernel, (1, 4, 0, 2, 3)).reshape(b * o, a * e * c)]
    reshape x5, local copies, waits for them, and re-layouts: 1.73 us -> 3.91 us  [stacked(): return jnp.transpose(kernel, (1, 4, 0, 2, 3)).reshape(b * o, a * e * c)]
    all_to_all x1, waiting for transfers between devices: 2.04 us -> 3.79 us  [shards(): recv = lax.all_to_all(send, 'tm', split_axis=0, concat_axis=0, tiled=True)]
  transfers between devices with their start and end apart: 13 -> 11, of which waited for: 7 -> 8; matrix products, arithmetic and copies ran while one was open for 6% -> 10% of each run, Pallas kernels for 21% -> 21%
where the time goes in v3:
time: 131 us; the launch traced here: 129 us
  waiting for transfers between devices  42 us (32%)
  starting transfers between devices  40 us (31%)
  Pallas kernels  29.4 us (22%)
  local copies, waits for them, and re-layouts  13.9 us (11%)
  other arithmetic  2.79 us (2%)
    ppermute x8, waiting for transfers between devices, both(): return (lax.ppermute(x, 'tm', up_tm), lax.ppermute(x, 'tm', dn_tm))  34.4 us
    ppermute x8, starting transfers between devices, both(): return (lax.ppermute(x, 'tm', up_tm), lax.ppermute(x, 'tm', dn_tm))  20 us
    all_to_all x1, starting transfers between devices, shards(): recv = lax.all_to_all(send, 'tm', split_axis=0, concat_axis=0, tiled=True)  13.5 us
    pallas_call x1, Pallas kernels, shards(): call(video_kernel, (rows(n), jax.ShapeDtypeStruct((tm, ch // 2 + quarter,...  7.73 us
    pallas_call x1, Pallas kernels, shards(): call(grad_kernel, rows(n + 2), [SMEM] + [VMEM] * 5, [], flops, 6 * MIB)  6.71 us
    pallas_call x1, Pallas kernels, shards(): call(first_kernel, (rows(n + 4), rows(n + 4)), [SMEM] + [VMEM] * 4, [], f...  6.42 us
    pallas_call x1, Pallas kernels, shards(): call(input_grad_kernel, rows(n), [VMEM] * 6, [], flops, 6 * MIB)  6.26 us
    transpose x3, local copies, waits for them, and re-layouts, stacked(): return jnp.transpose(kernel, (1, 4, 0, 2, 3)).reshape(b * o, a * e * c)  5.18 us
  transfers between devices with their start and end apart: 11, of which 8 were waited for; matrix products, arithmetic and copies ran while one was open for 10% of the time, Pallas kernels for 21%

profile of v3, /device:TPU:1, one launch (start us, length us, event | category | flops | bytes accessed | tf_op | source)
XLA Modules:
  0.0 129.1 jit_solution(10302409937589648384)
XLA Ops:
  2.3 4.5 %collective-permute-start = (bf16[5,64,128]{2,1,0:T(8,128)(2,1)S(1)}, bf16[5,64,128]{2,1,0:T(8,128)(2,1)S(1)}, u32[]{:S(2)}, u32[]{:S(2)}) collective-permute-start(bf16[5,64,128]{2,1,0:T(8,128)(2,1)S(1)} %pad_maximum_fusion.2), channel_id=1, source_target_pairs={{0,1},{1,2},{2,3},{4,5},{5,6},{6,7},{8,9},{9,10},{10,11},{12,13},{... | collective-permute-start | bytes 245768 | tf_op jit(solution)/shard_map/ppermute | solution.py:230
  6.8 1.9 %collective-permute-start.1 = (bf16[5,64,128]{2,1,0:T(8,128)(2,1)S(1)}, bf16[5,64,128]{2,1,0:T(8,128)(2,1)S(1)}, u32[]{:S(2)}, u32[]{:S(2)}) collective-permute-start(bf16[5,64,128]{2,1,0:T(8,128)(2,1)S(1)} %pad_maximum_fusion.3), channel_id=1, source_target_pairs={{1,0},{2,1},{3,2},{5,4},{6,5},{7,6},{9,8},{10,9},{11,10},{13,12},{... | collective-permute-start | bytes 245768 | tf_op jit(solution)/shard_map/ppermute | solution.py:231
  8.7 3.8 %collective-permute-done.1 = bf16[5,64,128]{2,1,0:T(8,128)(2,1)S(1)} collective-permute-done((bf16[5,64,128]{2,1,0:T(8,128)(2,1)S(1)}, bf16[5,64,128]{2,1,0:T(8,128)(2,1)S(1)}, u32[]{:S(2)}, u32[]{:S(2)}) %collective-permute-start.1) | collective-permute-done | bytes 81952 | tf_op jit(solution)/shard_map/ppermute | solution.py:231
  14.0 4.2 %collective-permute-start.2 = (bf16[70,64,128]{2,1,0:T(8,128)(2,1)S(1)}, bf16[70,64,128]{2,1,0:T(8,128)(2,1)}, u32[]{:S(2)}, u32[]{:S(2)}) collective-permute-start(bf16[70,64,128]{2,1,0:T(8,128)(2,1)S(1)} %pad_maximum_fusion.own.base), channel_id=1, source_target_pairs={{0,4},{4,8},{8,12},{12,16},{16,20},{20,24},{24,28},{28,32},{32,36}... | collective-permute-start | bytes 3440648 | tf_op jit(solution)/shard_map/ppermute | solution.py:228
  21.9 5.0 %collective-permute-start.6 = (bf16[68,64,128]{2,1,0:T(8,128)(2,1)}, bf16[68,64,128]{2,1,0:T(8,128)(2,1)}, u32[]{:S(2)}, u32[]{:S(2)}) collective-permute-start(bf16[68,64,128]{2,1,0:T(8,128)(2,1)} %pad_maximum_fusion.1.own), channel_id=1, source_target_pairs={{0,4},{4,8},{8,12},{12,16},{16,20},{20,24},{24,28},{28,32},{32,36}... | collective-permute-start | bytes 3342344 | tf_op jit(solution)/shard_map/ppermute | solution.py:228
  29.1 2.1 %copy.21 = bf16[3,64,3,3,64]{4,3,2,1,0:T(4,128)(2,1)} copy(bf16[3,64,3,3,64]{1,4,3,0,2:T(8,128)(2,1)} %bitcast.39) | data formatting | bytes 442368 | tf_op jit(solution)/shard_map/transpose | solution.py:198
  31.1 1.5 %reshape.98.w = bf16[192,576]{1,0:T(8,128)(2,1)S(1)} reshape(bf16[3,64,3,3,64]{4,3,2,1,0:T(4,128)(2,1)} %copy.21) | data formatting | bytes 442368 | tf_op jit(solution)/shard_map/reshape | solution.py:198
  32.6 2.1 %copy.22 = bf16[3,64,3,3,64]{4,3,2,1,0:T(4,128)(2,1)} copy(bf16[3,64,3,3,64]{1,4,3,0,2:T(8,128)(2,1)} %bitcast.40) | data formatting | bytes 442368 | tf_op jit(solution)/shard_map/transpose | solution.py:198
  34.7 1.5 %reshape.99.w = bf16[192,576]{1,0:T(8,128)(2,1)S(1)} reshape(bf16[3,64,3,3,64]{4,3,2,1,0:T(4,128)(2,1)} %copy.22) | data formatting | bytes 442368 | tf_op jit(solution)/shard_map/reshape | solution.py:198
  39.5 2.9 %collective-permute-done.2.prev = bf16[70,64,128]{2,1,0:T(8,128)(2,1)} collective-permute-done((bf16[70,64,128]{2,1,0:T(8,128)(2,1)S(1)}, bf16[70,64,128]{2,1,0:T(8,128)(2,1)}, u32[]{:S(2)}, u32[]{:S(2)}) %collective-permute-start.2) | collective-permute-done | bytes 1146912 | tf_op jit(solution)/shard_map/ppermute | solution.py:228
  42.3 5.2 %collective-permute-done.3.nxt = bf16[70,64,128]{2,1,0:T(8,128)(2,1)} collective-permute-done((bf16[70,64,128]{2,1,0:T(8,128)(2,1)S(1)}, bf16[70,64,128]{2,1,0:T(8,128)(2,1)}, u32[]{:S(2)}, u32[]{:S(2)}) %collective-permute-start.3) | collective-permute-done | bytes 1146912 | tf_op jit(solution)/shard_map/ppermute | solution.py:228
  47.5 6.4 %shard_map.129 = (bf16[68,64,128]{2,1,0:T(8,128)(2,1)S(1)}, bf16[68,64,128]{2,1,0:T(8,128)(2,1)S(1)}) custom-call(s32[3]{0:T(128)S(1)} %pad_add_fusion.pos, bf16[192,576]{1,0:T(8,128)(2,1)S(1)} %reshape.98.w, bf16[70,64,128]{2,1,0:T(8,128)(2,1)S(1)} %pad_maximum_fusion.own.base, bf16[70,64,128]{2,1,0:T(8,128)(2,1)} %collective-permute-done.2.prev, ...), custom_call_target="tpu_custom_call" | custom-call | flops 1811939328 | bytes 6291456 | tf_op jit(solution)/shard_map/pallas_call | solution.py:252
  54.0 2.3 %collective-permute-start.4 = (bf16[68,64,128]{2,1,0:T(8,128)(2,1)S(1)}, bf16[68,64,128]{2,1,0:T(8,128)(2,1)S(1)}, u32[]{:S(2)}, u32[]{:S(2)}) collective-permute-start(bf16[68,64,128]{2,1,0:T(8,128)(2,1)S(1)} %get-tuple-element.25.own), channel_id=1, source_target_pairs={{0,4},{4,8},{8,12},{12,16},{16,20},{20,24},{24,28},{28,32},{32,36}... | collective-permute-start | bytes 3342344 | tf_op jit(solution)/shard_map/ppermute | solution.py:228
  57.6 8.8 %collective-permute-done.6.prev = bf16[68,64,128]{2,1,0:T(8,128)(2,1)} collective-permute-done((bf16[68,64,128]{2,1,0:T(8,128)(2,1)}, bf16[68,64,128]{2,1,0:T(8,128)(2,1)}, u32[]{:S(2)}, u32[]{:S(2)}) %collective-permute-start.6) | collective-permute-done | bytes 1114144 | tf_op jit(solution)/shard_map/ppermute | solution.py:228
  66.3 5.0 %collective-permute-done.7.nxt = bf16[68,64,128]{2,1,0:T(8,128)(2,1)} collective-permute-done((bf16[68,64,128]{2,1,0:T(8,128)(2,1)}, bf16[68,64,128]{2,1,0:T(8,128)(2,1)}, u32[]{:S(2)}, u32[]{:S(2)}) %collective-permute-start.7) | collective-permute-done | bytes 1114144 | tf_op jit(solution)/shard_map/ppermute | solution.py:228
  71.3 6.7 %shard_map.131.own = bf16[66,64,128]{2,1,0:T(8,128)(2,1)} custom-call(s32[3]{0:T(128)S(1)} %pad_add_fusion.pos, bf16[192,576]{1,0:T(8,128)(2,1)S(1)} %reshape.100.w, bf16[68,64,128]{2,1,0:T(8,128)(2,1)S(1)} %get-tuple-element.29.slope, bf16[68,64,128]{2,1,0:T(8,128)(2,1)} %pad_maximum_fusion.1.own, bf16[68,64,128]{2,1,0:T(8,128)(2,1)} %collective-permute-done.6.prev, ...), custom_call_target="tpu_custom_call" | custom-call | flops 1811939328 | bytes 6291456 | tf_op jit(solution)/shard_map/pallas_call | solution.py:256
  78.0 3.3 %collective-permute-start.8 = (bf16[66,64,128]{2,1,0:T(8,128)(2,1)}, bf16[66,64,128]{2,1,0:T(8,128)(2,1)}, u32[]{:S(2)}, u32[]{:S(2)}) collective-permute-start(bf16[66,64,128]{2,1,0:T(8,128)(2,1)} %shard_map.131.own), channel_id=1, source_target_pairs={{0,4},{4,8},{8,12},{12,16},{16,20},{20,24},{24,28},{28,32},{32,36}... | collective-permute-start | bytes 3244040 | tf_op jit(solution)/shard_map/ppermute | solution.py:228
  82.7 7.4 %collective-permute-done.4.prev = bf16[68,64,128]{2,1,0:T(8,128)(2,1)S(1)} collective-permute-done((bf16[68,64,128]{2,1,0:T(8,128)(2,1)S(1)}, bf16[68,64,128]{2,1,0:T(8,128)(2,1)S(1)}, u32[]{:S(2)}, u32[]{:S(2)}) %collective-permute-start.4) | collective-permute-done | bytes 1114144 | tf_op jit(solution)/shard_map/ppermute | solution.py:228
  90.1 5.2 %collective-permute-done.5.nxt = bf16[68,64,128]{2,1,0:T(8,128)(2,1)S(1)} collective-permute-done((bf16[68,64,128]{2,1,0:T(8,128)(2,1)S(1)}, bf16[68,64,128]{2,1,0:T(8,128)(2,1)S(1)}, u32[]{:S(2)}, u32[]{:S(2)}) %collective-permute-start.5) | collective-permute-done | bytes 1114144 | tf_op jit(solution)/shard_map/ppermute | solution.py:228
  95.3 7.7 %shard_map.130 = (bf16[64,64,128]{2,1,0:T(8,128)(2,1)}, bf16[32,48,128]{2,1,0:T(8,128)(2,1)}) custom-call(s32[3]{0:T(128)S(1)} %pad_add_fusion.pos, s32[8]{0:T(128)S(1)} %copy-done.4, bf16[192,576]{1,0:T(8,128)(2,1)S(1)} %reshape.99.w, bf16[192,192]{1,0:T(8,128)(2,1)S(1)} %reshape.102.wp, f32[64,128]{1,0:T(8,128)S(1)} %broadcast_in_dim.38.head, ...), custom_call_target="tpu_custom_call" | custom-call | flops 2415919104 | bytes 6291456 | tf_op jit(solution)/shard_map/pallas_call | solution.py:262
  103.0 13.5 %all-to-all-start = ((bf16[32,48,128]{2,1,0:T(8,128)(2,1)}), bf16[32,48,128]{2,1,0:T(8,128)(2,1)S(1)}, u32[]{:S(2)}, u32[]{:S(2)}) async-start(bf16[32,48,128]{2,1,0:T(8,128)(2,1)} %get-tuple-element.33), calls=%async_computation | async-start | bytes 786432 | tf_op jit(solution)/shard_map/all_to_all | solution.py:273
  116.7 6.3 %shard_map.132 = bf16[64,64,128]{2,1,0:T(8,128)(2,1)} custom-call(bf16[192,576]{1,0:T(8,128)(2,1)S(1)} %reshape.101.w, bf16[64,64,128]{2,1,0:T(8,128)(2,1)S(1)} %bitcast.37, bf16[64,64,128]{2,1,0:T(8,128)(2,1)S(1)} %bitcast.35, bf16[66,64,128]{2,1,0:T(8,128)(2,1)} %shard_map.131.own, bf16[66,64,128]{2,1,0:T(8,128)(2,1)} %collective-permute-done.8.prev, ...), custom_call_target="tpu_custom_call" | custom-call | flops 1811939328 | bytes 6291456 | tf_op jit(solution)/shard_map/pallas_call | solution.py:274
  123.0 3.8 %all-to-all-done.recv = bf16[32,48,128]{2,1,0:T(8,128)(2,1)S(1)} async-done(((bf16[32,48,128]{2,1,0:T(8,128)(2,1)}), bf16[32,48,128]{2,1,0:T(8,128)(2,1)S(1)}, u32[]{:S(2)}, u32[]{:S(2)}) %all-to-all-start) | async-done | bytes 393248 | tf_op jit(solution)/shard_map/all_to_all | solution.py:273
  126.8 2.3 %shard_map.133 = (f32[16,128]{1,0:T(8,128)}, f32[1,64]{1,0:T(1,128)}) custom-call(s32[3]{0:T(128)S(1)} %pad_add_fusion.pos, s32[8]{0:T(128)S(1)} %copy-done.4, bf16[128,96]{1,0:T(8,128)(2,1)S(1)} %copy.28.wt, bf16[64,64]{1,0:T(8,128)(2,1)S(1)} %bitcast.38, f32[64,128]{1,0:T(8,128)S(1)} %broadcast_in_dim.39.head, bf16[32,48,128]{2,1,0:T(8,128)(2,1)S(1)} %all-to-all-done.recv), custom_call_target="tpu_custom_call" | custom-call | flops 90596968 | bytes 1048576 | tf_op jit(solution)/shard_map/pallas_call | solution.py:277
  (53 shorter events, 14.8 us)
Async XLA Ops:
  2.3 6.5 %collective-permute-start = (bf16[5,64,128]{2,1,0:T(8,128)(2,1)S(1)}, bf16[5,64,128]{2,1,0:T(8,128)(2,1)S(1)}, u32[]{:S(2)}, u32[]{:S(2)}) collective-permute-start(bf16[5,64,128]{2,1,0:T(8,128)(2,1)S(1)} %pad_maximum_fusion.2), channel_id=1, source_target_pairs={{0,1},{1,2},{2,3},{4,5},{5,6},{6,7},{8,9},{9,10},{10,11},{12,13},{... | collective-permute-start | bytes 245768 | tf_op jit(solution)/shard_map/ppermute | solution.py:230
  6.8 5.8 %collective-permute-start.1 = (bf16[5,64,128]{2,1,0:T(8,128)(2,1)S(1)}, bf16[5,64,128]{2,1,0:T(8,128)(2,1)S(1)}, u32[]{:S(2)}, u32[]{:S(2)}) collective-permute-start(bf16[5,64,128]{2,1,0:T(8,128)(2,1)S(1)} %pad_maximum_fusion.3), channel_id=1, source_target_pairs={{1,0},{2,1},{3,2},{5,4},{6,5},{7,6},{9,8},{10,9},{11,10},{13,12},{... | collective-permute-start | bytes 245768 | tf_op jit(solution)/shard_map/ppermute | solution.py:231
  12.6 6.9 %copy-start.6 = (bf16[3,3,3,64,64]{4,3,2,1,0:T(8,128)(2,1)S(1)}, bf16[3,3,3,64,64]{4,3,2,1,0:T(8,128)(2,1)}, u32[]{:S(2)}) copy-start(bf16[3,3,3,64,64]{4,3,2,1,0:T(8,128)(2,1)} %param.13) | copy-start | bytes 663556
  14.0 33.6 %copy-start.2 = (bf16[70,64,128]{2,1,0:T(8,128)(2,1)}, bf16[70,64,128]{2,1,0:T(8,128)(2,1)S(1)}, u32[]{:S(2)}) copy-start(bf16[70,64,128]{2,1,0:T(8,128)(2,1)S(1)} %pad_maximum_fusion.own.base) | copy-start | bytes 3440644
  14.0 28.3 %collective-permute-start.2 = (bf16[70,64,128]{2,1,0:T(8,128)(2,1)S(1)}, bf16[70,64,128]{2,1,0:T(8,128)(2,1)}, u32[]{:S(2)}, u32[]{:S(2)}) collective-permute-start(bf16[70,64,128]{2,1,0:T(8,128)(2,1)S(1)} %pad_maximum_fusion.own.base), channel_id=1, source_target_pairs={{0,4},{4,8},{8,12},{12,16},{16,20},{20,24},{24,28},{28,32},{32,36}... | collective-permute-start | bytes 3440648 | tf_op jit(solution)/shard_map/ppermute | solution.py:228
  18.2 29.3 %collective-permute-start.3 = (bf16[70,64,128]{2,1,0:T(8,128)(2,1)S(1)}, bf16[70,64,128]{2,1,0:T(8,128)(2,1)}, u32[]{:S(2)}, u32[]{:S(2)}) collective-permute-start(bf16[70,64,128]{2,1,0:T(8,128)(2,1)S(1)} %pad_maximum_fusion.own.base), channel_id=1, source_target_pairs={{4,0},{8,4},{12,8},{16,12},{20,16},{24,20},{28,24},{32,28},{36,32}... | collective-permute-start | bytes 3440648 | tf_op jit(solution)/shard_map/ppermute | solution.py:228
  19.5 1.2 copy-start.1
  20.8 7.5 %copy-start.5 = (bf16[3,3,3,64,64]{4,3,2,1,0:T(8,128)(2,1)S(1)}, bf16[3,3,3,64,64]{4,3,2,1,0:T(8,128)(2,1)}, u32[]{:S(2)}) copy-start(bf16[3,3,3,64,64]{4,3,2,1,0:T(8,128)(2,1)} %param.12) | copy-start | bytes 663556
  21.9 44.4 %collective-permute-start.6 = (bf16[68,64,128]{2,1,0:T(8,128)(2,1)}, bf16[68,64,128]{2,1,0:T(8,128)(2,1)}, u32[]{:S(2)}, u32[]{:S(2)}) collective-permute-start(bf16[68,64,128]{2,1,0:T(8,128)(2,1)} %pad_maximum_fusion.1.own), channel_id=1, source_target_pairs={{0,4},{4,8},{8,12},{12,16},{16,20},{20,24},{24,28},{28,32},{32,36}... | collective-permute-start | bytes 3342344 | tf_op jit(solution)/shard_map/ppermute | solution.py:228
  27.0 44.4 %collective-permute-start.7 = (bf16[68,64,128]{2,1,0:T(8,128)(2,1)}, bf16[68,64,128]{2,1,0:T(8,128)(2,1)}, u32[]{:S(2)}, u32[]{:S(2)}) collective-permute-start(bf16[68,64,128]{2,1,0:T(8,128)(2,1)} %pad_maximum_fusion.1.own), channel_id=1, source_target_pairs={{4,0},{8,4},{12,8},{16,12},{20,16},{24,20},{28,24},{32,28},{36,32}... | collective-permute-start | bytes 3342344 | tf_op jit(solution)/shard_map/ppermute | solution.py:228
  32.6 5.7 %copy-start.7 = (bf16[64,64]{1,0:T(8,128)(2,1)S(1)}, bf16[64,64]{1,0:T(8,128)(2,1)}, u32[]{:S(2)}) copy-start(bf16[64,64]{1,0:T(8,128)(2,1)} %param.17) | copy-start | bytes 24580
  34.7 3.9 %copy-start.8 = (bf16[64]{0:T(256)(128)(2,1)S(1)}, bf16[64]{0:T(256)(128)(2,1)}, u32[]{:S(2)}) copy-start(bf16[64]{0:T(256)(128)(2,1)} %param.15) | copy-start | bytes 388
  54.0 36.1 %collective-permute-start.4 = (bf16[68,64,128]{2,1,0:T(8,128)(2,1)S(1)}, bf16[68,64,128]{2,1,0:T(8,128)(2,1)S(1)}, u32[]{:S(2)}, u32[]{:S(2)}) collective-permute-start(bf16[68,64,128]{2,1,0:T(8,128)(2,1)S(1)} %get-tuple-element.25.own), channel_id=1, source_target_pairs={{0,4},{4,8},{8,12},{12,16},{16,20},{20,24},{24,28},{28,32},{32,36}... | collective-permute-start | bytes 3342344 | tf_op jit(solution)/shard_map/ppermute | solution.py:228
  56.3 39.0 %collective-permute-start.5 = (bf16[68,64,128]{2,1,0:T(8,128)(2,1)S(1)}, bf16[68,64,128]{2,1,0:T(8,128)(2,1)S(1)}, u32[]{:S(2)}, u32[]{:S(2)}) collective-permute-start(bf16[68,64,128]{2,1,0:T(8,128)(2,1)S(1)} %get-tuple-element.25.own), channel_id=1, source_target_pairs={{4,0},{8,4},{12,8},{16,12},{20,16},{24,20},{28,24},{32,28},{36,32}... | collective-permute-start | bytes 3342344 | tf_op jit(solution)/shard_map/ppermute | solution.py:228
  71.3 24.0 %copy-start.3 = (bf16[70,64,128]{2,1,0:T(8,128)(2,1)S(1)}, bf16[70,64,128]{2,1,0:T(8,128)(2,1)}, u32[]{:S(2)}) copy-start(bf16[70,64,128]{2,1,0:T(8,128)(2,1)} %copy-done.2) | copy-start | bytes 3440644
  71.3 24.0 %copy-start.4 = (s32[8]{0:T(128)S(1)}, s32[8]{0:T(128)}, u32[]{:S(2)}) copy-start(s32[8]{0:T(128)} %listed.3) | copy-start | bytes 100
  78.0 38.7 %copy-start = (bf16[1,64,64,128]{3,2,1,0:T(8,128)(2,1)S(1)}, bf16[1,64,64,128]{3,2,1,0:T(8,128)(2,1)}, u32[]{:S(2)}) copy-start(bf16[1,64,64,128]{3,2,1,0:T(8,128)(2,1)} %param.10) | copy-start | bytes 3145732
  78.0 38.7 %collective-permute-start.8 = (bf16[66,64,128]{2,1,0:T(8,128)(2,1)}, bf16[66,64,128]{2,1,0:T(8,128)(2,1)}, u32[]{:S(2)}, u32[]{:S(2)}) collective-permute-start(bf16[66,64,128]{2,1,0:T(8,128)(2,1)} %shard_map.131.own), channel_id=1, source_target_pairs={{0,4},{4,8},{8,12},{12,16},{16,20},{20,24},{24,28},{28,32},{32,36}... | collective-permute-start | bytes 3244040 | tf_op jit(solution)/shard_map/ppermute | solution.py:228
  81.4 35.3 %collective-permute-start.9 = (bf16[66,64,128]{2,1,0:T(8,128)(2,1)}, bf16[66,64,128]{2,1,0:T(8,128)(2,1)}, u32[]{:S(2)}, u32[]{:S(2)}) collective-permute-start(bf16[66,64,128]{2,1,0:T(8,128)(2,1)} %shard_map.131.own), channel_id=1, source_target_pairs={{4,0},{8,4},{12,8},{16,12},{20,16},{24,20},{28,24},{32,28},{36,32}... | collective-permute-start | bytes 3244040 | tf_op jit(solution)/shard_map/ppermute | solution.py:228
  103.0 23.7 %all-to-all-start = ((bf16[32,48,128]{2,1,0:T(8,128)(2,1)}), bf16[32,48,128]{2,1,0:T(8,128)(2,1)S(1)}, u32[]{:S(2)}, u32[]{:S(2)}) async-start(bf16[32,48,128]{2,1,0:T(8,128)(2,1)} %get-tuple-element.33), calls=%async_computation | async-start | bytes 786432 | tf_op jit(solution)/shard_map/all_to_all | solution.py:273

commit v4 on v3

--- a/solution.py
+++ b/solution.py
@@ -11,7 +11,6 @@
 F32 = jnp.float32
 BF16 = jnp.bfloat16
 MIB = 1 << 20
-UNROLL = 16
 
 
 def logistic(x):
@@ -33,7 +32,7 @@
     return [t.astype(BF16) for t in shifted(x, lane)]
 
 
-def conv_rows(load, weight_ref, rows, emit, silu_in=False, frames=3, unroll=UNROLL):
+def conv_rows(load, weight_ref, rows, emit, silu_in=False, frames=3):
     def pair(p):
         sides = []
         for j in range(2):
@@ -54,7 +53,8 @@
         emit(2 * p - 1, carry[1] + y[1][0] + y[2][1])
         return (y[0][0] + y[1][1], y[0][1])
 
-    lax.fori_loop(1, rows // 2, step, carry, unroll=unroll)
+    for p in range(1, rows // 2):
+        carry = step(p, carry)
 
 
 def row_mask(first, r, limit):
@@ -148,10 +148,11 @@
     lane = lax.broadcasted_iota(jnp.int32, (units, width), 1)
 
     def piece(t):
-        ok = jnp.where((t >= 0) & (t < frames), 1.0, 0.0).astype(BF16)
-        return recv[jnp.clip(t, 0, frames - 1), pl.ds(0, half)] * ok
-
-    def step(i, _):
+        if 0 <= t < frames:
+            return recv[t, pl.ds(0, half)]
+        return jnp.zeros((half, width), BF16)
+
+    for i in range(frames // 2):
         f = [piece(2 * i + d) for d in (-1, 0, 1, 2)]
         rhs = jnp.concatenate(
             [jnp.concatenate(f[:3], axis=0), jnp.concatenate(f[1:], axis=0)], axis=1
@@ -162,9 +163,7 @@
         right = pltpu.roll(b[:units], width // 2, 1) + b[units:]
         q = jnp.where(lane < width // 2, left, right)
         total[...] += q * logistic(q)
-        return 0
-
-    lax.fori_loop(0, frames // 2, step, 0, unroll=8)
+
     both = total[...]
     mean = (both + pltpu.roll(both, width // 2, 1)) * (1.0 / frames)
     mixed = jnp.zeros_like(mean)
@@ -177,6 +176,35 @@
     score[...] = jnp.sum(act, axis=0, keepdims=True)[:, : width // 2]
 
 
+def turned(x):
+    return x.astype(F32).T.astype(BF16)
+
+
+def weights_kernel(
+    pos, ka, kb, kp, kt, km, hp, ht, wa, wb, wbt, wat, wp, wt, mixer, plane_row, time_row, pool
+):
+    odd = lax.rem(pos[2], 2)
+    ch, width = plane_row.shape
+    order = [jnp.where(odd == 1, a, 2 - a) for a in range(3)]
+    for b in range(3):
+        rows = pl.ds(b * ch, ch)
+        for src, dst in ((ka, wa), (kb, wb)):
+            dst[rows] = turned(jnp.concatenate([src[a, b, e] for a in order for e in range(3)], axis=0))
+        for src, dst in ((kb, wbt), (ka, wat)):
+            dst[rows] = jnp.concatenate([src[2 - a, 2 - b, 2 - e] for a in order for e in range(3)], axis=1)
+        wp[rows] = turned(jnp.concatenate([kp[b, e] for e in range(3)], axis=0))
+    half = ch // 2
+    for i in range(2):
+        part = [kt[a, pl.ds(i * half, half)] for a in range(3)]
+        wt[pl.ds(i * ch, ch)] = turned(jnp.concatenate(part, axis=0))
+    mixer[...] = turned(km[...])
+    for src, dst in ((hp, plane_row), (ht, time_row)):
+        dst[...] = jnp.broadcast_to(src[...].astype(F32), (width, ch)).T
+    pairs = lax.broadcasted_iota(jnp.int32, pool.shape, 0) % width // 2
+    lanes = lax.broadcasted_iota(jnp.int32, pool.shape, 1) % (width // 2)
+    pool[...] = jnp.where(pairs == lanes, 0.25, 0.0).astype(BF16)
+
+
 VMEM = pl.BlockSpec(memory_space=pltpu.VMEM)
 SMEM = pl.BlockSpec(memory_space=pltpu.SMEM)
 
@@ -193,13 +221,9 @@
     )
 
 
-def stacked(kernel):
-    a, b, e, c, o = kernel.shape
-    return jnp.transpose(kernel, (1, 4, 0, 2, 3)).reshape(b * o, a * e * c)
-
-
-def flipped(kernel):
-    return jnp.swapaxes(kernel[::-1, ::-1, ::-1], 3, 4)
+def swaps(size):
+    pairs = [[(i, i + 1) for i in range(start, size - 1, 2)] for start in (0, 1)]
+    return [p + [(j, i) for i, j in p] for p in pairs]
 
 
 def shards(
@@ -217,33 +241,44 @@
     v, c = video_in[0], cotangent[0]
     n, ch, width = v.shape
     tm, sp = lax.axis_size("tm"), lax.axis_size("space")
-    up_tm = [(i, i + 1) for i in range(tm - 1)]
-    dn_tm = [(j, i) for i, j in up_tm]
-    up_sp = [(i, i + 1) for i in range(sp - 1)]
-    dn_sp = [(j, i) for i, j in up_sp]
+    swap_first, swap_second = swaps(tm)
     me = lax.axis_index("tm")
     pos = jnp.stack([lax.axis_index("space") * n, sp * n, me]).astype(jnp.int32)
 
     def both(x):
-        return lax.ppermute(x, "tm", up_tm), lax.ppermute(x, "tm", dn_tm)
-
-    up = lax.ppermute(jnp.concatenate([v[n - 3 :], c[n - 2 :]]), "space", up_sp)
-    dn = lax.ppermute(jnp.concatenate([v[:3], c[:2]]), "space", dn_sp)
+        return lax.ppermute(x, "tm", swap_first), lax.ppermute(x, "tm", swap_second)
+
+    even = lax.axis_index("space") % 2 == 0
+
+    def edge(at_end):
+        ends = [lax.dynamic_slice_in_dim(x, jnp.where(at_end, n - k, 0), k) for x, k in ((v, 3), (c, 2))]
+        return jnp.concatenate(ends)
+
+    row_first, row_second = swaps(sp)
+    got = lax.ppermute(edge(even), "space", row_first)
+    other = lax.ppermute(edge(~even), "space", row_second)
+    up, dn = jnp.where(even, other, got), jnp.where(even, got, other)
     v_own = jnp.concatenate([up[:3], v, dn[:3]])
     c_own = jnp.concatenate([up[3:], c, dn[3:]])
     v_p, v_n = both(v_own)
     c_p, c_n = both(c_own)
-    wa, wb = stacked(kernel_a), stacked(kernel_b)
-    wbt, wat = stacked(flipped(kernel_b)), stacked(flipped(kernel_a))
-    wp = stacked(plane_kernel[None])
-    spread = lambda h: jnp.broadcast_to(h.astype(F32)[:, None], (ch, width))
-    idx = jnp.arange(2 * width)[:, None] % width // 2
-    pool = jnp.where(idx == jnp.arange(width)[None, :] % (width // 2), 0.25, 0.0).astype(BF16)
-    wt = jnp.transpose(time_kernel.reshape(3, 2, ch // 2, ch), (1, 3, 0, 2)).reshape(2 * ch, 3 * ch // 2)
-    mixer, plane_row, time_row = time_mixer.T, spread(plane_head), spread(time_head)
-    wa, wb, wbt, wat, wp, wt, mixer, plane_row, time_row, pool = lax.optimization_barrier(
-        (wa, wb, wbt, wat, wp, wt, mixer, plane_row, time_row, pool)
-    )
+    kernel_a, kernel_b, _ = lax.optimization_barrier((kernel_a, kernel_b, c_own))
+    shapes = [((3 * ch, 9 * ch), BF16)] * 4 + [
+        ((3 * ch, 3 * ch), BF16),
+        ((2 * ch, 3 * ch // 2), BF16),
+        ((ch, ch), BF16),
+        ((ch, width), F32),
+        ((ch, width), F32),
+        ((2 * width, width), BF16),
+    ]
+    wa, wb, wbt, wat, wp, wt, mixer, plane_row, time_row, pool = call(
+        weights_kernel,
+        tuple(jax.ShapeDtypeStruct(shape, dtype) for shape, dtype in shapes),
+        [SMEM] + [VMEM] * 7,
+        [],
+        10**7,
+        2 * MIB,
+    )(pos, kernel_a, kernel_b, plane_kernel, time_kernel, time_mixer, plane_head[None], time_head[None])
 
     def rows(r, dtype=BF16):
         return jax.ShapeDtypeStruct((r, ch, width), dtype)

time: 131 us -> 124 us (0.947)
  local copies, waits for them, and re-layouts: 13.9 us -> 2.46 us
  waiting for transfers between devices: 42 us -> 49.5 us
  Pallas kernels: 29.4 us -> 28 us
    ppermute x10, waiting for transfers between devices: 38.2 us -> 45.5 us  [the longest x4 42.4 us: both(): lax.ppermute(x, 'tm', swap_first)]
    transpose x3 -> x0, local copies, waits for them, and re-layouts: 5.18 us -> none  [stacked(): return jnp.transpose(kernel, (1, 4, 0, 2, 3)).reshape(b * o, a * e * c)]
    reshape x7 -> x0, local copies, waits for them, and re-layouts: 4.84 us -> none  [the longest x5 3.91 us: stacked(): return jnp.transpose(kernel, (1, 4, 0, 2, 3)).reshape(b * o, a * e * c)]
    ppermute x10, starting transfers between devices: 26.4 us -> 22.6 us  [the longest x4 12.2 us: both(): lax.ppermute(x, 'tm', swap_first)]
    all_to_all x1, starting transfers between devices: 13.5 us -> 17.1 us  [shards(): recv = lax.all_to_all(send, 'tm', split_axis=0, concat_axis=0, tiled=True)]
    dynamic_slice x0 -> x2, local copies, waits for them, and re-layouts: none -> 1.7 us  [edge(): lax.dynamic_slice_in_dim(x, jnp.where(at_end, n - k, 0), k)]
    slice x2 -> x0, local copies, waits for them, and re-layouts: 1.61 us -> none  [shards(): up = lax.ppermute(jnp.concatenate([v[n - 3:], c[n - 2:]]), 'space', up_sp)]
  transfers between devices with their start and end apart: 11 -> 11, of which waited for: 8 -> 5; matrix products, arithmetic and copies ran while one was open for 10% -> 1% of each run, Pallas kernels for 21% -> 21%
where the time goes in v4:
time: 124 us; the launch traced here: 123 us
  waiting for transfers between devices  49.5 us (40%)
  starting transfers between devices  39.7 us (32%)
  Pallas kernels  28 us (23%)
  local copies, waits for them, and re-layouts  2.46 us (2%)
  other arithmetic  2.42 us (2%)
    ppermute x4, waiting for transfers between devices, both(): lax.ppermute(x, 'tm', swap_first)  42.4 us
    all_to_all x1, starting transfers between devices, shards(): recv = lax.all_to_all(send, 'tm', split_axis=0, concat_axis=0, tiled=True)  17.1 us
    ppermute x4, starting transfers between devices, both(): lax.ppermute(x, 'tm', swap_first)  12.2 us
    pallas_call x1, Pallas kernels, shards(): call(video_kernel, (rows(n), jax.ShapeDtypeStruct((tm, ch // 2 + quarter,...  7.37 us
    pallas_call x1, Pallas kernels, shards(): call(grad_kernel, rows(n + 2), [SMEM] + [VMEM] * 5, [], flops, 6 * MIB)  6 us
    pallas_call x1, Pallas kernels, shards(): call(input_grad_kernel, rows(n), [VMEM] * 6, [], flops, 6 * MIB)  5.93 us
    pallas_call x1, Pallas kernels, shards(): call(first_kernel, (rows(n + 4), rows(n + 4)), [SMEM] + [VMEM] * 4, [], f...  5.87 us
    ppermute x4, starting transfers between devices, both(): lax.ppermute(x, 'tm', swap_second)  5.75 us
  transfers between devices with their start and end apart: 11, of which 5 were waited for; matrix products, arithmetic and copies ran while one was open for 1% of the time, Pallas kernels for 21%

profile of v4, /device:TPU:1, one launch (start us, length us, event | category | flops | bytes accessed | tf_op | source)
XLA Modules:
  0.0 122.9 jit_solution(17953312401209872539)
XLA Ops:
  0.7 0.9 dynamic-slice_bitcast_fusion.1
  2.4 1.5 %collective-permute-start.1 = (bf16[5,64,128]{2,1,0:T(8,128)(2,1)S(1)}, bf16[5,64,128]{2,1,0:T(8,128)(2,1)S(1)}, u32[]{:S(2)}, u32[]{:S(2)}) collective-permute-start(bf16[5,64,128]{2,1,0:T(8,128)(2,1)S(1)} %pad_maximum_fusion.3), channel_id=1, source_target_pairs={{0,1},{2,3},{1,0},{3,2},{4,5},{6,7},{5,4},{7,6},{8,9},{10,11},{9,8... | collective-permute-start | bytes 245768 | tf_op jit(solution)/shard_map/ppermute | solution.py:258
  3.9 3.1 %collective-permute-start = (bf16[5,64,128]{2,1,0:T(8,128)(2,1)S(1)}, bf16[5,64,128]{2,1,0:T(8,128)(2,1)S(1)}, u32[]{:S(2)}, u32[]{:S(2)}) collective-permute-start(bf16[5,64,128]{2,1,0:T(8,128)(2,1)S(1)} %pad_maximum_fusion.2), channel_id=1, source_target_pairs={{1,2},{2,1},{5,6},{6,5},{9,10},{10,9},{13,14},{14,13},{17,18},{18,... | collective-permute-start | bytes 245768 | tf_op jit(solution)/shard_map/ppermute | solution.py:259
  7.0 3.0 %collective-permute-done = bf16[5,64,128]{2,1,0:T(8,128)(2,1)S(1)} collective-permute-done((bf16[5,64,128]{2,1,0:T(8,128)(2,1)S(1)}, bf16[5,64,128]{2,1,0:T(8,128)(2,1)S(1)}, u32[]{:S(2)}, u32[]{:S(2)}) %collective-permute-start) | collective-permute-done | bytes 81952 | tf_op jit(solution)/shard_map/ppermute | solution.py:259
  10.1 1.2 pad_maximum_fusion.own.base
  11.3 1.4 %collective-permute-start.2 = (bf16[70,64,128]{2,1,0:T(8,128)(2,1)}, bf16[70,64,128]{2,1,0:T(8,128)(2,1)}, u32[]{:S(2)}, u32[]{:S(2)}) collective-permute-start(bf16[70,64,128]{2,1,0:T(8,128)(2,1)} %pad_maximum_fusion.own.base), channel_id=1, source_target_pairs={{0,4},{8,12},{16,20},{24,28},{32,36},{40,44},{48,52},{56,60},{64,6... | collective-permute-start | bytes 3440648 | tf_op jit(solution)/shard_map/ppermute | solution.py:249
  12.7 1.7 %collective-permute-start.3 = (bf16[70,64,128]{2,1,0:T(8,128)(2,1)}, bf16[70,64,128]{2,1,0:T(8,128)(2,1)}, u32[]{:S(2)}, u32[]{:S(2)}) collective-permute-start(bf16[70,64,128]{2,1,0:T(8,128)(2,1)} %pad_maximum_fusion.own.base), channel_id=1, source_target_pairs={{4,8},{12,16},{20,24},{28,32},{36,40},{44,48},{52,56},{60,64},{68,... | collective-permute-start | bytes 3440648 | tf_op jit(solution)/shard_map/ppermute | solution.py:249
  14.4 1.1 pad_maximum_fusion.1.own
  15.6 2.5 %collective-permute-start.6 = (bf16[68,64,128]{2,1,0:T(8,128)(2,1)}, bf16[68,64,128]{2,1,0:T(8,128)(2,1)}, u32[]{:S(2)}, u32[]{:S(2)}) collective-permute-start(bf16[68,64,128]{2,1,0:T(8,128)(2,1)} %pad_maximum_fusion.1.own), channel_id=1, source_target_pairs={{0,4},{8,12},{16,20},{24,28},{32,36},{40,44},{48,52},{56,60},{64,6... | collective-permute-start | bytes 3342344 | tf_op jit(solution)/shard_map/ppermute | solution.py:249
  18.1 1.7 %collective-permute-start.7 = (bf16[68,64,128]{2,1,0:T(8,128)(2,1)}, bf16[68,64,128]{2,1,0:T(8,128)(2,1)}, u32[]{:S(2)}, u32[]{:S(2)}) collective-permute-start(bf16[68,64,128]{2,1,0:T(8,128)(2,1)} %pad_maximum_fusion.1.own), channel_id=1, source_target_pairs={{4,8},{12,16},{20,24},{28,32},{36,40},{44,48},{52,56},{60,64},{68,... | collective-permute-start | bytes 3342344 | tf_op jit(solution)/shard_map/ppermute | solution.py:249
  19.9 1.1 shard_map.129
  21.7 17.3 %collective-permute-done.2.prev = bf16[70,64,128]{2,1,0:T(8,128)(2,1)} collective-permute-done((bf16[70,64,128]{2,1,0:T(8,128)(2,1)}, bf16[70,64,128]{2,1,0:T(8,128)(2,1)}, u32[]{:S(2)}, u32[]{:S(2)}) %collective-permute-start.2) | collective-permute-done | bytes 1146912 | tf_op jit(solution)/shard_map/ppermute | solution.py:249
  39.0 5.9 %shard_map.130 = (bf16[68,64,128]{2,1,0:T(8,128)(2,1)S(1)}, bf16[68,64,128]{2,1,0:T(8,128)(2,1)S(1)}) custom-call(s32[3]{0:T(128)S(1)} %pad_add_fusion.pos, bf16[192,576]{1,0:T(8,128)(2,1)S(1)} %get-tuple-element.28.w, bf16[70,64,128]{2,1,0:T(8,128)(2,1)} %pad_maximum_fusion.own.base, bf16[70,64,128]{2,1,0:T(8,128)(2,1)} %collective-permute-done.2.prev, ...), custom_call_target="tpu_custom_call" | custom-call | flops 1811939328 | bytes 6291456 | tf_op jit(solution)/shard_map/pallas_call | solution.py:287
  44.8 4.2 %collective-permute-start.4 = (bf16[68,64,128]{2,1,0:T(8,128)(2,1)S(1)}, bf16[68,64,128]{2,1,0:T(8,128)(2,1)S(1)}, u32[]{:S(2)}, u32[]{:S(2)}) collective-permute-start(bf16[68,64,128]{2,1,0:T(8,128)(2,1)S(1)} %get-tuple-element.29.own), channel_id=1, source_target_pairs={{0,4},{8,12},{16,20},{24,28},{32,36},{40,44},{48,52},{56,60},{64,6... | collective-permute-start | bytes 3342344 | tf_op jit(solution)/shard_map/ppermute | solution.py:249
  49.7 13.0 %collective-permute-done.6.prev = bf16[68,64,128]{2,1,0:T(8,128)(2,1)} collective-permute-done((bf16[68,64,128]{2,1,0:T(8,128)(2,1)}, bf16[68,64,128]{2,1,0:T(8,128)(2,1)}, u32[]{:S(2)}, u32[]{:S(2)}) %collective-permute-start.6) | collective-permute-done | bytes 1114144 | tf_op jit(solution)/shard_map/ppermute | solution.py:249
  62.7 6.0 %shard_map.132.own = bf16[66,64,128]{2,1,0:T(8,128)(2,1)} custom-call(s32[3]{0:T(128)S(1)} %pad_add_fusion.pos, bf16[192,576]{1,0:T(8,128)(2,1)S(1)} %get-tuple-element.32.w, bf16[68,64,128]{2,1,0:T(8,128)(2,1)S(1)} %get-tuple-element.33.slope, bf16[68,64,128]{2,1,0:T(8,128)(2,1)} %pad_maximum_fusion.1.own, ...), custom_call_target="tpu_custom_call" | custom-call | flops 1811939328 | bytes 6291456 | tf_op jit(solution)/shard_map/pallas_call | solution.py:291
  68.7 4.1 %collective-permute-start.8 = (bf16[66,64,128]{2,1,0:T(8,128)(2,1)}, bf16[66,64,128]{2,1,0:T(8,128)(2,1)}, u32[]{:S(2)}, u32[]{:S(2)}) collective-permute-start(bf16[66,64,128]{2,1,0:T(8,128)(2,1)} %shard_map.132.own), channel_id=1, source_target_pairs={{0,4},{8,12},{16,20},{24,28},{32,36},{40,44},{48,52},{56,60},{64,6... | collective-permute-start | bytes 3244040 | tf_op jit(solution)/shard_map/ppermute | solution.py:249
  72.8 1.7 %collective-permute-start.9 = (bf16[66,64,128]{2,1,0:T(8,128)(2,1)}, bf16[66,64,128]{2,1,0:T(8,128)(2,1)}, u32[]{:S(2)}, u32[]{:S(2)}) collective-permute-start(bf16[66,64,128]{2,1,0:T(8,128)(2,1)} %shard_map.132.own), channel_id=1, source_target_pairs={{4,8},{12,16},{20,24},{28,32},{36,40},{44,48},{52,56},{60,64},{68,... | collective-permute-start | bytes 3244040 | tf_op jit(solution)/shard_map/ppermute | solution.py:249
  74.5 12.2 %collective-permute-done.4.prev = bf16[68,64,128]{2,1,0:T(8,128)(2,1)S(1)} collective-permute-done((bf16[68,64,128]{2,1,0:T(8,128)(2,1)S(1)}, bf16[68,64,128]{2,1,0:T(8,128)(2,1)S(1)}, u32[]{:S(2)}, u32[]{:S(2)}) %collective-permute-start.4) | collective-permute-done | bytes 1114144 | tf_op jit(solution)/shard_map/ppermute | solution.py:249
  86.7 7.4 %shard_map.131 = (bf16[64,64,128]{2,1,0:T(8,128)(2,1)}, bf16[32,48,128]{2,1,0:T(8,128)(2,1)}) custom-call(s32[3]{0:T(128)S(1)} %pad_add_fusion.pos, s32[8]{0:T(128)S(1)} %copy-done.9, bf16[192,576]{1,0:T(8,128)(2,1)S(1)} %get-tuple-element.24.w, bf16[192,192]{1,0:T(8,128)(2,1)S(1)} %get-tuple-element.25.wp, f32[64,128]{1,0:T(8,128)S(1)} %get-tuple-element.26.head, ...), custom_call_target="tpu_custom_call" | custom-call | flops 2415919104 | bytes 6291456 | tf_op jit(solution)/shard_map/pallas_call | solution.py:297
  94.1 17.1 %all-to-all-start = ((bf16[32,48,128]{2,1,0:T(8,128)(2,1)}), bf16[32,48,128]{2,1,0:T(8,128)(2,1)S(1)}, u32[]{:S(2)}, u32[]{:S(2)}) async-start(bf16[32,48,128]{2,1,0:T(8,128)(2,1)} %get-tuple-element.37), calls=%async_computation | async-start | bytes 786432 | tf_op jit(solution)/shard_map/all_to_all | solution.py:308
  111.2 5.9 %shard_map.133 = bf16[64,64,128]{2,1,0:T(8,128)(2,1)} custom-call(bf16[192,576]{1,0:T(8,128)(2,1)S(1)} %copy-done.11, bf16[64,64,128]{2,1,0:T(8,128)(2,1)S(1)} %bitcast.21, bf16[64,64,128]{2,1,0:T(8,128)(2,1)S(1)} %bitcast.19, bf16[66,64,128]{2,1,0:T(8,128)(2,1)} %shard_map.132.own, bf16[66,64,128]{2,1,0:T(8,128)(2,1)} %collective-permute-done.8.prev, ...), custom_call_target="tpu_custom_call" | custom-call | flops 1811939328 | bytes 6291456 | tf_op jit(solution)/shard_map/pallas_call | solution.py:309
  117.2 4.0 %all-to-all-done.recv = bf16[32,48,128]{2,1,0:T(8,128)(2,1)S(1)} async-done(((bf16[32,48,128]{2,1,0:T(8,128)(2,1)}), bf16[32,48,128]{2,1,0:T(8,128)(2,1)S(1)}, u32[]{:S(2)}, u32[]{:S(2)}) %all-to-all-start) | async-done | bytes 393248 | tf_op jit(solution)/shard_map/all_to_all | solution.py:308
  121.1 1.8 %shard_map.134 = (f32[16,128]{1,0:T(8,128)}, f32[1,64]{1,0:T(1,128)}) custom-call(s32[3]{0:T(128)S(1)} %pad_add_fusion.pos, s32[8]{0:T(128)S(1)} %copy-done.9, bf16[128,96]{1,0:T(8,128)(2,1)S(1)} %get-tuple-element.34.wt, bf16[64,64]{1,0:T(8,128)(2,1)S(1)} %get-tuple-element.35.mixer, f32[64,128]{1,0:T(8,128)S(1)} %get-tuple-element.36.head, ...), custom_call_target="tpu_custom_call" | custom-call | flops 90596968 | bytes 1048576 | tf_op jit(solution)/shard_map/pallas_call | solution.py:312
  (40 shorter events, 2.4 us)
Async XLA Ops:
  0.6 9.5 %copy-start = (bf16[1,64,64,128]{3,2,1,0:T(8,128)(2,1)S(1)}, bf16[1,64,64,128]{3,2,1,0:T(8,128)(2,1)}, u32[]{:S(2)}) copy-start(bf16[1,64,64,128]{3,2,1,0:T(8,128)(2,1)} %param.10) | copy-start | bytes 3145732
  2.4 4.6 %collective-permute-start.1 = (bf16[5,64,128]{2,1,0:T(8,128)(2,1)S(1)}, bf16[5,64,128]{2,1,0:T(8,128)(2,1)S(1)}, u32[]{:S(2)}, u32[]{:S(2)}) collective-permute-start(bf16[5,64,128]{2,1,0:T(8,128)(2,1)S(1)} %pad_maximum_fusion.3), channel_id=1, source_target_pairs={{0,1},{2,3},{1,0},{3,2},{4,5},{6,7},{5,4},{7,6},{8,9},{10,11},{9,8... | collective-permute-start | bytes 245768 | tf_op jit(solution)/shard_map/ppermute | solution.py:258
  3.9 6.2 %collective-permute-start = (bf16[5,64,128]{2,1,0:T(8,128)(2,1)S(1)}, bf16[5,64,128]{2,1,0:T(8,128)(2,1)S(1)}, u32[]{:S(2)}, u32[]{:S(2)}) collective-permute-start(bf16[5,64,128]{2,1,0:T(8,128)(2,1)S(1)} %pad_maximum_fusion.2), channel_id=1, source_target_pairs={{1,2},{2,1},{5,6},{6,5},{9,10},{10,9},{13,14},{14,13},{17,18},{18,... | collective-permute-start | bytes 245768 | tf_op jit(solution)/shard_map/ppermute | solution.py:259
  10.1 4.3 %copy-start.1 = (bf16[1,64,64,128]{3,2,1,0:T(8,128)(2,1)S(1)}, bf16[1,64,64,128]{3,2,1,0:T(8,128)(2,1)}, u32[]{:S(2)}) copy-start(bf16[1,64,64,128]{3,2,1,0:T(8,128)(2,1)} %param.11) | copy-start | bytes 3145732
  11.3 27.7 %collective-permute-start.2 = (bf16[70,64,128]{2,1,0:T(8,128)(2,1)}, bf16[70,64,128]{2,1,0:T(8,128)(2,1)}, u32[]{:S(2)}, u32[]{:S(2)}) collective-permute-start(bf16[70,64,128]{2,1,0:T(8,128)(2,1)} %pad_maximum_fusion.own.base), channel_id=1, source_target_pairs={{0,4},{8,12},{16,20},{24,28},{32,36},{40,44},{48,52},{56,60},{64,6... | collective-permute-start | bytes 3440648 | tf_op jit(solution)/shard_map/ppermute | solution.py:249
  12.7 26.3 %collective-permute-start.3 = (bf16[70,64,128]{2,1,0:T(8,128)(2,1)}, bf16[70,64,128]{2,1,0:T(8,128)(2,1)}, u32[]{:S(2)}, u32[]{:S(2)}) collective-permute-start(bf16[70,64,128]{2,1,0:T(8,128)(2,1)} %pad_maximum_fusion.own.base), channel_id=1, source_target_pairs={{4,8},{12,16},{20,24},{28,32},{36,40},{44,48},{52,56},{60,64},{68,... | collective-permute-start | bytes 3440648 | tf_op jit(solution)/shard_map/ppermute | solution.py:249
  14.4 5.5 %copy-start.2 = (bf16[3,3,3,64,64]{4,3,2,1,0:T(8,128)(2,1)S(1)}, bf16[3,3,3,64,64]{4,3,2,1,0:T(8,128)(2,1)}, u32[]{:S(2)}) copy-start(bf16[3,3,3,64,64]{4,3,2,1,0:T(8,128)(2,1)} %ka) | copy-start | bytes 663556
  14.4 5.5 %copy-start.3 = (bf16[3,3,3,64,64]{4,3,2,1,0:T(8,128)(2,1)S(1)}, bf16[3,3,3,64,64]{4,3,2,1,0:T(8,128)(2,1)}, u32[]{:S(2)}) copy-start(bf16[3,3,3,64,64]{4,3,2,1,0:T(8,128)(2,1)} %kb) | copy-start | bytes 663556
  14.4 5.5 %copy-start.4 = (bf16[3,3,64,64]{3,2,1,0:T(8,128)(2,1)S(1)}, bf16[3,3,64,64]{3,2,1,0:T(8,128)(2,1)}, u32[]{:S(2)}) copy-start(bf16[3,3,64,64]{3,2,1,0:T(8,128)(2,1)} %kp.1) | copy-start | bytes 221188
  14.4 5.5 %copy-start.5 = (bf16[3,64,64]{2,1,0:T(8,128)(2,1)S(1)}, bf16[3,64,64]{2,1,0:T(8,128)(2,1)}, u32[]{:S(2)}) copy-start(bf16[3,64,64]{2,1,0:T(8,128)(2,1)} %kt.1) | copy-start | bytes 73732
  14.4 5.5 %copy-start.6 = (bf16[64,64]{1,0:T(8,128)(2,1)S(1)}, bf16[64,64]{1,0:T(8,128)(2,1)}, u32[]{:S(2)}) copy-start(bf16[64,64]{1,0:T(8,128)(2,1)} %km.1) | copy-start | bytes 24580
  14.4 5.5 %copy-start.7 = (bf16[64]{0:T(256)(128)(2,1)S(1)}, bf16[64]{0:T(256)(128)(2,1)}, u32[]{:S(2)}) copy-start(bf16[64]{0:T(256)(128)(2,1)} %param.15) | copy-start | bytes 388
  14.4 5.5 %copy-start.8 = (bf16[64]{0:T(256)(128)(2,1)S(1)}, bf16[64]{0:T(256)(128)(2,1)}, u32[]{:S(2)}) copy-start(bf16[64]{0:T(256)(128)(2,1)} %param.18) | copy-start | bytes 388
  15.6 47.1 %collective-permute-start.6 = (bf16[68,64,128]{2,1,0:T(8,128)(2,1)}, bf16[68,64,128]{2,1,0:T(8,128)(2,1)}, u32[]{:S(2)}, u32[]{:S(2)}) collective-permute-start(bf16[68,64,128]{2,1,0:T(8,128)(2,1)} %pad_maximum_fusion.1.own), channel_id=1, source_target_pairs={{0,4},{8,12},{16,20},{24,28},{32,36},{40,44},{48,52},{56,60},{64,6... | collective-permute-start | bytes 3342344 | tf_op jit(solution)/shard_map/ppermute | solution.py:249
  18.1 44.6 %collective-permute-start.7 = (bf16[68,64,128]{2,1,0:T(8,128)(2,1)}, bf16[68,64,128]{2,1,0:T(8,128)(2,1)}, u32[]{:S(2)}, u32[]{:S(2)}) collective-permute-start(bf16[68,64,128]{2,1,0:T(8,128)(2,1)} %pad_maximum_fusion.1.own), channel_id=1, source_target_pairs={{4,8},{12,16},{20,24},{28,32},{36,40},{44,48},{52,56},{60,64},{68,... | collective-permute-start | bytes 3342344 | tf_op jit(solution)/shard_map/ppermute | solution.py:249
  21.0 0.7 copy-start.10
  44.8 41.9 %collective-permute-start.4 = (bf16[68,64,128]{2,1,0:T(8,128)(2,1)S(1)}, bf16[68,64,128]{2,1,0:T(8,128)(2,1)S(1)}, u32[]{:S(2)}, u32[]{:S(2)}) collective-permute-start(bf16[68,64,128]{2,1,0:T(8,128)(2,1)S(1)} %get-tuple-element.29.own), channel_id=1, source_target_pairs={{0,4},{8,12},{16,20},{24,28},{32,36},{40,44},{48,52},{56,60},{64,6... | collective-permute-start | bytes 3342344 | tf_op jit(solution)/shard_map/ppermute | solution.py:249
  49.0 37.7 %collective-permute-start.5 = (bf16[68,64,128]{2,1,0:T(8,128)(2,1)S(1)}, bf16[68,64,128]{2,1,0:T(8,128)(2,1)S(1)}, u32[]{:S(2)}, u32[]{:S(2)}) collective-permute-start(bf16[68,64,128]{2,1,0:T(8,128)(2,1)S(1)} %get-tuple-element.29.own), channel_id=1, source_target_pairs={{4,8},{12,16},{20,24},{28,32},{36,40},{44,48},{52,56},{60,64},{68,... | collective-permute-start | bytes 3342344 | tf_op jit(solution)/shard_map/ppermute | solution.py:249
  62.7 24.0 %copy-start.9 = (s32[8]{0:T(128)S(1)}, s32[8]{0:T(128)}, u32[]{:S(2)}) copy-start(s32[8]{0:T(128)} %listed.3) | copy-start | bytes 100
  68.7 42.5 %collective-permute-start.8 = (bf16[66,64,128]{2,1,0:T(8,128)(2,1)}, bf16[66,64,128]{2,1,0:T(8,128)(2,1)}, u32[]{:S(2)}, u32[]{:S(2)}) collective-permute-start(bf16[66,64,128]{2,1,0:T(8,128)(2,1)} %shard_map.132.own), channel_id=1, source_target_pairs={{0,4},{8,12},{16,20},{24,28},{32,36},{40,44},{48,52},{56,60},{64,6... | collective-permute-start | bytes 3244040 | tf_op jit(solution)/shard_map/ppermute | solution.py:249
  72.8 38.4 %collective-permute-start.9 = (bf16[66,64,128]{2,1,0:T(8,128)(2,1)}, bf16[66,64,128]{2,1,0:T(8,128)(2,1)}, u32[]{:S(2)}, u32[]{:S(2)}) collective-permute-start(bf16[66,64,128]{2,1,0:T(8,128)(2,1)} %shard_map.132.own), channel_id=1, source_target_pairs={{4,8},{12,16},{20,24},{28,32},{36,40},{44,48},{52,56},{60,64},{68,... | collective-permute-start | bytes 3244040 | tf_op jit(solution)/shard_map/ppermute | solution.py:249
  86.7 24.5 %copy-start.11 = (bf16[192,576]{1,0:T(8,128)(2,1)S(1)}, bf16[192,576]{1,0:T(8,128)(2,1)}, u32[]{:S(2)}) copy-start(bf16[192,576]{1,0:T(8,128)(2,1)} %copy-done.10) | copy-start | bytes 663556
  94.1 27.0 %all-to-all-start = ((bf16[32,48,128]{2,1,0:T(8,128)(2,1)}), bf16[32,48,128]{2,1,0:T(8,128)(2,1)S(1)}, u32[]{:S(2)}, u32[]{:S(2)}) async-start(bf16[32,48,128]{2,1,0:T(8,128)(2,1)} %get-tuple-element.37), calls=%async_computation | async-start | bytes 786432 | tf_op jit(solution)/shard_map/all_to_all | solution.py:308

commit v5 on v4

--- a/solution.py
+++ b/solution.py
@@ -32,7 +32,7 @@
     return [t.astype(BF16) for t in shifted(x, lane)]
 
 
-def conv_rows(load, weight_ref, rows, emit, silu_in=False, frames=3):
+def conv_rows(load, weight, rows, emit, silu_in=False, frames=3):
     def pair(p):
         sides = []
         for j in range(2):
@@ -40,7 +40,7 @@
             for a in range(frames):
                 parts += taps(load(a, 2 * p + j), silu_in)
             sides.append(jnp.concatenate(parts, axis=0))
-        y = jnp.dot(weight_ref[...], jnp.concatenate(sides, axis=1), preferred_element_type=F32)
+        y = jnp.dot(weight, jnp.concatenate(sides, axis=1), preferred_element_type=F32)
         n, w = y.shape[0] // 3, y.shape[1] // 2
         return [[y[b * n : (b + 1) * n, j * w : (j + 1) * w] for j in range(2)] for b in range(3)]
 
@@ -72,7 +72,7 @@
         inner[r] = (act * row_mask(pos[0] - 2, r, pos[1])).astype(BF16)
         slope[r] = (s + act * (1.0 - s)).astype(BF16)
 
-    conv_rows(lambda a, i: vol[a][i], w, n + 6, emit, silu_in=True)
+    conv_rows(lambda a, i: vol[a][i], w[...], n + 6, emit, silu_in=True)
 
 
 def grad_kernel(pos, w, slope, own, prev, nxt, grad):
@@ -83,7 +83,7 @@
         out = value * slope[r + 1].astype(F32)
         grad[r] = (out * row_mask(pos[0] - 1, r, pos[1])).astype(BF16)
 
-    conv_rows(lambda a, i: vol[a][i], w, n + 4, emit)
+    conv_rows(lambda a, i: vol[a][i], w[...], n + 4, emit)
 
 
 def video_kernel(pos, listed, w, wp, head, pool, base, own, prev, nxt, video, send, rim, sums):
@@ -94,13 +94,13 @@
         out = (base[r + 2].astype(F32) + value) * row_mask(pos[0] - 1, r, pos[1])
         rim[r] = out.astype(BF16)
 
-    conv_rows(lambda a, i: vol[a][i], w, n + 4, emit)
+    conv_rows(lambda a, i: vol[a][i], w[...], n + 4, emit)
 
     def emit_plane(r, value):
         act = value * logistic(value) * head[...]
         sums[pl.ds(r, 1)] = jnp.sum(act, axis=0, keepdims=True)
 
-    conv_rows(lambda a, i: rim[i], wp, n + 2, emit_plane, frames=1)
+    conv_rows(lambda a, i: rim[i], wp[...], n + 2, emit_plane, frames=1)
 
     def pool_row(i, _):
         a, b = rim[2 * i + 1], rim[2 * i + 2]
@@ -127,16 +127,23 @@
             ).astype(BF16)
 
 
-def input_grad_kernel(w, cot, vin, own, prev, nxt, out):
-    n = cot.shape[0]
-    vol = (prev, own, nxt)
-
+def near_kernel(w, near, own, part):
+    vol = (near, own)
+
+    def emit(r, value):
+        part[r] = value
+
+    conv_rows(lambda a, i: vol[a][i], w[:, : 2 * w.shape[1] // 3], own.shape[0], emit, frames=2)
+
+
+def input_grad_kernel(w, cot, vin, part, far, out):
     def emit(r, value):
         x = vin[r].astype(F32)
         s = logistic(x)
-        out[r] = (cot[r].astype(F32) + value * (s * (1.0 + x * (1.0 - s)))).astype(BF16)
-
-    conv_rows(lambda a, i: vol[a][i], w, n + 2, emit)
+        grad = (part[r] + value) * (s * (1.0 + x * (1.0 - s)))
+        out[r] = (cot[r].astype(F32) + grad).astype(BF16)
+
+    conv_rows(lambda a, i: far[i], w[:, 2 * w.shape[1] // 3 :], far.shape[0], emit, frames=1)
 
 
 def time_kernel_body(pos, listed, wt, mixer, head, recv, plane, score, total):
@@ -246,7 +253,8 @@
     pos = jnp.stack([lax.axis_index("space") * n, sp * n, me]).astype(jnp.int32)
 
     def both(x):
-        return lax.ppermute(x, "tm", swap_first), lax.ppermute(x, "tm", swap_second)
+        far = lax.ppermute(x, "tm", swap_second)
+        return lax.ppermute(x, "tm", swap_first), far
 
     even = lax.axis_index("space") % 2 == 0
 
@@ -306,8 +314,11 @@
         6 * MIB,
     )(pos, listed, wb, wp, plane_row, pool, v_own, inner, in_p, in_n)
     recv = lax.all_to_all(send, "tm", split_axis=0, concat_axis=0, tiled=True)
-    input_grad = call(input_grad_kernel, rows(n), [VMEM] * 6, [], flops, 6 * MIB)(
-        wat, c, v, grad, gr_p, gr_n
+    part = call(
+        near_kernel, jax.ShapeDtypeStruct((n, ch, width), F32), [VMEM] * 3, [], flops * 2 // 3, 6 * MIB
+    )(wat, gr_p, grad)
+    input_grad = call(input_grad_kernel, rows(n), [VMEM] * 5, [], flops // 3, 6 * MIB)(
+        wat, c, v, part, gr_n
     )
     plane_scores, time_scores = call(
         time_kernel_body,

time: 124 us -> 122 us (0.984)
  waiting for transfers between devices: 49.5 us -> 43 us
  local copies, waits for them, and re-layouts: 2.46 us -> 8.54 us
    unnamed x24 -> x38, local copies, waits for them, and re-layouts: 0.75 us -> 6.83 us
    ppermute x8, waiting for transfers between devices: 42.5 us -> 37.6 us  [the longest x4 37.6 us: both(): return (lax.ppermute(x, 'tm', swap_first), far)]
    all_to_all x1, waiting for transfers between devices: 3.97 us -> 2.41 us  [shards(): recv = lax.all_to_all(send, 'tm', split_axis=0, concat_axis=0, tiled=True)]
    pallas_call x1 -> x2, Pallas kernels: 5.93 us -> 7.45 us  [the longest x1 3.93 us: shards(): call(input_grad_kernel, rows(n), [VMEM] * 5, [], flops // 3, 6 * MIB)]
  transfers between devices with their start and end apart: 11 -> 11, of which waited for: 5 -> 5; matrix products, arithmetic and copies ran while one was open for 1% -> 1% of each run, Pallas kernels for 21% -> 22%
where the time goes in v5:
time: 122 us
  waiting for transfers between devices  43 us (35%)
  starting transfers between devices  39.7 us (33%)
  Pallas kernels  28 us (23%)
  local copies, waits for them, and re-layouts  8.54 us (7%)
  other arithmetic  1.39 us (1%)
    ppermute x4, waiting for transfers between devices, both(): return (lax.ppermute(x, 'tm', swap_first), far)  37.6 us
    all_to_all x1, starting transfers between devices, shards(): recv = lax.all_to_all(send, 'tm', split_axis=0, concat_axis=0, tiled=True)  17.1 us
    ppermute x4, starting transfers between devices, both(): return (lax.ppermute(x, 'tm', swap_first), far)  12.3 us
    unnamed x38, local copies, waits for them, and re-layouts  6.83 us
    pallas_call x1, Pallas kernels, shards(): call(video_kernel, (rows(n), jax.ShapeDtypeStruct((tm, ch // 2 + quarter,...  6.39 us
    pallas_call x1, Pallas kernels, shards(): call(grad_kernel, rows(n + 2), [SMEM] + [VMEM] * 5, [], flops, 6 * MIB)  5.86 us
    ppermute x4, starting transfers between devices, both(): far = lax.ppermute(x, 'tm', swap_second)  5.72 us
    pallas_call x1, Pallas kernels, shards(): call(first_kernel, (rows(n + 4), rows(n + 4)), [SMEM] + [VMEM] * 4, [], f...  5.47 us
  transfers between devices with their start and end apart: 11, of which 5 were waited for; matrix products, arithmetic and copies ran while one was open for 1% of the time, Pallas kernels for 22%

profile of v5, /device:TPU:1, one launch (start us, length us, event | category | flops | bytes accessed | tf_op | source)
XLA Modules:
  0.0 121.6 jit_solution(15339383215709894792)
XLA Ops:
  2.4 1.5 %collective-permute-start.1 = (bf16[5,64,128]{2,1,0:T(8,128)(2,1)S(1)}, bf16[5,64,128]{2,1,0:T(8,128)(2,1)S(1)}, u32[]{:S(2)}, u32[]{:S(2)}) collective-permute-start(bf16[5,64,128]{2,1,0:T(8,128)(2,1)S(1)} %pad_maximum_fusion.3), channel_id=1, source_target_pairs={{0,1},{2,3},{1,0},{3,2},{4,5},{6,7},{5,4},{7,6},{8,9},{10,11},{9,8... | collective-permute-start | bytes 245768 | tf_op jit(solution)/shard_map/ppermute | solution.py:266
  3.9 3.1 %collective-permute-start = (bf16[5,64,128]{2,1,0:T(8,128)(2,1)S(1)}, bf16[5,64,128]{2,1,0:T(8,128)(2,1)S(1)}, u32[]{:S(2)}, u32[]{:S(2)}) collective-permute-start(bf16[5,64,128]{2,1,0:T(8,128)(2,1)S(1)} %pad_maximum_fusion.2), channel_id=1, source_target_pairs={{1,2},{2,1},{5,6},{6,5},{9,10},{10,9},{13,14},{14,13},{17,18},{18,... | collective-permute-start | bytes 245768 | tf_op jit(solution)/shard_map/ppermute | solution.py:267
  7.0 3.0 %collective-permute-done = bf16[5,64,128]{2,1,0:T(8,128)(2,1)S(1)} collective-permute-done((bf16[5,64,128]{2,1,0:T(8,128)(2,1)S(1)}, bf16[5,64,128]{2,1,0:T(8,128)(2,1)S(1)}, u32[]{:S(2)}, u32[]{:S(2)}) %collective-permute-start) | collective-permute-done | bytes 81952 | tf_op jit(solution)/shard_map/ppermute | solution.py:267
  10.3 1.5 %collective-permute-start.2 = (bf16[70,64,128]{2,1,0:T(8,128)(2,1)S(1)}, bf16[70,64,128]{2,1,0:T(8,128)(2,1)}, u32[]{:S(2)}, u32[]{:S(2)}) collective-permute-start(bf16[70,64,128]{2,1,0:T(8,128)(2,1)S(1)} %pad_maximum_fusion.own.base), channel_id=1, source_target_pairs={{0,4},{8,12},{16,20},{24,28},{32,36},{40,44},{48,52},{56,60},{64,6... | collective-permute-start | bytes 3440648 | tf_op jit(solution)/shard_map/ppermute | solution.py:257
  11.7 1.7 %collective-permute-start.3 = (bf16[70,64,128]{2,1,0:T(8,128)(2,1)S(1)}, bf16[70,64,128]{2,1,0:T(8,128)(2,1)}, u32[]{:S(2)}, u32[]{:S(2)}) collective-permute-start(bf16[70,64,128]{2,1,0:T(8,128)(2,1)S(1)} %pad_maximum_fusion.own.base), channel_id=1, source_target_pairs={{4,8},{12,16},{20,24},{28,32},{36,40},{44,48},{52,56},{60,64},{68,... | collective-permute-start | bytes 3440648 | tf_op jit(solution)/shard_map/ppermute | solution.py:256
  13.5 1.1 pad_maximum_fusion.1.own
  14.6 2.5 %collective-permute-start.6 = (bf16[68,64,128]{2,1,0:T(8,128)(2,1)}, bf16[68,64,128]{2,1,0:T(8,128)(2,1)}, u32[]{:S(2)}, u32[]{:S(2)}) collective-permute-start(bf16[68,64,128]{2,1,0:T(8,128)(2,1)} %pad_maximum_fusion.1.own), channel_id=1, source_target_pairs={{0,4},{8,12},{16,20},{24,28},{32,36},{40,44},{48,52},{56,60},{64,6... | collective-permute-start | bytes 3342344 | tf_op jit(solution)/shard_map/ppermute | solution.py:257
  17.1 1.7 %collective-permute-start.7 = (bf16[68,64,128]{2,1,0:T(8,128)(2,1)}, bf16[68,64,128]{2,1,0:T(8,128)(2,1)}, u32[]{:S(2)}, u32[]{:S(2)}) collective-permute-start(bf16[68,64,128]{2,1,0:T(8,128)(2,1)} %pad_maximum_fusion.1.own), channel_id=1, source_target_pairs={{4,8},{12,16},{20,24},{28,32},{36,40},{44,48},{52,56},{60,64},{68,... | collective-permute-start | bytes 3342344 | tf_op jit(solution)/shard_map/ppermute | solution.py:256
  19.9 1.0 copy-done.3
  23.1 1.0 shard_map.129
  26.0 11.8 %collective-permute-done.2.prev = bf16[70,64,128]{2,1,0:T(8,128)(2,1)} collective-permute-done((bf16[70,64,128]{2,1,0:T(8,128)(2,1)S(1)}, bf16[70,64,128]{2,1,0:T(8,128)(2,1)}, u32[]{:S(2)}, u32[]{:S(2)}) %collective-permute-start.2) | collective-permute-done | bytes 1146912 | tf_op jit(solution)/shard_map/ppermute | solution.py:257
  37.8 5.5 %shard_map.130 = (bf16[68,64,128]{2,1,0:T(8,128)(2,1)S(1)}, bf16[68,64,128]{2,1,0:T(8,128)(2,1)S(1)}) custom-call(s32[3]{0:T(128)S(1)} %pad_add_fusion.pos, bf16[192,576]{1,0:T(8,128)(2,1)S(1)} %get-tuple-element.28.w, bf16[70,64,128]{2,1,0:T(8,128)(2,1)S(1)} %pad_maximum_fusion.own.base, bf16[70,64,128]{2,1,0:T(8,128)(2,1)} %collective-permute-done.2.prev, ...), custom_call_target="tpu_custom_call" | custom-call | flops 1811939328 | bytes 6291456 | tf_op jit(solution)/shard_map/pallas_call | solution.py:295
  43.3 4.2 %collective-permute-start.4 = (bf16[68,64,128]{2,1,0:T(8,128)(2,1)S(1)}, bf16[68,64,128]{2,1,0:T(8,128)(2,1)S(1)}, u32[]{:S(2)}, u32[]{:S(2)}) collective-permute-start(bf16[68,64,128]{2,1,0:T(8,128)(2,1)S(1)} %get-tuple-element.29.own), channel_id=1, source_target_pairs={{0,4},{8,12},{16,20},{24,28},{32,36},{40,44},{48,52},{56,60},{64,6... | collective-permute-start | bytes 3342344 | tf_op jit(solution)/shard_map/ppermute | solution.py:257
  48.2 13.4 %collective-permute-done.6.prev = bf16[68,64,128]{2,1,0:T(8,128)(2,1)} collective-permute-done((bf16[68,64,128]{2,1,0:T(8,128)(2,1)}, bf16[68,64,128]{2,1,0:T(8,128)(2,1)}, u32[]{:S(2)}, u32[]{:S(2)}) %collective-permute-start.6) | collective-permute-done | bytes 1114144 | tf_op jit(solution)/shard_map/ppermute | solution.py:257
  61.6 5.9 %shard_map.132.own = bf16[66,64,128]{2,1,0:T(8,128)(2,1)} custom-call(s32[3]{0:T(128)S(1)} %pad_add_fusion.pos, bf16[192,576]{1,0:T(8,128)(2,1)S(1)} %get-tuple-element.32.w, bf16[68,64,128]{2,1,0:T(8,128)(2,1)S(1)} %get-tuple-element.33.slope, bf16[68,64,128]{2,1,0:T(8,128)(2,1)} %pad_maximum_fusion.1.own, ...), custom_call_target="tpu_custom_call" | custom-call | flops 1811939328 | bytes 6291456 | tf_op jit(solution)/shard_map/pallas_call | solution.py:299
  67.4 4.1 %collective-permute-start.8 = (bf16[66,64,128]{2,1,0:T(8,128)(2,1)}, bf16[66,64,128]{2,1,0:T(8,128)(2,1)}, u32[]{:S(2)}, u32[]{:S(2)}) collective-permute-start(bf16[66,64,128]{2,1,0:T(8,128)(2,1)} %shard_map.132.own), channel_id=1, source_target_pairs={{0,4},{8,12},{16,20},{24,28},{32,36},{40,44},{48,52},{56,60},{64,6... | collective-permute-start | bytes 3244040 | tf_op jit(solution)/shard_map/ppermute | solution.py:257
  71.5 1.6 %collective-permute-start.9 = (bf16[66,64,128]{2,1,0:T(8,128)(2,1)}, bf16[66,64,128]{2,1,0:T(8,128)(2,1)}, u32[]{:S(2)}, u32[]{:S(2)}) collective-permute-start(bf16[66,64,128]{2,1,0:T(8,128)(2,1)} %shard_map.132.own), channel_id=1, source_target_pairs={{4,8},{12,16},{20,24},{28,32},{36,40},{44,48},{52,56},{60,64},{68,... | collective-permute-start | bytes 3244040 | tf_op jit(solution)/shard_map/ppermute | solution.py:256
  73.2 12.4 %collective-permute-done.4.prev = bf16[68,64,128]{2,1,0:T(8,128)(2,1)S(1)} collective-permute-done((bf16[68,64,128]{2,1,0:T(8,128)(2,1)S(1)}, bf16[68,64,128]{2,1,0:T(8,128)(2,1)S(1)}, u32[]{:S(2)}, u32[]{:S(2)}) %collective-permute-start.4) | collective-permute-done | bytes 1114144 | tf_op jit(solution)/shard_map/ppermute | solution.py:257
  85.6 6.4 %shard_map.131 = (bf16[64,64,128]{2,1,0:T(8,128)(2,1)}, bf16[32,48,128]{2,1,0:T(8,128)(2,1)S(1)}) custom-call(s32[3]{0:T(128)S(1)} %pad_add_fusion.pos, s32[8]{0:T(128)S(1)} %copy-done.18, bf16[192,576]{1,0:T(8,128)(2,1)S(1)} %get-tuple-element.24.w, bf16[192,192]{1,0:T(8,128)(2,1)S(1)} %get-tuple-element.25.wp, f32[64,128]{1,0:T(8,128)S(1)} %get-tuple-element.26.head, ...), custom_call_target="tpu_custom_call" | custom-call | flops 2415919104 | bytes 6291456 | tf_op jit(solution)/shard_map/pallas_call | solution.py:305
  92.7 17.1 %all-to-all-start = ((bf16[32,48,128]{2,1,0:T(8,128)(2,1)}), bf16[32,48,128]{2,1,0:T(8,128)(2,1)S(1)}, u32[]{:S(2)}, u32[]{:S(2)}) async-start(bf16[32,48,128]{2,1,0:T(8,128)(2,1)} %copy-done.4), calls=%async_computation | async-start | bytes 786432 | tf_op jit(solution)/shard_map/all_to_all | solution.py:316
  109.8 3.5 %shard_map.133.part = f32[64,64,128]{2,1,0:T(8,128)S(1)} custom-call(bf16[192,576]{1,0:T(8,128)(2,1)S(1)} %get-tuple-element.31.w, bf16[66,64,128]{2,1,0:T(8,128)(2,1)} %collective-permute-done.8.near, bf16[66,64,128]{2,1,0:T(8,128)(2,1)} %shard_map.132.own), custom_call_target="tpu_custom_call" | custom-call | flops 1207959552 | bytes 6291456 | tf_op jit(solution)/shard_map/pallas_call | solution.py:317
  113.4 3.9 %shard_map.134 = bf16[64,64,128]{2,1,0:T(8,128)(2,1)} custom-call(bf16[192,576]{1,0:T(8,128)(2,1)S(1)} %get-tuple-element.31.w, bf16[64,64,128]{2,1,0:T(8,128)(2,1)S(1)} %bitcast.21, bf16[64,64,128]{2,1,0:T(8,128)(2,1)S(1)} %bitcast.19, f32[64,64,128]{2,1,0:T(8,128)S(1)} %shard_map.133.part, bf16[66,64,128]{2,1,0:T(8,128)(2,1)} %collective-permute-done.9.far), custom_call_target="tpu_custom_call" | custom-call | flops 603979776 | bytes 6291456 | tf_op jit(solution)/shard_map/pallas_call | solution.py:320
  117.3 2.4 %all-to-all-done.recv = bf16[32,48,128]{2,1,0:T(8,128)(2,1)S(1)} async-done(((bf16[32,48,128]{2,1,0:T(8,128)(2,1)}), bf16[32,48,128]{2,1,0:T(8,128)(2,1)S(1)}, u32[]{:S(2)}, u32[]{:S(2)}) %all-to-all-start) | async-done | bytes 393248 | tf_op jit(solution)/shard_map/all_to_all | solution.py:316
  119.8 1.8 %shard_map.135 = (f32[16,128]{1,0:T(8,128)}, f32[1,64]{1,0:T(1,128)}) custom-call(s32[3]{0:T(128)S(1)} %copy-done.15, s32[8]{0:T(128)S(1)} %copy-done.18, bf16[128,96]{1,0:T(8,128)(2,1)S(1)} %copy-done.8, bf16[64,64]{1,0:T(8,128)(2,1)S(1)} %copy-done.13, f32[64,128]{1,0:T(8,128)S(1)} %copy-done.10, bf16[32,48,128]{2,1,0:T(8,128)(2,1)S(1)} %all-to-all-done.recv), custom_call_target="tpu_custom_call" | custom-call | flops 90596968 | bytes 1048576 | tf_op jit(solution)/shard_map/pallas_call | solution.py:323
  (55 shorter events, 8.5 us)
Async XLA Ops:
  0.6 9.5 %copy-start = (bf16[1,64,64,128]{3,2,1,0:T(8,128)(2,1)S(1)}, bf16[1,64,64,128]{3,2,1,0:T(8,128)(2,1)}, u32[]{:S(2)}) copy-start(bf16[1,64,64,128]{3,2,1,0:T(8,128)(2,1)} %param.10) | copy-start | bytes 3145732
  2.4 4.6 %collective-permute-start.1 = (bf16[5,64,128]{2,1,0:T(8,128)(2,1)S(1)}, bf16[5,64,128]{2,1,0:T(8,128)(2,1)S(1)}, u32[]{:S(2)}, u32[]{:S(2)}) collective-permute-start(bf16[5,64,128]{2,1,0:T(8,128)(2,1)S(1)} %pad_maximum_fusion.3), channel_id=1, source_target_pairs={{0,1},{2,3},{1,0},{3,2},{4,5},{6,7},{5,4},{7,6},{8,9},{10,11},{9,8... | collective-permute-start | bytes 245768 | tf_op jit(solution)/shard_map/ppermute | solution.py:266
  3.9 6.2 %collective-permute-start = (bf16[5,64,128]{2,1,0:T(8,128)(2,1)S(1)}, bf16[5,64,128]{2,1,0:T(8,128)(2,1)S(1)}, u32[]{:S(2)}, u32[]{:S(2)}) collective-permute-start(bf16[5,64,128]{2,1,0:T(8,128)(2,1)S(1)} %pad_maximum_fusion.2), channel_id=1, source_target_pairs={{1,2},{2,1},{5,6},{6,5},{9,10},{10,9},{13,14},{14,13},{17,18},{18,... | collective-permute-start | bytes 245768 | tf_op jit(solution)/shard_map/ppermute | solution.py:267
  10.1 3.3 %copy-start.1 = (bf16[1,64,64,128]{3,2,1,0:T(8,128)(2,1)S(1)}, bf16[1,64,64,128]{3,2,1,0:T(8,128)(2,1)}, u32[]{:S(2)}) copy-start(bf16[1,64,64,128]{3,2,1,0:T(8,128)(2,1)} %param.11) | copy-start | bytes 3145732
  10.3 27.5 %collective-permute-start.2 = (bf16[70,64,128]{2,1,0:T(8,128)(2,1)S(1)}, bf16[70,64,128]{2,1,0:T(8,128)(2,1)}, u32[]{:S(2)}, u32[]{:S(2)}) collective-permute-start(bf16[70,64,128]{2,1,0:T(8,128)(2,1)S(1)} %pad_maximum_fusion.own.base), channel_id=1, source_target_pairs={{0,4},{8,12},{16,20},{24,28},{32,36},{40,44},{48,52},{56,60},{64,6... | collective-permute-start | bytes 3440648 | tf_op jit(solution)/shard_map/ppermute | solution.py:257
  11.7 26.1 %collective-permute-start.3 = (bf16[70,64,128]{2,1,0:T(8,128)(2,1)S(1)}, bf16[70,64,128]{2,1,0:T(8,128)(2,1)}, u32[]{:S(2)}, u32[]{:S(2)}) collective-permute-start(bf16[70,64,128]{2,1,0:T(8,128)(2,1)S(1)} %pad_maximum_fusion.own.base), channel_id=1, source_target_pairs={{4,8},{12,16},{20,24},{28,32},{36,40},{44,48},{52,56},{60,64},{68,... | collective-permute-start | bytes 3440648 | tf_op jit(solution)/shard_map/ppermute | solution.py:256
  13.4 5.5 %copy-start.6 = (bf16[3,64,64]{2,1,0:T(8,128)(2,1)S(1)}, bf16[3,64,64]{2,1,0:T(8,128)(2,1)}, u32[]{:S(2)}) copy-start(bf16[3,64,64]{2,1,0:T(8,128)(2,1)} %kt.1) | copy-start | bytes 73732
  13.4 5.5 %copy-start.11 = (bf16[64,64]{1,0:T(8,128)(2,1)S(1)}, bf16[64,64]{1,0:T(8,128)(2,1)}, u32[]{:S(2)}) copy-start(bf16[64,64]{1,0:T(8,128)(2,1)} %km.1) | copy-start | bytes 24580
  14.6 47.0 %collective-permute-start.6 = (bf16[68,64,128]{2,1,0:T(8,128)(2,1)}, bf16[68,64,128]{2,1,0:T(8,128)(2,1)}, u32[]{:S(2)}, u32[]{:S(2)}) collective-permute-start(bf16[68,64,128]{2,1,0:T(8,128)(2,1)} %pad_maximum_fusion.1.own), channel_id=1, source_target_pairs={{0,4},{8,12},{16,20},{24,28},{32,36},{40,44},{48,52},{56,60},{64,6... | collective-permute-start | bytes 3342344 | tf_op jit(solution)/shard_map/ppermute | solution.py:257
  17.1 44.5 %collective-permute-start.7 = (bf16[68,64,128]{2,1,0:T(8,128)(2,1)}, bf16[68,64,128]{2,1,0:T(8,128)(2,1)}, u32[]{:S(2)}, u32[]{:S(2)}) collective-permute-start(bf16[68,64,128]{2,1,0:T(8,128)(2,1)} %pad_maximum_fusion.1.own), channel_id=1, source_target_pairs={{4,8},{12,16},{20,24},{28,32},{36,40},{44,48},{52,56},{60,64},{68,... | collective-permute-start | bytes 3342344 | tf_op jit(solution)/shard_map/ppermute | solution.py:256
  18.9 66.7 %copy-start.14 = (s32[3]{0:T(128)}, s32[3]{0:T(128)S(1)}, u32[]{:S(2)}) copy-start(s32[3]{0:T(128)S(1)} %pad_add_fusion.pos) | copy-start | bytes 40
  18.9 1.0 copy-start.2
  19.9 1.0 copy-start.3
  20.9 0.9 copy-start.5
  43.3 42.3 %collective-permute-start.4 = (bf16[68,64,128]{2,1,0:T(8,128)(2,1)S(1)}, bf16[68,64,128]{2,1,0:T(8,128)(2,1)S(1)}, u32[]{:S(2)}, u32[]{:S(2)}) collective-permute-start(bf16[68,64,128]{2,1,0:T(8,128)(2,1)S(1)} %get-tuple-element.29.own), channel_id=1, source_target_pairs={{0,4},{8,12},{16,20},{24,28},{32,36},{40,44},{48,52},{56,60},{64,6... | collective-permute-start | bytes 3342344 | tf_op jit(solution)/shard_map/ppermute | solution.py:257
  47.5 38.1 %collective-permute-start.5 = (bf16[68,64,128]{2,1,0:T(8,128)(2,1)S(1)}, bf16[68,64,128]{2,1,0:T(8,128)(2,1)S(1)}, u32[]{:S(2)}, u32[]{:S(2)}) collective-permute-start(bf16[68,64,128]{2,1,0:T(8,128)(2,1)S(1)} %get-tuple-element.29.own), channel_id=1, source_target_pairs={{4,8},{12,16},{20,24},{28,32},{36,40},{44,48},{52,56},{60,64},{68,... | collective-permute-start | bytes 3342344 | tf_op jit(solution)/shard_map/ppermute | solution.py:256
  61.6 24.0 %copy-start.18 = (s32[8]{0:T(128)S(1)}, s32[8]{0:T(128)}, u32[]{:S(2)}) copy-start(s32[8]{0:T(128)} %listed.3) | copy-start | bytes 100
  67.4 42.4 %collective-permute-start.8 = (bf16[66,64,128]{2,1,0:T(8,128)(2,1)}, bf16[66,64,128]{2,1,0:T(8,128)(2,1)}, u32[]{:S(2)}, u32[]{:S(2)}) collective-permute-start(bf16[66,64,128]{2,1,0:T(8,128)(2,1)} %shard_map.132.own), channel_id=1, source_target_pairs={{0,4},{8,12},{16,20},{24,28},{32,36},{40,44},{48,52},{56,60},{64,6... | collective-permute-start | bytes 3244040 | tf_op jit(solution)/shard_map/ppermute | solution.py:257
  71.5 41.9 %collective-permute-start.9 = (bf16[66,64,128]{2,1,0:T(8,128)(2,1)}, bf16[66,64,128]{2,1,0:T(8,128)(2,1)}, u32[]{:S(2)}, u32[]{:S(2)}) collective-permute-start(bf16[66,64,128]{2,1,0:T(8,128)(2,1)} %shard_map.132.own), channel_id=1, source_target_pairs={{4,8},{12,16},{20,24},{28,32},{36,40},{44,48},{52,56},{60,64},{68,... | collective-permute-start | bytes 3244040 | tf_op jit(solution)/shard_map/ppermute | solution.py:256
  92.7 27.1 %all-to-all-start = ((bf16[32,48,128]{2,1,0:T(8,128)(2,1)}), bf16[32,48,128]{2,1,0:T(8,128)(2,1)S(1)}, u32[]{:S(2)}, u32[]{:S(2)}) async-start(bf16[32,48,128]{2,1,0:T(8,128)(2,1)} %copy-done.4), calls=%async_computation | async-start | bytes 786432 | tf_op jit(solution)/shard_map/all_to_all | solution.py:316
  113.4 6.4 %copy-start.8 = (bf16[128,96]{1,0:T(8,128)(2,1)S(1)}, bf16[128,96]{1,0:T(8,128)(2,1)}, u32[]{:S(2)}) copy-start(bf16[128,96]{1,0:T(8,128)(2,1)} %copy-done.7) | copy-start | bytes 73732
  113.4 6.4 %copy-start.10 = (f32[64,128]{1,0:T(8,128)S(1)}, f32[64,128]{1,0:T(8,128)}, u32[]{:S(2)}) copy-start(f32[64,128]{1,0:T(8,128)} %copy-done.9) | copy-start | bytes 98308
  113.4 6.4 %copy-start.13 = (bf16[64,64]{1,0:T(8,128)(2,1)S(1)}, bf16[64,64]{1,0:T(8,128)(2,1)}, u32[]{:S(2)}) copy-start(bf16[64,64]{1,0:T(8,128)(2,1)} %copy-done.12) | copy-start | bytes 24580
  113.4 6.4 %copy-start.15 = (s32[3]{0:T(128)S(1)}, s32[3]{0:T(128)}, u32[]{:S(2)}) copy-start(s32[3]{0:T(128)} %copy-done.14) | copy-start | bytes 40
  (6 other events, 3.9 us)

commit v6 on v5

--- a/solution.py
+++ b/solution.py
@@ -25,11 +25,11 @@
 
 
 def taps(x, silu_in):
-    x = x.astype(F32)
     lane = lax.broadcasted_iota(jnp.int32, x.shape, 1)
     if silu_in:
-        x = x * logistic(x)
-    return [t.astype(BF16) for t in shifted(x, lane)]
+        x = x.astype(F32)
+        x = (x * logistic(x)).astype(BF16)
+    return list(shifted(x, lane))
 
 
 def conv_rows(load, weight, rows, emit, silu_in=False, frames=3):
@@ -146,12 +146,12 @@
     conv_rows(lambda a, i: far[i], w[:, 2 * w.shape[1] // 3 :], far.shape[0], emit, frames=1)
 
 
-def time_kernel_body(pos, listed, wt, mixer, head, recv, plane, score, total):
+def time_kernel_body(pos, listed, wt, mixer, head, recv, plane, score):
     frames = recv.shape[0]
     half, width = wt.shape[1] // 3, recv.shape[2]
     units = wt.shape[0] // 2
     plane[...] = recv[listed[pos[2] // (frames // LISTED)], pl.ds(half, plane.shape[0])].astype(F32)
-    total[...] = jnp.zeros_like(total)
+    total = jnp.zeros((units, width), F32)
     lane = lax.broadcasted_iota(jnp.int32, (units, width), 1)
 
     def piece(t):
@@ -169,16 +169,15 @@
         left = a[:units] + pltpu.roll(a[units:], width // 2, 1)
         right = pltpu.roll(b[:units], width // 2, 1) + b[units:]
         q = jnp.where(lane < width // 2, left, right)
-        total[...] += q * logistic(q)
-
-    both = total[...]
-    mean = (both + pltpu.roll(both, width // 2, 1)) * (1.0 / frames)
-    mixed = jnp.zeros_like(mean)
-    rest = mean
+        total = total + q * logistic(q)
+
+    mean = (total + pltpu.roll(total, width // 2, 1)) * (1.0 / frames)
+    parts, rest = [], mean
     for _ in range(3):
-        top = rest.astype(BF16)
-        mixed = mixed + jnp.dot(mixer[...], top, preferred_element_type=F32)
-        rest = rest - top.astype(F32)
+        parts.append(rest.astype(BF16))
+        rest = rest - parts[-1].astype(F32)
+    mixers = jnp.concatenate([mixer[...]] * 3, axis=1)
+    mixed = jnp.dot(mixers, jnp.concatenate(parts, axis=0), preferred_element_type=F32)
     act = mixed * logistic(mixed) * head[...]
     score[...] = jnp.sum(act, axis=0, keepdims=True)[:, : width // 2]
 
@@ -324,7 +323,7 @@
         time_kernel_body,
         (jax.ShapeDtypeStruct((quarter, width), F32), jax.ShapeDtypeStruct((1, width // 2), F32)),
         [SMEM, SMEM, VMEM, VMEM, VMEM, VMEM],
-        [pltpu.VMEM((ch, width), F32)],
+        [],
         flops // 20,
         MIB,
     )(pos, listed, wt, mixer, time_row, recv)

time: 122 us -> 122 us (level)
  transfers between devices with their start and end apart: 11 -> 11, of which waited for: 5 -> 5; matrix products, arithmetic and copies ran while one was open for 1% -> 1% of each run, Pallas kernels for 22% -> 21%
where the time goes in v6:
time: 122 us; the launch traced here: 121 us
  waiting for transfers between devices  44.1 us (36%)
  starting transfers between devices  39.7 us (33%)
  Pallas kernels  26.8 us (22%)
  local copies, waits for them, and re-layouts  8.54 us (7%)
  other arithmetic  1.39 us (1%)
    ppermute x4, waiting for transfers between devices, both(): return (lax.ppermute(x, 'tm', swap_first), far)  38.4 us
    all_to_all x1, starting transfers between devices, shards(): recv = lax.all_to_all(send, 'tm', split_axis=0, concat_axis=0, tiled=True)  17.1 us
    ppermute x4, starting transfers between devices, both(): return (lax.ppermute(x, 'tm', swap_first), far)  12.3 us
    unnamed x38, local copies, waits for them, and re-layouts  6.83 us
    pallas_call x1, Pallas kernels, shards(): call(video_kernel, (rows(n), jax.ShapeDtypeStruct((tm, ch // 2 + quarter,...  6.22 us
    pallas_call x1, Pallas kernels, shards(): call(grad_kernel, rows(n + 2), [SMEM] + [VMEM] * 5, [], flops, 6 * MIB)  5.84 us
    ppermute x4, starting transfers between devices, both(): far = lax.ppermute(x, 'tm', swap_second)  5.72 us
    pallas_call x1, Pallas kernels, shards(): call(first_kernel, (rows(n + 4), rows(n + 4)), [SMEM] + [VMEM] * 4, [], f...  4.67 us
  transfers between devices with their start and end apart: 11, of which 5 were waited for; matrix products, arithmetic and copies ran while one was open for 1% of the time, Pallas kernels for 21%

profile of v6, /device:TPU:1, one launch (start us, length us, event | category | flops | bytes accessed | tf_op | source)
XLA Modules:
  0.0 121.5 jit_solution(18271281671397310721)
XLA Ops:
  2.4 1.5 %collective-permute-start.1 = (bf16[5,64,128]{2,1,0:T(8,128)(2,1)S(1)}, bf16[5,64,128]{2,1,0:T(8,128)(2,1)S(1)}, u32[]{:S(2)}, u32[]{:S(2)}) collective-permute-start(bf16[5,64,128]{2,1,0:T(8,128)(2,1)S(1)} %pad_maximum_fusion.3), channel_id=1, source_target_pairs={{0,1},{2,3},{1,0},{3,2},{4,5},{6,7},{5,4},{7,6},{8,9},{10,11},{9,8... | collective-permute-start | bytes 245768 | tf_op jit(solution)/shard_map/ppermute | solution.py:265
  3.9 3.1 %collective-permute-start = (bf16[5,64,128]{2,1,0:T(8,128)(2,1)S(1)}, bf16[5,64,128]{2,1,0:T(8,128)(2,1)S(1)}, u32[]{:S(2)}, u32[]{:S(2)}) collective-permute-start(bf16[5,64,128]{2,1,0:T(8,128)(2,1)S(1)} %pad_maximum_fusion.2), channel_id=1, source_target_pairs={{1,2},{2,1},{5,6},{6,5},{9,10},{10,9},{13,14},{14,13},{17,18},{18,... | collective-permute-start | bytes 245768 | tf_op jit(solution)/shard_map/ppermute | solution.py:266
  7.0 3.0 %collective-permute-done = bf16[5,64,128]{2,1,0:T(8,128)(2,1)S(1)} collective-permute-done((bf16[5,64,128]{2,1,0:T(8,128)(2,1)S(1)}, bf16[5,64,128]{2,1,0:T(8,128)(2,1)S(1)}, u32[]{:S(2)}, u32[]{:S(2)}) %collective-permute-start) | collective-permute-done | bytes 81952 | tf_op jit(solution)/shard_map/ppermute | solution.py:266
  10.3 1.5 %collective-permute-start.2 = (bf16[70,64,128]{2,1,0:T(8,128)(2,1)S(1)}, bf16[70,64,128]{2,1,0:T(8,128)(2,1)}, u32[]{:S(2)}, u32[]{:S(2)}) collective-permute-start(bf16[70,64,128]{2,1,0:T(8,128)(2,1)S(1)} %pad_maximum_fusion.own.base), channel_id=1, source_target_pairs={{0,4},{8,12},{16,20},{24,28},{32,36},{40,44},{48,52},{56,60},{64,6... | collective-permute-start | bytes 3440648 | tf_op jit(solution)/shard_map/ppermute | solution.py:256
  11.7 1.7 %collective-permute-start.3 = (bf16[70,64,128]{2,1,0:T(8,128)(2,1)S(1)}, bf16[70,64,128]{2,1,0:T(8,128)(2,1)}, u32[]{:S(2)}, u32[]{:S(2)}) collective-permute-start(bf16[70,64,128]{2,1,0:T(8,128)(2,1)S(1)} %pad_maximum_fusion.own.base), channel_id=1, source_target_pairs={{4,8},{12,16},{20,24},{28,32},{36,40},{44,48},{52,56},{60,64},{68,... | collective-permute-start | bytes 3440648 | tf_op jit(solution)/shard_map/ppermute | solution.py:255
  13.5 1.1 pad_maximum_fusion.1.own
  14.6 2.5 %collective-permute-start.6 = (bf16[68,64,128]{2,1,0:T(8,128)(2,1)}, bf16[68,64,128]{2,1,0:T(8,128)(2,1)}, u32[]{:S(2)}, u32[]{:S(2)}) collective-permute-start(bf16[68,64,128]{2,1,0:T(8,128)(2,1)} %pad_maximum_fusion.1.own), channel_id=1, source_target_pairs={{0,4},{8,12},{16,20},{24,28},{32,36},{40,44},{48,52},{56,60},{64,6... | collective-permute-start | bytes 3342344 | tf_op jit(solution)/shard_map/ppermute | solution.py:256
  17.1 1.7 %collective-permute-start.7 = (bf16[68,64,128]{2,1,0:T(8,128)(2,1)}, bf16[68,64,128]{2,1,0:T(8,128)(2,1)}, u32[]{:S(2)}, u32[]{:S(2)}) collective-permute-start(bf16[68,64,128]{2,1,0:T(8,128)(2,1)} %pad_maximum_fusion.1.own), channel_id=1, source_target_pairs={{4,8},{12,16},{20,24},{28,32},{36,40},{44,48},{52,56},{60,64},{68,... | collective-permute-start | bytes 3342344 | tf_op jit(solution)/shard_map/ppermute | solution.py:255
  19.9 1.0 copy-done.3
  23.1 1.0 shard_map.129
  26.0 11.8 %collective-permute-done.2.prev = bf16[70,64,128]{2,1,0:T(8,128)(2,1)} collective-permute-done((bf16[70,64,128]{2,1,0:T(8,128)(2,1)S(1)}, bf16[70,64,128]{2,1,0:T(8,128)(2,1)}, u32[]{:S(2)}, u32[]{:S(2)}) %collective-permute-start.2) | collective-permute-done | bytes 1146912 | tf_op jit(solution)/shard_map/ppermute | solution.py:256
  37.8 4.7 %shard_map.130 = (bf16[68,64,128]{2,1,0:T(8,128)(2,1)S(1)}, bf16[68,64,128]{2,1,0:T(8,128)(2,1)S(1)}) custom-call(s32[3]{0:T(128)S(1)} %pad_add_fusion.pos, bf16[192,576]{1,0:T(8,128)(2,1)S(1)} %get-tuple-element.28.w, bf16[70,64,128]{2,1,0:T(8,128)(2,1)S(1)} %pad_maximum_fusion.own.base, bf16[70,64,128]{2,1,0:T(8,128)(2,1)} %collective-permute-done.2.prev, ...), custom_call_target="tpu_custom_call" | custom-call | flops 1811939328 | bytes 6291456 | tf_op jit(solution)/shard_map/pallas_call | solution.py:294
  42.5 4.2 %collective-permute-start.4 = (bf16[68,64,128]{2,1,0:T(8,128)(2,1)S(1)}, bf16[68,64,128]{2,1,0:T(8,128)(2,1)S(1)}, u32[]{:S(2)}, u32[]{:S(2)}) collective-permute-start(bf16[68,64,128]{2,1,0:T(8,128)(2,1)S(1)} %get-tuple-element.29.own), channel_id=1, source_target_pairs={{0,4},{8,12},{16,20},{24,28},{32,36},{40,44},{48,52},{56,60},{64,6... | collective-permute-start | bytes 3342344 | tf_op jit(solution)/shard_map/ppermute | solution.py:256
  47.4 14.2 %collective-permute-done.6.prev = bf16[68,64,128]{2,1,0:T(8,128)(2,1)} collective-permute-done((bf16[68,64,128]{2,1,0:T(8,128)(2,1)}, bf16[68,64,128]{2,1,0:T(8,128)(2,1)}, u32[]{:S(2)}, u32[]{:S(2)}) %collective-permute-start.6) | collective-permute-done | bytes 1114144 | tf_op jit(solution)/shard_map/ppermute | solution.py:256
  61.6 5.8 %shard_map.132.own = bf16[66,64,128]{2,1,0:T(8,128)(2,1)} custom-call(s32[3]{0:T(128)S(1)} %pad_add_fusion.pos, bf16[192,576]{1,0:T(8,128)(2,1)S(1)} %get-tuple-element.32.w, bf16[68,64,128]{2,1,0:T(8,128)(2,1)S(1)} %get-tuple-element.33.slope, bf16[68,64,128]{2,1,0:T(8,128)(2,1)} %pad_maximum_fusion.1.own, ...), custom_call_target="tpu_custom_call" | custom-call | flops 1811939328 | bytes 6291456 | tf_op jit(solution)/shard_map/pallas_call | solution.py:298
  67.4 4.1 %collective-permute-start.8 = (bf16[66,64,128]{2,1,0:T(8,128)(2,1)}, bf16[66,64,128]{2,1,0:T(8,128)(2,1)}, u32[]{:S(2)}, u32[]{:S(2)}) collective-permute-start(bf16[66,64,128]{2,1,0:T(8,128)(2,1)} %shard_map.132.own), channel_id=1, source_target_pairs={{0,4},{8,12},{16,20},{24,28},{32,36},{40,44},{48,52},{56,60},{64,6... | collective-permute-start | bytes 3244040 | tf_op jit(solution)/shard_map/ppermute | solution.py:256
  71.5 1.6 %collective-permute-start.9 = (bf16[66,64,128]{2,1,0:T(8,128)(2,1)}, bf16[66,64,128]{2,1,0:T(8,128)(2,1)}, u32[]{:S(2)}, u32[]{:S(2)}) collective-permute-start(bf16[66,64,128]{2,1,0:T(8,128)(2,1)} %shard_map.132.own), channel_id=1, source_target_pairs={{4,8},{12,16},{20,24},{28,32},{36,40},{44,48},{52,56},{60,64},{68,... | collective-permute-start | bytes 3244040 | tf_op jit(solution)/shard_map/ppermute | solution.py:255
  73.2 12.4 %collective-permute-done.4.prev = bf16[68,64,128]{2,1,0:T(8,128)(2,1)S(1)} collective-permute-done((bf16[68,64,128]{2,1,0:T(8,128)(2,1)S(1)}, bf16[68,64,128]{2,1,0:T(8,128)(2,1)S(1)}, u32[]{:S(2)}, u32[]{:S(2)}) %collective-permute-start.4) | collective-permute-done | bytes 1114144 | tf_op jit(solution)/shard_map/ppermute | solution.py:256
  85.6 6.2 %shard_map.131 = (bf16[64,64,128]{2,1,0:T(8,128)(2,1)}, bf16[32,48,128]{2,1,0:T(8,128)(2,1)S(1)}) custom-call(s32[3]{0:T(128)S(1)} %pad_add_fusion.pos, s32[8]{0:T(128)S(1)} %copy-done.18, bf16[192,576]{1,0:T(8,128)(2,1)S(1)} %get-tuple-element.24.w, bf16[192,192]{1,0:T(8,128)(2,1)S(1)} %get-tuple-element.25.wp, f32[64,128]{1,0:T(8,128)S(1)} %get-tuple-element.26.head, ...), custom_call_target="tpu_custom_call" | custom-call | flops 2415919104 | bytes 6291456 | tf_op jit(solution)/shard_map/pallas_call | solution.py:304
  92.5 17.1 %all-to-all-start = ((bf16[32,48,128]{2,1,0:T(8,128)(2,1)}), bf16[32,48,128]{2,1,0:T(8,128)(2,1)S(1)}, u32[]{:S(2)}, u32[]{:S(2)}) async-start(bf16[32,48,128]{2,1,0:T(8,128)(2,1)} %copy-done.4), calls=%async_computation | async-start | bytes 786432 | tf_op jit(solution)/shard_map/all_to_all | solution.py:315
  109.7 3.5 %shard_map.133.part = f32[64,64,128]{2,1,0:T(8,128)S(1)} custom-call(bf16[192,576]{1,0:T(8,128)(2,1)S(1)} %get-tuple-element.31.w, bf16[66,64,128]{2,1,0:T(8,128)(2,1)} %collective-permute-done.8.near, bf16[66,64,128]{2,1,0:T(8,128)(2,1)} %shard_map.132.own), custom_call_target="tpu_custom_call" | custom-call | flops 1207959552 | bytes 6291456 | tf_op jit(solution)/shard_map/pallas_call | solution.py:316
  113.2 3.8 %shard_map.134 = bf16[64,64,128]{2,1,0:T(8,128)(2,1)} custom-call(bf16[192,576]{1,0:T(8,128)(2,1)S(1)} %get-tuple-element.31.w, bf16[64,64,128]{2,1,0:T(8,128)(2,1)S(1)} %bitcast.21, bf16[64,64,128]{2,1,0:T(8,128)(2,1)S(1)} %bitcast.19, f32[64,64,128]{2,1,0:T(8,128)S(1)} %shard_map.133.part, bf16[66,64,128]{2,1,0:T(8,128)(2,1)} %collective-permute-done.9.far), custom_call_target="tpu_custom_call" | custom-call | flops 603979776 | bytes 6291456 | tf_op jit(solution)/shard_map/pallas_call | solution.py:319
  117.0 2.7 %all-to-all-done.recv = bf16[32,48,128]{2,1,0:T(8,128)(2,1)S(1)} async-done(((bf16[32,48,128]{2,1,0:T(8,128)(2,1)}), bf16[32,48,128]{2,1,0:T(8,128)(2,1)S(1)}, u32[]{:S(2)}, u32[]{:S(2)}) %all-to-all-start) | async-done | bytes 393248 | tf_op jit(solution)/shard_map/all_to_all | solution.py:315
  119.7 1.8 %shard_map.135 = (f32[16,128]{1,0:T(8,128)}, f32[1,64]{1,0:T(1,128)}) custom-call(s32[3]{0:T(128)S(1)} %copy-done.15, s32[8]{0:T(128)S(1)} %copy-done.18, bf16[128,96]{1,0:T(8,128)(2,1)S(1)} %copy-done.8, bf16[64,64]{1,0:T(8,128)(2,1)S(1)} %copy-done.13, f32[64,128]{1,0:T(8,128)S(1)} %copy-done.10, bf16[32,48,128]{2,1,0:T(8,128)(2,1)S(1)} %all-to-all-done.recv), custom_call_target="tpu_custom_call" | custom-call | flops 90596968 | bytes 1048576 | tf_op jit(solution)/shard_map/pallas_call | solution.py:322
  (55 shorter events, 8.5 us)
Async XLA Ops:
  0.6 9.5 %copy-start = (bf16[1,64,64,128]{3,2,1,0:T(8,128)(2,1)S(1)}, bf16[1,64,64,128]{3,2,1,0:T(8,128)(2,1)}, u32[]{:S(2)}) copy-start(bf16[1,64,64,128]{3,2,1,0:T(8,128)(2,1)} %param.10) | copy-start | bytes 3145732
  2.4 4.6 %collective-permute-start.1 = (bf16[5,64,128]{2,1,0:T(8,128)(2,1)S(1)}, bf16[5,64,128]{2,1,0:T(8,128)(2,1)S(1)}, u32[]{:S(2)}, u32[]{:S(2)}) collective-permute-start(bf16[5,64,128]{2,1,0:T(8,128)(2,1)S(1)} %pad_maximum_fusion.3), channel_id=1, source_target_pairs={{0,1},{2,3},{1,0},{3,2},{4,5},{6,7},{5,4},{7,6},{8,9},{10,11},{9,8... | collective-permute-start | bytes 245768 | tf_op jit(solution)/shard_map/ppermute | solution.py:265
  3.9 6.2 %collective-permute-start = (bf16[5,64,128]{2,1,0:T(8,128)(2,1)S(1)}, bf16[5,64,128]{2,1,0:T(8,128)(2,1)S(1)}, u32[]{:S(2)}, u32[]{:S(2)}) collective-permute-start(bf16[5,64,128]{2,1,0:T(8,128)(2,1)S(1)} %pad_maximum_fusion.2), channel_id=1, source_target_pairs={{1,2},{2,1},{5,6},{6,5},{9,10},{10,9},{13,14},{14,13},{17,18},{18,... | collective-permute-start | bytes 245768 | tf_op jit(solution)/shard_map/ppermute | solution.py:266
  10.1 3.3 %copy-start.1 = (bf16[1,64,64,128]{3,2,1,0:T(8,128)(2,1)S(1)}, bf16[1,64,64,128]{3,2,1,0:T(8,128)(2,1)}, u32[]{:S(2)}) copy-start(bf16[1,64,64,128]{3,2,1,0:T(8,128)(2,1)} %param.11) | copy-start | bytes 3145732
  10.3 27.5 %collective-permute-start.2 = (bf16[70,64,128]{2,1,0:T(8,128)(2,1)S(1)}, bf16[70,64,128]{2,1,0:T(8,128)(2,1)}, u32[]{:S(2)}, u32[]{:S(2)}) collective-permute-start(bf16[70,64,128]{2,1,0:T(8,128)(2,1)S(1)} %pad_maximum_fusion.own.base), channel_id=1, source_target_pairs={{0,4},{8,12},{16,20},{24,28},{32,36},{40,44},{48,52},{56,60},{64,6... | collective-permute-start | bytes 3440648 | tf_op jit(solution)/shard_map/ppermute | solution.py:256
  11.7 26.1 %collective-permute-start.3 = (bf16[70,64,128]{2,1,0:T(8,128)(2,1)S(1)}, bf16[70,64,128]{2,1,0:T(8,128)(2,1)}, u32[]{:S(2)}, u32[]{:S(2)}) collective-permute-start(bf16[70,64,128]{2,1,0:T(8,128)(2,1)S(1)} %pad_maximum_fusion.own.base), channel_id=1, source_target_pairs={{4,8},{12,16},{20,24},{28,32},{36,40},{44,48},{52,56},{60,64},{68,... | collective-permute-start | bytes 3440648 | tf_op jit(solution)/shard_map/ppermute | solution.py:255
  13.4 5.5 %copy-start.6 = (bf16[3,64,64]{2,1,0:T(8,128)(2,1)S(1)}, bf16[3,64,64]{2,1,0:T(8,128)(2,1)}, u32[]{:S(2)}) copy-start(bf16[3,64,64]{2,1,0:T(8,128)(2,1)} %kt.1) | copy-start | bytes 73732
  13.4 5.5 %copy-start.11 = (bf16[64,64]{1,0:T(8,128)(2,1)S(1)}, bf16[64,64]{1,0:T(8,128)(2,1)}, u32[]{:S(2)}) copy-start(bf16[64,64]{1,0:T(8,128)(2,1)} %km.1) | copy-start | bytes 24580
  14.6 47.0 %collective-permute-start.6 = (bf16[68,64,128]{2,1,0:T(8,128)(2,1)}, bf16[68,64,128]{2,1,0:T(8,128)(2,1)}, u32[]{:S(2)}, u32[]{:S(2)}) collective-permute-start(bf16[68,64,128]{2,1,0:T(8,128)(2,1)} %pad_maximum_fusion.1.own), channel_id=1, source_target_pairs={{0,4},{8,12},{16,20},{24,28},{32,36},{40,44},{48,52},{56,60},{64,6... | collective-permute-start | bytes 3342344 | tf_op jit(solution)/shard_map/ppermute | solution.py:256
  17.1 44.5 %collective-permute-start.7 = (bf16[68,64,128]{2,1,0:T(8,128)(2,1)}, bf16[68,64,128]{2,1,0:T(8,128)(2,1)}, u32[]{:S(2)}, u32[]{:S(2)}) collective-permute-start(bf16[68,64,128]{2,1,0:T(8,128)(2,1)} %pad_maximum_fusion.1.own), channel_id=1, source_target_pairs={{4,8},{12,16},{20,24},{28,32},{36,40},{44,48},{52,56},{60,64},{68,... | collective-permute-start | bytes 3342344 | tf_op jit(solution)/shard_map/ppermute | solution.py:255
  18.9 66.7 %copy-start.14 = (s32[3]{0:T(128)}, s32[3]{0:T(128)S(1)}, u32[]{:S(2)}) copy-start(s32[3]{0:T(128)S(1)} %pad_add_fusion.pos) | copy-start | bytes 40
  18.9 1.0 copy-start.2
  19.9 1.0 copy-start.3
  20.9 0.9 copy-start.5
  42.5 43.1 %collective-permute-start.4 = (bf16[68,64,128]{2,1,0:T(8,128)(2,1)S(1)}, bf16[68,64,128]{2,1,0:T(8,128)(2,1)S(1)}, u32[]{:S(2)}, u32[]{:S(2)}) collective-permute-start(bf16[68,64,128]{2,1,0:T(8,128)(2,1)S(1)} %get-tuple-element.29.own), channel_id=1, source_target_pairs={{0,4},{8,12},{16,20},{24,28},{32,36},{40,44},{48,52},{56,60},{64,6... | collective-permute-start | bytes 3342344 | tf_op jit(solution)/shard_map/ppermute | solution.py:256
  46.7 38.9 %collective-permute-start.5 = (bf16[68,64,128]{2,1,0:T(8,128)(2,1)S(1)}, bf16[68,64,128]{2,1,0:T(8,128)(2,1)S(1)}, u32[]{:S(2)}, u32[]{:S(2)}) collective-permute-start(bf16[68,64,128]{2,1,0:T(8,128)(2,1)S(1)} %get-tuple-element.29.own), channel_id=1, source_target_pairs={{4,8},{12,16},{20,24},{28,32},{36,40},{44,48},{52,56},{60,64},{68,... | collective-permute-start | bytes 3342344 | tf_op jit(solution)/shard_map/ppermute | solution.py:255
  61.6 24.0 %copy-start.18 = (s32[8]{0:T(128)S(1)}, s32[8]{0:T(128)}, u32[]{:S(2)}) copy-start(s32[8]{0:T(128)} %listed.3) | copy-start | bytes 100
  67.4 42.2 %collective-permute-start.8 = (bf16[66,64,128]{2,1,0:T(8,128)(2,1)}, bf16[66,64,128]{2,1,0:T(8,128)(2,1)}, u32[]{:S(2)}, u32[]{:S(2)}) collective-permute-start(bf16[66,64,128]{2,1,0:T(8,128)(2,1)} %shard_map.132.own), channel_id=1, source_target_pairs={{0,4},{8,12},{16,20},{24,28},{32,36},{40,44},{48,52},{56,60},{64,6... | collective-permute-start | bytes 3244040 | tf_op jit(solution)/shard_map/ppermute | solution.py:256
  71.5 41.7 %collective-permute-start.9 = (bf16[66,64,128]{2,1,0:T(8,128)(2,1)}, bf16[66,64,128]{2,1,0:T(8,128)(2,1)}, u32[]{:S(2)}, u32[]{:S(2)}) collective-permute-start(bf16[66,64,128]{2,1,0:T(8,128)(2,1)} %shard_map.132.own), channel_id=1, source_target_pairs={{4,8},{12,16},{20,24},{28,32},{36,40},{44,48},{52,56},{60,64},{68,... | collective-permute-start | bytes 3244040 | tf_op jit(solution)/shard_map/ppermute | solution.py:255
  92.5 27.1 %all-to-all-start = ((bf16[32,48,128]{2,1,0:T(8,128)(2,1)}), bf16[32,48,128]{2,1,0:T(8,128)(2,1)S(1)}, u32[]{:S(2)}, u32[]{:S(2)}) async-start(bf16[32,48,128]{2,1,0:T(8,128)(2,1)} %copy-done.4), calls=%async_computation | async-start | bytes 786432 | tf_op jit(solution)/shard_map/all_to_all | solution.py:315
  113.2 6.5 %copy-start.8 = (bf16[128,96]{1,0:T(8,128)(2,1)S(1)}, bf16[128,96]{1,0:T(8,128)(2,1)}, u32[]{:S(2)}) copy-start(bf16[128,96]{1,0:T(8,128)(2,1)} %copy-done.7) | copy-start | bytes 73732
  113.2 6.5 %copy-start.10 = (f32[64,128]{1,0:T(8,128)S(1)}, f32[64,128]{1,0:T(8,128)}, u32[]{:S(2)}) copy-start(f32[64,128]{1,0:T(8,128)} %copy-done.9) | copy-start | bytes 98308
  113.2 6.5 %copy-start.13 = (bf16[64,64]{1,0:T(8,128)(2,1)S(1)}, bf16[64,64]{1,0:T(8,128)(2,1)}, u32[]{:S(2)}) copy-start(bf16[64,64]{1,0:T(8,128)(2,1)} %copy-done.12) | copy-start | bytes 24580
  113.2 6.5 %copy-start.15 = (s32[3]{0:T(128)S(1)}, s32[3]{0:T(128)}, u32[]{:S(2)}) copy-start(s32[3]{0:T(128)} %copy-done.14) | copy-start | bytes 40
  (6 other events, 3.9 us)

commit v7 on v6

--- a/solution.py
+++ b/solution.py
@@ -127,21 +127,22 @@
             ).astype(BF16)
 
 
-def near_kernel(w, near, own, part):
+def near_kernel(w, near, own, cot, vin, part, slope):
     vol = (near, own)
 
-    def emit(r, value):
-        part[r] = value
-
-    conv_rows(lambda a, i: vol[a][i], w[:, : 2 * w.shape[1] // 3], own.shape[0], emit, frames=2)
-
-
-def input_grad_kernel(w, cot, vin, part, far, out):
     def emit(r, value):
         x = vin[r].astype(F32)
         s = logistic(x)
-        grad = (part[r] + value) * (s * (1.0 + x * (1.0 - s)))
-        out[r] = (cot[r].astype(F32) + grad).astype(BF16)
+        rise = s * (1.0 + x * (1.0 - s))
+        slope[r] = rise
+        part[r] = cot[r].astype(F32) + value * rise
+
+    conv_rows(lambda a, i: vol[a][i], w[:, : 2 * w.shape[1] // 3], own.shape[0], emit, frames=2)
+
+
+def input_grad_kernel(w, part, slope, far, out):
+    def emit(r, value):
+        out[r] = (part[r] + value * slope[r]).astype(BF16)
 
     conv_rows(lambda a, i: far[i], w[:, 2 * w.shape[1] // 3 :], far.shape[0], emit, frames=1)
 
@@ -313,11 +314,12 @@
         6 * MIB,
     )(pos, listed, wb, wp, plane_row, pool, v_own, inner, in_p, in_n)
     recv = lax.all_to_all(send, "tm", split_axis=0, concat_axis=0, tiled=True)
-    part = call(
-        near_kernel, jax.ShapeDtypeStruct((n, ch, width), F32), [VMEM] * 3, [], flops * 2 // 3, 6 * MIB
-    )(wat, gr_p, grad)
-    input_grad = call(input_grad_kernel, rows(n), [VMEM] * 5, [], flops // 3, 6 * MIB)(
-        wat, c, v, part, gr_n
+    wide = jax.ShapeDtypeStruct((n, ch, width), F32)
+    part, rise = call(near_kernel, (wide, wide), [VMEM] * 5, [], flops * 2 // 3, 8 * MIB)(
+        wat, gr_p, grad, c, v
+    )
+    input_grad = call(input_grad_kernel, rows(n), [VMEM] * 4, [], flops // 3, 6 * MIB)(
+        wat, part, rise, gr_n
     )
     plane_scores, time_scores = call(
         time_kernel_body,

time: 122 us -> 125 us (1.025)
  waiting for transfers between devices: 44.1 us -> 48.1 us
    all_to_all x1, waiting for transfers between devices: 2.65 us -> 7.5 us  [shards(): recv = lax.all_to_all(send, 'tm', split_axis=0, concat_axis=0, tiled=True)]
    ppermute x1, starting transfers between devices: 1.5 us -> 0.09 us  [shards(): got = lax.ppermute(edge(even), 'space', row_first)]
    ppermute x1, starting transfers between devices: 3.11 us -> 4.51 us  [shards(): other = lax.ppermute(edge(~even), 'space', row_second)]
  transfers between devices with their start and end apart: 11 -> 11, of which waited for: 5 -> 5; matrix products, arithmetic and copies ran while one was open for 1% -> 1% of each run, Pallas kernels for 21% -> 20%
where the time goes in v7:
time: 125 us
  waiting for transfers between devices  48.1 us (38%)
  starting transfers between devices  39.4 us (32%)
  Pallas kernels  26.4 us (21%)
  local copies, waits for them, and re-layouts  8.55 us (7%)
  other arithmetic  1.39 us (1%)
    ppermute x4, waiting for transfers between devices, both(): return (lax.ppermute(x, 'tm', swap_first), far)  38.6 us
    all_to_all x1, starting transfers between devices, shards(): recv = lax.all_to_all(send, 'tm', split_axis=0, concat_axis=0, tiled=True)  17 us
    ppermute x4, starting transfers between devices, both(): return (lax.ppermute(x, 'tm', swap_first), far)  12 us
    all_to_all x1, waiting for transfers between devices, shards(): recv = lax.all_to_all(send, 'tm', split_axis=0, concat_axis=0, tiled=True)  7.5 us
    unnamed x38, local copies, waits for them, and re-layouts  6.84 us
    pallas_call x1, Pallas kernels, shards(): call(video_kernel, (rows(n), jax.ShapeDtypeStruct((tm, ch // 2 + quarter,...  6.22 us
    pallas_call x1, Pallas kernels, shards(): call(grad_kernel, rows(n + 2), [SMEM] + [VMEM] * 5, [], flops, 6 * MIB)  5.84 us
    ppermute x4, starting transfers between devices, both(): far = lax.ppermute(x, 'tm', swap_second)  5.73 us
  transfers between devices with their start and end apart: 11, of which 5 were waited for; matrix products, arithmetic and copies ran while one was open for 1% of the time, Pallas kernels for 20%

profile of v7, /device:TPU:1, one launch (start us, length us, event | category | flops | bytes accessed | tf_op | source)
XLA Modules:
  0.0 124.6 jit_solution(16950682578841719719)
XLA Ops:
  2.4 4.5 %collective-permute-start = (bf16[5,64,128]{2,1,0:T(8,128)(2,1)S(1)}, bf16[5,64,128]{2,1,0:T(8,128)(2,1)S(1)}, u32[]{:S(2)}, u32[]{:S(2)}) collective-permute-start(bf16[5,64,128]{2,1,0:T(8,128)(2,1)S(1)} %pad_maximum_fusion.2), channel_id=1, source_target_pairs={{1,2},{2,1},{5,6},{6,5},{9,10},{10,9},{13,14},{14,13},{17,18},{18,... | collective-permute-start | bytes 245768 | tf_op jit(solution)/shard_map/ppermute | solution.py:267
  7.0 2.0 %collective-permute-done = bf16[5,64,128]{2,1,0:T(8,128)(2,1)S(1)} collective-permute-done((bf16[5,64,128]{2,1,0:T(8,128)(2,1)S(1)}, bf16[5,64,128]{2,1,0:T(8,128)(2,1)S(1)}, u32[]{:S(2)}, u32[]{:S(2)}) %collective-permute-start) | collective-permute-done | bytes 81952 | tf_op jit(solution)/shard_map/ppermute | solution.py:267
  9.2 1.4 %collective-permute-start.2 = (bf16[70,64,128]{2,1,0:T(8,128)(2,1)S(1)}, bf16[70,64,128]{2,1,0:T(8,128)(2,1)}, u32[]{:S(2)}, u32[]{:S(2)}) collective-permute-start(bf16[70,64,128]{2,1,0:T(8,128)(2,1)S(1)} %pad_maximum_fusion.own.base), channel_id=1, source_target_pairs={{0,4},{8,12},{16,20},{24,28},{32,36},{40,44},{48,52},{56,60},{64,6... | collective-permute-start | bytes 3440648 | tf_op jit(solution)/shard_map/ppermute | solution.py:257
  10.6 1.7 %collective-permute-start.3 = (bf16[70,64,128]{2,1,0:T(8,128)(2,1)S(1)}, bf16[70,64,128]{2,1,0:T(8,128)(2,1)}, u32[]{:S(2)}, u32[]{:S(2)}) collective-permute-start(bf16[70,64,128]{2,1,0:T(8,128)(2,1)S(1)} %pad_maximum_fusion.own.base), channel_id=1, source_target_pairs={{4,8},{12,16},{20,24},{28,32},{36,40},{44,48},{52,56},{60,64},{68,... | collective-permute-start | bytes 3440648 | tf_op jit(solution)/shard_map/ppermute | solution.py:256
  12.3 1.1 pad_maximum_fusion.1.own
  13.5 2.5 %collective-permute-start.6 = (bf16[68,64,128]{2,1,0:T(8,128)(2,1)}, bf16[68,64,128]{2,1,0:T(8,128)(2,1)}, u32[]{:S(2)}, u32[]{:S(2)}) collective-permute-start(bf16[68,64,128]{2,1,0:T(8,128)(2,1)} %pad_maximum_fusion.1.own), channel_id=1, source_target_pairs={{0,4},{8,12},{16,20},{24,28},{32,36},{40,44},{48,52},{56,60},{64,6... | collective-permute-start | bytes 3342344 | tf_op jit(solution)/shard_map/ppermute | solution.py:257
  16.0 1.7 %collective-permute-start.7 = (bf16[68,64,128]{2,1,0:T(8,128)(2,1)}, bf16[68,64,128]{2,1,0:T(8,128)(2,1)}, u32[]{:S(2)}, u32[]{:S(2)}) collective-permute-start(bf16[68,64,128]{2,1,0:T(8,128)(2,1)} %pad_maximum_fusion.1.own), channel_id=1, source_target_pairs={{4,8},{12,16},{20,24},{28,32},{36,40},{44,48},{52,56},{60,64},{68,... | collective-permute-start | bytes 3342344 | tf_op jit(solution)/shard_map/ppermute | solution.py:256
  17.8 1.0 copy-done.2
  18.8 1.0 copy-done.3
  22.0 1.0 shard_map.129
  24.9 11.8 %collective-permute-done.2.prev = bf16[70,64,128]{2,1,0:T(8,128)(2,1)} collective-permute-done((bf16[70,64,128]{2,1,0:T(8,128)(2,1)S(1)}, bf16[70,64,128]{2,1,0:T(8,128)(2,1)}, u32[]{:S(2)}, u32[]{:S(2)}) %collective-permute-start.2) | collective-permute-done | bytes 1146912 | tf_op jit(solution)/shard_map/ppermute | solution.py:257
  36.7 4.7 %shard_map.130 = (bf16[68,64,128]{2,1,0:T(8,128)(2,1)S(1)}, bf16[68,64,128]{2,1,0:T(8,128)(2,1)S(1)}) custom-call(s32[3]{0:T(128)S(1)} %pad_add_fusion.pos, bf16[192,576]{1,0:T(8,128)(2,1)S(1)} %get-tuple-element.30.w, bf16[70,64,128]{2,1,0:T(8,128)(2,1)S(1)} %pad_maximum_fusion.own.base, bf16[70,64,128]{2,1,0:T(8,128)(2,1)} %collective-permute-done.2.prev, ...), custom_call_target="tpu_custom_call" | custom-call | flops 1811939328 | bytes 6291456 | tf_op jit(solution)/shard_map/pallas_call | solution.py:295
  41.4 4.1 %collective-permute-start.4 = (bf16[68,64,128]{2,1,0:T(8,128)(2,1)S(1)}, bf16[68,64,128]{2,1,0:T(8,128)(2,1)S(1)}, u32[]{:S(2)}, u32[]{:S(2)}) collective-permute-start(bf16[68,64,128]{2,1,0:T(8,128)(2,1)S(1)} %get-tuple-element.31.own), channel_id=1, source_target_pairs={{0,4},{8,12},{16,20},{24,28},{32,36},{40,44},{48,52},{56,60},{64,6... | collective-permute-start | bytes 3342344 | tf_op jit(solution)/shard_map/ppermute | solution.py:257
  46.2 14.3 %collective-permute-done.6.prev = bf16[68,64,128]{2,1,0:T(8,128)(2,1)} collective-permute-done((bf16[68,64,128]{2,1,0:T(8,128)(2,1)}, bf16[68,64,128]{2,1,0:T(8,128)(2,1)}, u32[]{:S(2)}, u32[]{:S(2)}) %collective-permute-start.6) | collective-permute-done | bytes 1114144 | tf_op jit(solution)/shard_map/ppermute | solution.py:257
  60.5 5.8 %shard_map.132.own = bf16[66,64,128]{2,1,0:T(8,128)(2,1)} custom-call(s32[3]{0:T(128)S(1)} %pad_add_fusion.pos, bf16[192,576]{1,0:T(8,128)(2,1)S(1)} %get-tuple-element.34.w, bf16[68,64,128]{2,1,0:T(8,128)(2,1)S(1)} %get-tuple-element.35.slope, bf16[68,64,128]{2,1,0:T(8,128)(2,1)} %pad_maximum_fusion.1.own, ...), custom_call_target="tpu_custom_call" | custom-call | flops 1811939328 | bytes 6291456 | tf_op jit(solution)/shard_map/pallas_call | solution.py:299
  66.3 4.0 %collective-permute-start.8 = (bf16[66,64,128]{2,1,0:T(8,128)(2,1)}, bf16[66,64,128]{2,1,0:T(8,128)(2,1)}, u32[]{:S(2)}, u32[]{:S(2)}) collective-permute-start(bf16[66,64,128]{2,1,0:T(8,128)(2,1)} %shard_map.132.own), channel_id=1, source_target_pairs={{0,4},{8,12},{16,20},{24,28},{32,36},{40,44},{48,52},{56,60},{64,6... | collective-permute-start | bytes 3244040 | tf_op jit(solution)/shard_map/ppermute | solution.py:257
  70.3 1.6 %collective-permute-start.9 = (bf16[66,64,128]{2,1,0:T(8,128)(2,1)}, bf16[66,64,128]{2,1,0:T(8,128)(2,1)}, u32[]{:S(2)}, u32[]{:S(2)}) collective-permute-start(bf16[66,64,128]{2,1,0:T(8,128)(2,1)} %shard_map.132.own), channel_id=1, source_target_pairs={{4,8},{12,16},{20,24},{28,32},{36,40},{44,48},{52,56},{60,64},{68,... | collective-permute-start | bytes 3244040 | tf_op jit(solution)/shard_map/ppermute | solution.py:256
  72.0 12.5 %collective-permute-done.4.prev = bf16[68,64,128]{2,1,0:T(8,128)(2,1)S(1)} collective-permute-done((bf16[68,64,128]{2,1,0:T(8,128)(2,1)S(1)}, bf16[68,64,128]{2,1,0:T(8,128)(2,1)S(1)}, u32[]{:S(2)}, u32[]{:S(2)}) %collective-permute-start.4) | collective-permute-done | bytes 1114144 | tf_op jit(solution)/shard_map/ppermute | solution.py:257
  84.5 6.2 %shard_map.131 = (bf16[64,64,128]{2,1,0:T(8,128)(2,1)}, bf16[32,48,128]{2,1,0:T(8,128)(2,1)S(1)}) custom-call(s32[3]{0:T(128)S(1)} %pad_add_fusion.pos, s32[8]{0:T(128)S(1)} %copy-done.18, bf16[192,576]{1,0:T(8,128)(2,1)S(1)} %get-tuple-element.26.w, bf16[192,192]{1,0:T(8,128)(2,1)S(1)} %get-tuple-element.27.wp, f32[64,128]{1,0:T(8,128)S(1)} %get-tuple-element.28.head, ...), custom_call_target="tpu_custom_call" | custom-call | flops 2415919104 | bytes 6291456 | tf_op jit(solution)/shard_map/pallas_call | solution.py:305
  91.4 17.0 %all-to-all-start = ((bf16[32,48,128]{2,1,0:T(8,128)(2,1)}), bf16[32,48,128]{2,1,0:T(8,128)(2,1)S(1)}, u32[]{:S(2)}, u32[]{:S(2)}) async-start(bf16[32,48,128]{2,1,0:T(8,128)(2,1)} %copy-done.4), calls=%async_computation | async-start | bytes 786432 | tf_op jit(solution)/shard_map/all_to_all | solution.py:316
  108.4 3.5 %shard_map.133 = (f32[64,64,128]{2,1,0:T(8,128)S(1)}, f32[64,64,128]{2,1,0:T(8,128)S(1)}) custom-call(bf16[192,576]{1,0:T(8,128)(2,1)S(1)} %get-tuple-element.33.w, bf16[66,64,128]{2,1,0:T(8,128)(2,1)} %collective-permute-done.8.near, bf16[66,64,128]{2,1,0:T(8,128)(2,1)} %shard_map.132.own, bf16[64,64,128]{2,1,0:T(8,128)(2,1)S(1)} %bitcast.21, ...), custom_call_target="tpu_custom_call" | custom-call | flops 1207959552 | bytes 8388608 | tf_op jit(solution)/shard_map/pallas_call | solution.py:318
  112.0 3.3 %shard_map.134 = bf16[64,64,128]{2,1,0:T(8,128)(2,1)} custom-call(bf16[192,576]{1,0:T(8,128)(2,1)S(1)} %get-tuple-element.33.w, f32[64,64,128]{2,1,0:T(8,128)S(1)} %get-tuple-element.36.part, f32[64,64,128]{2,1,0:T(8,128)S(1)} %get-tuple-element.37.slope, bf16[66,64,128]{2,1,0:T(8,128)(2,1)} %collective-permute-done.9.far), custom_call_target="tpu_custom_call" | custom-call | flops 603979776 | bytes 6291456 | tf_op jit(solution)/shard_map/pallas_call | solution.py:321
  115.3 7.5 %all-to-all-done.recv = bf16[32,48,128]{2,1,0:T(8,128)(2,1)S(1)} async-done(((bf16[32,48,128]{2,1,0:T(8,128)(2,1)}), bf16[32,48,128]{2,1,0:T(8,128)(2,1)S(1)}, u32[]{:S(2)}, u32[]{:S(2)}) %all-to-all-start) | async-done | bytes 393248 | tf_op jit(solution)/shard_map/all_to_all | solution.py:316
  122.8 1.8 %shard_map.135 = (f32[16,128]{1,0:T(8,128)}, f32[1,64]{1,0:T(1,128)}) custom-call(s32[3]{0:T(128)S(1)} %copy-done.15, s32[8]{0:T(128)S(1)} %copy-done.18, bf16[128,96]{1,0:T(8,128)(2,1)S(1)} %copy-done.8, bf16[64,64]{1,0:T(8,128)(2,1)S(1)} %copy-done.13, f32[64,128]{1,0:T(8,128)S(1)} %copy-done.10, bf16[32,48,128]{2,1,0:T(8,128)(2,1)S(1)} %all-to-all-done.recv), custom_call_target="tpu_custom_call" | custom-call | flops 90596968 | bytes 1048576 | tf_op jit(solution)/shard_map/pallas_call | solution.py:324
  (55 shorter events, 7.6 us)
Async XLA Ops:
  0.6 8.4 %copy-start = (bf16[1,64,64,128]{3,2,1,0:T(8,128)(2,1)S(1)}, bf16[1,64,64,128]{3,2,1,0:T(8,128)(2,1)}, u32[]{:S(2)}) copy-start(bf16[1,64,64,128]{3,2,1,0:T(8,128)(2,1)} %param.10) | copy-start | bytes 3145732
  2.4 6.6 %collective-permute-start = (bf16[5,64,128]{2,1,0:T(8,128)(2,1)S(1)}, bf16[5,64,128]{2,1,0:T(8,128)(2,1)S(1)}, u32[]{:S(2)}, u32[]{:S(2)}) collective-permute-start(bf16[5,64,128]{2,1,0:T(8,128)(2,1)S(1)} %pad_maximum_fusion.2), channel_id=1, source_target_pairs={{1,2},{2,1},{5,6},{6,5},{9,10},{10,9},{13,14},{14,13},{17,18},{18,... | collective-permute-start | bytes 245768 | tf_op jit(solution)/shard_map/ppermute | solution.py:267
  6.9 2.1 %collective-permute-start.1 = (bf16[5,64,128]{2,1,0:T(8,128)(2,1)S(1)}, bf16[5,64,128]{2,1,0:T(8,128)(2,1)S(1)}, u32[]{:S(2)}, u32[]{:S(2)}) collective-permute-start(bf16[5,64,128]{2,1,0:T(8,128)(2,1)S(1)} %pad_maximum_fusion.3), channel_id=1, source_target_pairs={{0,1},{2,3},{1,0},{3,2},{4,5},{6,7},{5,4},{7,6},{8,9},{10,11},{9,8... | collective-permute-start | bytes 245768 | tf_op jit(solution)/shard_map/ppermute | solution.py:266
  9.1 3.2 %copy-start.1 = (bf16[1,64,64,128]{3,2,1,0:T(8,128)(2,1)S(1)}, bf16[1,64,64,128]{3,2,1,0:T(8,128)(2,1)}, u32[]{:S(2)}) copy-start(bf16[1,64,64,128]{3,2,1,0:T(8,128)(2,1)} %param.11) | copy-start | bytes 3145732
  9.2 27.5 %collective-permute-start.2 = (bf16[70,64,128]{2,1,0:T(8,128)(2,1)S(1)}, bf16[70,64,128]{2,1,0:T(8,128)(2,1)}, u32[]{:S(2)}, u32[]{:S(2)}) collective-permute-start(bf16[70,64,128]{2,1,0:T(8,128)(2,1)S(1)} %pad_maximum_fusion.own.base), channel_id=1, source_target_pairs={{0,4},{8,12},{16,20},{24,28},{32,36},{40,44},{48,52},{56,60},{64,6... | collective-permute-start | bytes 3440648 | tf_op jit(solution)/shard_map/ppermute | solution.py:257
  10.6 26.1 %collective-permute-start.3 = (bf16[70,64,128]{2,1,0:T(8,128)(2,1)S(1)}, bf16[70,64,128]{2,1,0:T(8,128)(2,1)}, u32[]{:S(2)}, u32[]{:S(2)}) collective-permute-start(bf16[70,64,128]{2,1,0:T(8,128)(2,1)S(1)} %pad_maximum_fusion.own.base), channel_id=1, source_target_pairs={{4,8},{12,16},{20,24},{28,32},{36,40},{44,48},{52,56},{60,64},{68,... | collective-permute-start | bytes 3440648 | tf_op jit(solution)/shard_map/ppermute | solution.py:256
  12.3 5.5 %copy-start.6 = (bf16[3,64,64]{2,1,0:T(8,128)(2,1)S(1)}, bf16[3,64,64]{2,1,0:T(8,128)(2,1)}, u32[]{:S(2)}) copy-start(bf16[3,64,64]{2,1,0:T(8,128)(2,1)} %kt.1) | copy-start | bytes 73732
  12.3 5.4 %copy-start.11 = (bf16[64,64]{1,0:T(8,128)(2,1)S(1)}, bf16[64,64]{1,0:T(8,128)(2,1)}, u32[]{:S(2)}) copy-start(bf16[64,64]{1,0:T(8,128)(2,1)} %km.1) | copy-start | bytes 24580
  13.5 47.0 %collective-permute-start.6 = (bf16[68,64,128]{2,1,0:T(8,128)(2,1)}, bf16[68,64,128]{2,1,0:T(8,128)(2,1)}, u32[]{:S(2)}, u32[]{:S(2)}) collective-permute-start(bf16[68,64,128]{2,1,0:T(8,128)(2,1)} %pad_maximum_fusion.1.own), channel_id=1, source_target_pairs={{0,4},{8,12},{16,20},{24,28},{32,36},{40,44},{48,52},{56,60},{64,6... | collective-permute-start | bytes 3342344 | tf_op jit(solution)/shard_map/ppermute | solution.py:257
  16.0 44.5 %collective-permute-start.7 = (bf16[68,64,128]{2,1,0:T(8,128)(2,1)}, bf16[68,64,128]{2,1,0:T(8,128)(2,1)}, u32[]{:S(2)}, u32[]{:S(2)}) collective-permute-start(bf16[68,64,128]{2,1,0:T(8,128)(2,1)} %pad_maximum_fusion.1.own), channel_id=1, source_target_pairs={{4,8},{12,16},{20,24},{28,32},{36,40},{44,48},{52,56},{60,64},{68,... | collective-permute-start | bytes 3342344 | tf_op jit(solution)/shard_map/ppermute | solution.py:256
  17.8 66.7 %copy-start.14 = (s32[3]{0:T(128)}, s32[3]{0:T(128)S(1)}, u32[]{:S(2)}) copy-start(s32[3]{0:T(128)S(1)} %pad_add_fusion.pos) | copy-start | bytes 40
  17.8 1.0 copy-start.2
  18.8 1.0 copy-start.3
  19.8 0.9 copy-start.5
  41.4 43.1 %collective-permute-start.4 = (bf16[68,64,128]{2,1,0:T(8,128)(2,1)S(1)}, bf16[68,64,128]{2,1,0:T(8,128)(2,1)S(1)}, u32[]{:S(2)}, u32[]{:S(2)}) collective-permute-start(bf16[68,64,128]{2,1,0:T(8,128)(2,1)S(1)} %get-tuple-element.31.own), channel_id=1, source_target_pairs={{0,4},{8,12},{16,20},{24,28},{32,36},{40,44},{48,52},{56,60},{64,6... | collective-permute-start | bytes 3342344 | tf_op jit(solution)/shard_map/ppermute | solution.py:257
  45.5 39.0 %collective-permute-start.5 = (bf16[68,64,128]{2,1,0:T(8,128)(2,1)S(1)}, bf16[68,64,128]{2,1,0:T(8,128)(2,1)S(1)}, u32[]{:S(2)}, u32[]{:S(2)}) collective-permute-start(bf16[68,64,128]{2,1,0:T(8,128)(2,1)S(1)} %get-tuple-element.31.own), channel_id=1, source_target_pairs={{4,8},{12,16},{20,24},{28,32},{36,40},{44,48},{52,56},{60,64},{68,... | collective-permute-start | bytes 3342344 | tf_op jit(solution)/shard_map/ppermute | solution.py:256
  60.5 24.0 %copy-start.18 = (s32[8]{0:T(128)S(1)}, s32[8]{0:T(128)}, u32[]{:S(2)}) copy-start(s32[8]{0:T(128)} %listed.3) | copy-start | bytes 100
  66.3 42.1 %collective-permute-start.8 = (bf16[66,64,128]{2,1,0:T(8,128)(2,1)}, bf16[66,64,128]{2,1,0:T(8,128)(2,1)}, u32[]{:S(2)}, u32[]{:S(2)}) collective-permute-start(bf16[66,64,128]{2,1,0:T(8,128)(2,1)} %shard_map.132.own), channel_id=1, source_target_pairs={{0,4},{8,12},{16,20},{24,28},{32,36},{40,44},{48,52},{56,60},{64,6... | collective-permute-start | bytes 3244040 | tf_op jit(solution)/shard_map/ppermute | solution.py:257
  70.3 41.6 %collective-permute-start.9 = (bf16[66,64,128]{2,1,0:T(8,128)(2,1)}, bf16[66,64,128]{2,1,0:T(8,128)(2,1)}, u32[]{:S(2)}, u32[]{:S(2)}) collective-permute-start(bf16[66,64,128]{2,1,0:T(8,128)(2,1)} %shard_map.132.own), channel_id=1, source_target_pairs={{4,8},{12,16},{20,24},{28,32},{36,40},{44,48},{52,56},{60,64},{68,... | collective-permute-start | bytes 3244040 | tf_op jit(solution)/shard_map/ppermute | solution.py:256
  91.4 31.4 %all-to-all-start = ((bf16[32,48,128]{2,1,0:T(8,128)(2,1)}), bf16[32,48,128]{2,1,0:T(8,128)(2,1)S(1)}, u32[]{:S(2)}, u32[]{:S(2)}) async-start(bf16[32,48,128]{2,1,0:T(8,128)(2,1)} %copy-done.4), calls=%async_computation | async-start | bytes 786432 | tf_op jit(solution)/shard_map/all_to_all | solution.py:316
  112.0 10.9 %copy-start.8 = (bf16[128,96]{1,0:T(8,128)(2,1)S(1)}, bf16[128,96]{1,0:T(8,128)(2,1)}, u32[]{:S(2)}) copy-start(bf16[128,96]{1,0:T(8,128)(2,1)} %copy-done.7) | copy-start | bytes 73732
  112.0 10.9 %copy-start.10 = (f32[64,128]{1,0:T(8,128)S(1)}, f32[64,128]{1,0:T(8,128)}, u32[]{:S(2)}) copy-start(f32[64,128]{1,0:T(8,128)} %copy-done.9) | copy-start | bytes 98308
  112.0 10.8 %copy-start.13 = (bf16[64,64]{1,0:T(8,128)(2,1)S(1)}, bf16[64,64]{1,0:T(8,128)(2,1)}, u32[]{:S(2)}) copy-start(bf16[64,64]{1,0:T(8,128)(2,1)} %copy-done.12) | copy-start | bytes 24580
  112.0 10.8 %copy-start.15 = (s32[3]{0:T(128)S(1)}, s32[3]{0:T(128)}, u32[]{:S(2)}) copy-start(s32[3]{0:T(128)} %copy-done.14) | copy-start | bytes 40
  (6 other events, 3.9 us)
